TPU v7x, 128 devices: a whole 4x4x4 slice. The times are simulated.
128 devices in a mesh: dp: 2 (over x_lo), expert: 64 (over x_hi, z, y, core).
Axes of the slice: x: 4 (x_hi: 2, x_lo: 2; x = x_hi * 2 + x_lo), y: 4, z: 4, core: 2. Of those that a mesh axis runs over, the one named last changes fastest.
Arguments:
- tokens: bfloat16 [2048, 7168], P(('dp', 'expert')), may hold values from -6 to 6
- picks: int32 [2048, 8], P(('dp', 'expert')), may hold values from 0 to 63, all different within a row; in each aligned block of 16 rows (0 to 15, 16 to 31, ...) at most 4 rows name the same one
- mix_weights: float32 [2048, 8], P(('dp', 'expert')), may hold values from 0.1 to 0.6
- pairs: int32 [16, 2], replicated, may hold values from 0 to 63, as said below
- gate_weight: bfloat16 [64, 7168, 1024], P('expert', None, 'dp'), may hold values from -0.0625 to 0.0625
- up_weight: bfloat16 [64, 7168, 1024], P('expert', None, 'dp'), may hold values from -0.0625 to 0.0625
- down_weight: bfloat16 [64, 1024, 7168], P('expert', 'dp'), may hold values from -0.1875 to 0.1875
Outputs:
- combined: bfloat16 [2048, 7168], P(('dp', 'expert'))
Inputs may be any that keep to these rules, and one draw needn't show every extreme that they name: `picks`: each row names 8 different slots. The rows of one device name one slot at most 4 times, and in every draw some device's rows name some slot exactly 4 times. Each row is a pair (a, a + 32) with a below 32; no position stands in two pairs; positions 0 and 31 always stand in a pair.
All inputs are finite; a program needn't handle non-finite values.
Results may differ from a plain program's by a relative error of at most 0.012.
Values may be sent and summed in bfloat16 or wider, within the bound.
No kernel may reach another device: no remote copies, remote signals or barrier semaphores. Data moves between devices by JAX's collectives and lax.ppermute only.
A program may use at most 128 MiB of HBM per device.

v0:
```python
import functools
import itertools

import jax
import jax.numpy as jnp
from jax import lax
from jax.experimental import pallas as pl
from jax.experimental.pallas import tpu as pltpu
from jax.sharding import Mesh, PartitionSpec as P

ALL_AXES = ("dp", "xh", "z", "y", "c")
RING = 4
CORES = 2
CAP = 4
TOP = 8
GROUP = 16
META = 128
MAIN = 2560
SIDE = 1024
BLOCK = 128
TAIL = MAIN + 2 * SIDE
SHIFTS = (0, 1, 3, 2)
MAIN_ROUTE = (("z", "y"), ("y", "x"), ("x", "z"))
SIDE_ROUTE = (("x", "x"), ("z", "z"), ("y", "y"))
SMALL_VMEM = 24 << 20
LARGE_VMEM = 56 << 20


def flat_index(x, z, y, c):
    return ((((x % 2) * 2 + x // 2) * RING + z) * RING + y) * CORES + c


def ring_perm(axes, shift, cross=False):
    pairs = []
    for x, z, y, c in itertools.product(range(RING), range(RING), range(RING), range(CORES)):
        there = {"x": x, "z": z, "y": y}
        there[axes[c]] = (there[axes[c]] + shift) % RING
        target = flat_index(there["x"], there["z"], there["y"], 1 - c if cross else c)
        pairs.append((flat_index(x, z, y, c), target))
    return pairs


def together(*values):
    return lax.optimization_barrier(values)


def back_perm(axes, shift, cross=False):
    return [(target, source) for source, target in ring_perm(axes, shift, cross)]


def gathered(value, axes):
    return [value] + [lax.ppermute(value, ALL_AXES, ring_perm(axes, s)) for s in SHIFTS[1:]]


def scattered(blocks, axes):
    return [blocks[0]] + [lax.ppermute(b, ALL_AXES, back_perm(axes, s)) for b, s in zip(blocks[1:], SHIFTS[1:])]


def other_core(value):
    return lax.ppermute(value, "c", [(0, 1), (1, 0)])


def hop(blocks, axes, perm, numbers, cross=False):
    return [other_core(blocks[r]) if r == 0 else lax.ppermute(blocks[r], ALL_AXES, perm(axes, SHIFTS[r], cross))
            for r in numbers]


def column_chunks(width):
    steps, start = [], 0
    while start < width:
        size = min(1280, width - start)
        steps.append((start, size))
        start += size
    return steps


def iota(shape, dim):
    return lax.broadcasted_iota(jnp.int32, shape, dim)


def slots_of(meta, experts):
    turned = jnp.transpose(meta.astype(jnp.float32))
    owner = turned[:TOP]
    match = [owner == e.astype(jnp.float32) for e in experts]
    hits = [jnp.max(jnp.where(m, 1.0, 0.0), axis=0, keepdims=True) for m in match]
    stacked = jnp.concatenate(hits, axis=0)
    row, col = iota((BLOCK, BLOCK), 0), iota((BLOCK, BLOCK), 1)
    before = jnp.where((row // GROUP == col // GROUP) & (row < col), 1.0, 0.0)
    rank = jnp.dot(stacked.astype(jnp.bfloat16), before.astype(jnp.bfloat16),
                   preferred_element_type=jnp.float32)
    base = (iota((1, BLOCK), 1) // GROUP * CAP).astype(jnp.float32)
    slot = iota((BLOCK // RING, BLOCK), 0).astype(jnp.float32)
    place = [slot == jnp.where(h > 0.5, base + rank[e:e + 1], -1.0) for e, h in enumerate(hits)]
    return place, match, turned


def experts_at(info, first_expert, cores):
    own = [info[first_expert + r] for r in range(RING)]
    return own + [e ^ 1 for e in own] if cores == CORES else own


def pack_kernel(first_expert, width, pieces, info, *refs):
    blocks, outs = [refs[RING * i:RING * i + RING] for i in range(pieces)], refs[RING * pieces:]
    experts = experts_at(info, first_expert, len(outs) // RING)
    rows = BLOCK // RING
    for b in range(RING):
        place, _, _ = slots_of(blocks[0][b][:, width:width + META], experts)
        spread = jnp.concatenate([jnp.where(p, 1.0, 0.0) for p in place], axis=0).astype(jnp.bfloat16)
        for piece in range(pieces):
            for start, size in column_chunks(width):
                got = jnp.dot(spread, blocks[piece][b][:, start:start + size], preferred_element_type=jnp.float32)
                got = got.astype(jnp.bfloat16)
                at = piece * width + start
                for e, out in enumerate(outs):
                    out[rows * b:rows * (b + 1), at:at + size] = got[rows * e:rows * (e + 1)]


VMEM_SPEC = pl.BlockSpec(memory_space=pltpu.VMEM)
SMEM_SPEC = pl.BlockSpec(memory_space=pltpu.SMEM)
HBM_SPEC = pl.BlockSpec(memory_space=pltpu.HBM)


def pack(info, first_expert, cores, *pieces):
    width = pieces[0][0].shape[1] - META
    total = width * len(pieces)
    out = pl.pallas_call(
        functools.partial(pack_kernel, first_expert, width, len(pieces)),
        out_shape=[jax.ShapeDtypeStruct((BLOCK, total), jnp.bfloat16)] * (cores * RING),
        in_specs=[SMEM_SPEC] + [VMEM_SPEC] * (RING * len(pieces)),
        out_specs=[VMEM_SPEC] * (cores * RING),
        compiler_params=pltpu.CompilerParams(vmem_limit_bytes=SMALL_VMEM),
        cost_estimate=pl.CostEstimate(
            flops=2 * cores * RING * BLOCK * BLOCK * total, bytes_accessed=16 * BLOCK * total, transcendentals=0),
    )(info, *[b for p in pieces for b in p])
    return list(out[:RING]), list(out[RING:])


def combine_kernel(first_expert, width, count, mode, info, *refs):
    blocks, metas, rest = refs[:count], refs[count:count + RING], refs[count + RING:]
    experts = experts_at(info, first_expert, count // RING)
    rows = BLOCK // RING
    for b in range(RING):
        place, match, turned = slots_of(metas[b][...], experts)
        parts = []
        for offset in (TOP, 2 * TOP):
            mix = turned[offset:offset + TOP]
            picked = [jnp.sum(jnp.where(m, mix, 0.0), axis=0, keepdims=True) for m in match]
            weight = jnp.concatenate([jnp.where(p, w, 0.0) for p, w in zip(place, picked)], axis=0)
            parts.append(jnp.transpose(weight))
        mixer = jnp.concatenate(parts, axis=0).astype(jnp.bfloat16)
        for start, size in column_chunks(width):
            cols = slice(start, start + size)
            data = jnp.concatenate([block[rows * b:rows * (b + 1), cols] for block in blocks], axis=0)
            got = jnp.dot(mixer, data, preferred_element_type=jnp.float32)
            got = got[:BLOCK] + got[BLOCK:]
            if mode == "add":
                got = got + rest[0][BLOCK * b:BLOCK * (b + 1), cols].astype(jnp.float32)
            if mode == "joined":
                rest[0][BLOCK * b:BLOCK * (b + 1), cols] = got.astype(jnp.bfloat16)
            else:
                rest[-RING + b][:, cols] = got.astype(jnp.bfloat16)


def combine(info, first_expert, blocks, metas, width, column=0, mode="blocks", add=None):
    row_spec = pl.BlockSpec((BLOCK, width), lambda i: (0, column))
    meta_spec = pl.BlockSpec((BLOCK, META), lambda i: (0, width // META))
    extra = [] if add is None else [add]
    if mode == "joined":
        out, out_specs = jax.ShapeDtypeStruct((RING * BLOCK, width), jnp.bfloat16), VMEM_SPEC
    else:
        out, out_specs = [jax.ShapeDtypeStruct((BLOCK, width), jnp.bfloat16)] * RING, [VMEM_SPEC] * RING
    return pl.pallas_call(
        functools.partial(combine_kernel, first_expert, width, len(blocks), mode),
        grid=(1,),
        out_shape=out,
        in_specs=[SMEM_SPEC] + [row_spec] * len(blocks) + [meta_spec] * RING + [VMEM_SPEC] * len(extra),
        out_specs=out_specs,
        compiler_params=pltpu.CompilerParams(vmem_limit_bytes=SMALL_VMEM),
        cost_estimate=pl.CostEstimate(
            flops=4 * len(blocks) * BLOCK * BLOCK * width, bytes_accessed=24 * BLOCK * width, transcendentals=0),
    )(info, *blocks, *metas, *extra)


def weight_copies(chunks, gate_hbm, up_hbm, w_in, in_sem):
    half = w_in.shape[1] // 2
    copies, at = [], 0
    for i, (col, size) in enumerate(chunks):
        col = pl.multiple_of(col, BLOCK)
        copies.append((
            pltpu.make_async_copy(gate_hbm.at[pl.ds(col, size)], w_in.at[pl.ds(at, size), pl.ds(0, half)],
                                  in_sem.at[2 * i]),
            pltpu.make_async_copy(up_hbm.at[pl.ds(col, size)], w_in.at[pl.ds(at, size), pl.ds(half, half)],
                                  in_sem.at[2 * i + 1])))
        at += size
    return copies


def block_copies(blocks, target, sems, first):
    return [pltpu.make_async_copy(blocks[r], target.at[pl.ds(r * BLOCK, BLOCK)], sems.at[first + r])
            for r in range(RING)]


def start_all(copies):
    for copy in copies:
        copy.start()


def wait_all(copies):
    for copy in copies:
        copy.wait()


def project_kernel(info, *refs):
    blocks, (gate_hbm, up_hbm, total, x, w_in, x_sem, in_sem) = refs[:RING], refs[RING:]
    base = info[0] * TAIL
    steps = column_chunks(MAIN)
    x_copies = block_copies(blocks, x, x_sem, 0)
    in_copies = weight_copies([(base + start, size) for start, size in steps], gate_hbm, up_hbm, w_in, in_sem)
    start_all(x_copies)
    for pair in in_copies:
        start_all(pair)
    wait_all(x_copies)
    for (start, size), pair in zip(steps, in_copies):
        wait_all(pair)
        cols = slice(start, start + size)
        got = jnp.dot(x[:, cols], w_in[cols, :], preferred_element_type=jnp.float32)
        if start == 0:
            total[...] = got
        else:
            total[...] += got


def project(info, blocks, gate_w, up_w):
    rows, hid = RING * BLOCK, gate_w.shape[1]
    return pl.pallas_call(
        project_kernel,
        out_shape=jax.ShapeDtypeStruct((rows, 2 * hid), jnp.float32),
        in_specs=[SMEM_SPEC] + [HBM_SPEC] * 6,
        out_specs=VMEM_SPEC,
        scratch_shapes=[
            pltpu.VMEM((rows, MAIN), jnp.bfloat16), pltpu.VMEM((MAIN, 2 * hid), jnp.bfloat16),
            pltpu.SemaphoreType.DMA((RING,)), pltpu.SemaphoreType.DMA((2 * len(column_chunks(MAIN)),)),
        ],
        compiler_params=pltpu.CompilerParams(vmem_limit_bytes=LARGE_VMEM),
        cost_estimate=pl.CostEstimate(
            flops=4 * rows * MAIN * hid, bytes_accessed=2 * (2 * MAIN * hid + rows * MAIN), transcendentals=0),
    )(info, *blocks, gate_w, up_w)


def expert_kernel(info, *refs):
    near, far, side = refs[0], refs[1:1 + RING], refs[1 + RING:1 + 2 * RING]
    gate_hbm, up_hbm, down_hbm = refs[9:12]
    main_outs, side_outs, hidden_far = refs[12:16], refs[16:20], refs[20]
    (x2, xs, w_in, w_out, a1, a2, a_s, h1, h2, hs, o1, o_s,
     x_sem, in_sem, down_sem, out_sem) = refs[21:]
    core = info[0]
    first = core == 0
    half = w_in.shape[1] // 2
    at_main, at_far = core * TAIL, (1 - core) * TAIL
    at_side = (MAIN + core * SIDE, MAIN + (1 - core) * SIDE)
    main_steps, side_steps = column_chunks(MAIN), column_chunks(SIDE)

    steps = [(xs, a_s, h * SIDE + start, size, at_side[h] + start) for h in range(2) for start, size in side_steps]
    steps += [(x2, a2, start, size, at_far + start) for start, size in main_steps]
    side_copies, far_copies = block_copies(side, xs, x_sem, 0), block_copies(far, x2, x_sem, RING)
    near_copy = pltpu.make_async_copy(near, a1, x_sem.at[2 * RING])
    in_copies = weight_copies([step[3:][::-1] for step in steps], gate_hbm, up_hbm, w_in, in_sem)
    outs = [(0, o1, main_outs, start, size, at_main + start) for start, size in main_steps]
    outs += [(1, o_s, side_outs, h * SIDE + start, size, at_side[h] + start)
             for h in range(2) for start, size in side_steps]
    down_copies, at = [], 0
    for i, (_, _, _, _, size, col) in enumerate(outs):
        down_copies.append(pltpu.make_async_copy(
            down_hbm.at[:, pl.ds(pl.multiple_of(col, BLOCK), size)], w_out.at[:, pl.ds(at, size)], down_sem.at[i]))
        at += size
    start_all(side_copies)
    start_all(in_copies[0])
    start_all(far_copies)
    for pair in in_copies[1:]:
        start_all(pair)
    near_copy.start()
    start_all(down_copies)

    at = 0
    for (x, total, off, size, _), pair in zip(steps, in_copies):
        if off == 0:
            wait_all(side_copies if x is xs else far_copies)
        wait_all(pair)
        got = jnp.dot(x[:, off:off + size], w_in[at:at + size, :], preferred_element_type=jnp.float32)
        if off == 0:
            total[...] = got
        else:
            total[...] += got
        at += size
    near_copy.wait()

    def activate(i, carry):
        x, y, z = i // 16, i // 4 % 4, i % 4
        left, right = i, z * 16 + x * 4 + y
        i1 = pl.multiple_of(jnp.where(first, left, right) * 8, 8)
        i2 = pl.multiple_of(jnp.where(first, right, left) * 8, 8)
        i3 = pl.multiple_of((y * 16 + z * 4 + x) * 8, 8)
        both = a1[pl.ds(i1, 8)] + a2[pl.ds(i2, 8)] + a_s[pl.ds(i3, 8)]
        gate, up = both[:, :half], both[:, half:]
        value = gate / (1.0 + jnp.exp(-gate)) * up
        h1[pl.ds(i1, 8)] = value
        h2[pl.ds(i2, 8)] = value
        hs[pl.ds(i3, 8)] = value
        return carry

    lax.fori_loop(0, RING ** 3, activate, 0, unroll=4)
    hidden_far[...] = h2[...].astype(jnp.bfloat16)
    hidden = (h1[...].astype(jnp.bfloat16), hs[...].astype(jnp.bfloat16))
    out_copies, at = [], 0
    for i, ((part, rows, targets, off, size, _), copy) in enumerate(zip(outs, down_copies)):
        copy.wait()
        got = jnp.dot(hidden[part], w_out[:, at:at + size], preferred_element_type=jnp.float32)
        rows[:, off:off + size] = got.astype(jnp.bfloat16)
        for r in range(RING):
            out_copies.append(pltpu.make_async_copy(
                rows.at[pl.ds(r * BLOCK, BLOCK), pl.ds(off, size)],
                targets[r].at[:, pl.ds(off, size)], out_sem.at[RING * i + r]))
            out_copies[-1].start()
        at += size
    wait_all(out_copies)


def expert(info, near, far, side, gate_w, up_w, down_w):
    rows, (width, hid) = RING * BLOCK, gate_w.shape
    n_main, n_side = len(column_chunks(MAIN)), len(column_chunks(SIDE))
    part = MAIN + 2 * SIDE
    block = lambda w: jax.ShapeDtypeStruct((BLOCK, w), jnp.bfloat16)
    bf, f32 = jnp.bfloat16, jnp.float32
    out = pl.pallas_call(
        expert_kernel,
        out_shape=[block(MAIN)] * RING + [block(2 * SIDE)] * RING + [jax.ShapeDtypeStruct((rows, hid), bf)],
        in_specs=[SMEM_SPEC] + [HBM_SPEC] * 12,
        out_specs=[HBM_SPEC] * 8 + [VMEM_SPEC],
        scratch_shapes=[
            pltpu.VMEM((rows, MAIN), bf), pltpu.VMEM((rows, 2 * SIDE), bf),
            pltpu.VMEM((part, 2 * hid), bf), pltpu.VMEM((hid, part), bf),
            pltpu.VMEM((rows, 2 * hid), f32), pltpu.VMEM((rows, 2 * hid), f32), pltpu.VMEM((rows, 2 * hid), f32),
            pltpu.VMEM((rows, hid), f32), pltpu.VMEM((rows, hid), f32), pltpu.VMEM((rows, hid), f32),
            pltpu.VMEM((rows, MAIN), bf), pltpu.VMEM((rows, 2 * SIDE), bf),
            pltpu.SemaphoreType.DMA((2 * RING + 1,)), pltpu.SemaphoreType.DMA((2 * (n_main + 2 * n_side),)),
            pltpu.SemaphoreType.DMA((n_main + 2 * n_side,)),
            pltpu.SemaphoreType.DMA((RING * (n_main + 2 * n_side),)),
        ],
        compiler_params=pltpu.CompilerParams(vmem_limit_bytes=LARGE_VMEM),
        cost_estimate=pl.CostEstimate(
            flops=6 * rows * part * hid, bytes_accessed=2 * (3 * part * hid + 2 * rows * part),
            transcendentals=rows * hid),
    )(info, near, *far, *side, gate_w, up_w, down_w)
    return list(out[:RING]), list(out[RING:2 * RING]), out[2 * RING]


def spread_kernel(info, hidden, down_hbm, *refs):
    outs, (w_out, down_sem) = refs[:RING], refs[RING:]
    base = (1 - info[0]) * TAIL
    steps = column_chunks(MAIN)
    copies = [pltpu.make_async_copy(
        down_hbm.at[:, pl.ds(pl.multiple_of(base + start, BLOCK), size)], w_out.at[:, pl.ds(start, size)],
        down_sem.at[i]) for i, (start, size) in enumerate(steps)]
    start_all(copies)
    for (start, size), copy in zip(steps, copies):
        copy.wait()
        cols = slice(start, start + size)
        got = jnp.dot(hidden[...], w_out[:, cols], preferred_element_type=jnp.float32).astype(jnp.bfloat16)
        for r in range(RING):
            outs[r][:, cols] = got[BLOCK * r:BLOCK * (r + 1)]


def spread(info, hidden, down_w):
    rows, hid = hidden.shape
    out = pl.pallas_call(
        spread_kernel,
        out_shape=[jax.ShapeDtypeStruct((BLOCK, MAIN), jnp.bfloat16)] * RING,
        in_specs=[SMEM_SPEC, VMEM_SPEC, HBM_SPEC],
        out_specs=[VMEM_SPEC] * RING,
        scratch_shapes=[
            pltpu.VMEM((hid, MAIN), jnp.bfloat16), pltpu.SemaphoreType.DMA((len(column_chunks(MAIN)),))],
        compiler_params=pltpu.CompilerParams(vmem_limit_bytes=LARGE_VMEM),
        cost_estimate=pl.CostEstimate(
            flops=2 * rows * MAIN * hid, bytes_accessed=2 * MAIN * (hid + rows), transcendentals=0),
    )(info, hidden, down_w)
    return list(out)


def summed(blocks):
    return sum(b.astype(jnp.float32) for b in blocks).astype(jnp.bfloat16)


def split_rows(value):
    return list(value.reshape(RING, -1, value.shape[-1]))


def per_device(tokens, picks, mix_weights, pairs, gate_weight, up_weight, down_weight):
    tok_rows, width = tokens.shape
    c = lax.axis_index("c")
    x = lax.axis_index("xh") * 2 + lax.axis_index("dp")
    z = lax.axis_index("z")
    y = lax.axis_index("y")
    first = c == 0

    shifts = jnp.array(SHIFTS, jnp.int32)
    place = lambda x, z, y: ((x // 2 * RING + z) * RING + y) * CORES + c + 0 * shifts
    along_x = place((x + shifts) % RING, z, y)
    along_z = place(x, (z + shifts) % RING, y)
    along_y = place(x, z, (y + shifts) % RING)
    info = jnp.concatenate([jnp.stack([c, c, c, c]), jnp.where(first, along_x, along_z), along_y]).astype(jnp.int32)
    at_main, at_side = 4, 8

    moved = jnp.any(picks[:, :, None] == pairs.reshape(-1), axis=-1)
    owner = jnp.where(moved, picks ^ 32, picks)
    mix_hi = lax.reduce_precision(mix_weights, 8, 7)
    meta = jnp.concatenate([owner.astype(jnp.float32), mix_hi, mix_weights - mix_hi], axis=1)
    meta = jnp.pad(meta, ((0, 0), (0, META - 3 * TOP))).astype(jnp.bfloat16)

    left = jnp.concatenate([tokens[:, :MAIN], meta, tokens[:, MAIN:MAIN + SIDE], meta], axis=1)
    right = jnp.concatenate([tokens[:, TAIL:], meta, tokens[:, MAIN + SIDE:TAIL], meta], axis=1)
    mine = jnp.where(first, left, right)
    theirs = other_core(jnp.where(first, right, left))
    both = jnp.where(first, jnp.concatenate([mine, theirs]), jnp.concatenate([theirs, mine]))
    main, side = both[:, :MAIN + META], both[:, MAIN + META:]
    main, side = together(gathered(main, MAIN_ROUTE[0]), gathered(side, SIDE_ROUTE[0]))
    main, side = together(jnp.concatenate(main, axis=0), jnp.concatenate(side, axis=0))
    main, side = together(gathered(main, MAIN_ROUTE[1]), gathered(side, SIDE_ROUTE[1]))

    main_hop, side_hop = MAIN_ROUTE[2], SIDE_ROUTE[2]
    side_far = [other_core(b) for b in side]
    main_own, main_far = pack(info, at_main, CORES, main)
    main_own, side_far = together(main_own, side_far)
    own, here = together(hop(main_own, main_hop, ring_perm, (1, 2, 3)), hop(main_far, main_hop, ring_perm, (0,)))
    side_own, _ = pack(info, at_side, 1, side, side_far)
    across = hop(side_own, side_hop, ring_perm, (3,))
    main_far, side_own, own = together(main_far, side_own, own)
    far = hop(main_far, main_hop, ring_perm, (1, 2, 3), cross=True)
    beside = hop(side_own, side_hop, ring_perm, (1, 2))
    gate_w, up_w, down_w = gate_weight[0], up_weight[0], down_weight[0]
    near = project(info, main_own[:1] + own, gate_w, up_w)
    far, beside, across = together(far, beside, across)
    main_own, side_own, hidden = expert(
        info, near, here + far, side_own[:1] + beside + across, gate_w, up_w, down_w)
    main_far = spread(info, hidden, down_w)
    own, beside = together(
        hop(main_own, main_hop, back_perm, (1, 2, 3)), hop(side_own, side_hop, back_perm, (1, 2)))
    main_far, side_own, own = together(main_far, side_own, own)
    far, across = together(
        hop(main_far, main_hop, back_perm, (1, 2, 3, 0), cross=True), hop(side_own, side_hop, back_perm, (3,)))
    main_own = main_own[:1] + own
    main_far = far[3:] + far[:3]
    side_own = side_own[:1] + beside + across
    side_add = other_core(combine(info, at_side, side_own, side, SIDE, 1, "joined"))
    main = combine(info, at_main, main_own + main_far, main, MAIN)
    side = combine(info, at_side, side_own, side, SIDE, 0, "add", side_add)
    main, side = together(scattered(main, MAIN_ROUTE[1]), scattered(side, SIDE_ROUTE[1]))
    main, side = together(summed(main), summed(side))
    main, side = together(
        scattered(split_rows(main), MAIN_ROUTE[0]), scattered(split_rows(side), SIDE_ROUTE[0]))
    main, side = summed(main), summed(side)
    done = jnp.concatenate([main, side], axis=1)
    own = jnp.where(first, done[:tok_rows], done[tok_rows:])
    rest = other_core(jnp.where(first, done[tok_rows:], done[:tok_rows]))
    lower = jnp.where(first, own, rest)
    upper = jnp.where(first, rest, own)
    return jnp.concatenate([lower, upper[:, MAIN:], upper[:, :MAIN]], axis=1)


def solution(mesh):
    fine = Mesh(mesh.devices.reshape(2, 2, RING, RING, CORES), ALL_AXES)
    experts = ("xh", "z", "y", "c")
    return jax.shard_map(
        per_device,
        mesh=fine,
        in_specs=(
            P(ALL_AXES, None),
            P(ALL_AXES, None),
            P(ALL_AXES, None),
            P(),
            P(experts, None, "dp"),
            P(experts, None, "dp"),
            P(experts, "dp", None),
        ),
        out_specs=P(ALL_AXES, None),
        check_vma=False,
    )
```

profile of v0, /device:TPU:1, one launch (start us, length us, event | category | flops | bytes accessed | tf_op | source)
XLA Modules:
  0.0 203.5 jit_solution(12971985241182344882)
XLA Ops:
  5.4 1.5 collective-permute-start
  8.0 3.1 %collective-permute-start.3 = (bf16[32,2688]{1,0:T(8,128)(2,1)S(1)}, bf16[32,2688]{1,0:T(8,128)(2,1)S(1)}, u32[]{:S(2)}, u32[]{:S(2)}) collective-permute-start(bf16[32,2688]{1,0:T(8,128)(2,1)S(1)} %slice.50), channel_id=1, source_target_pairs={{0,16},{1,5},{2,18},{3,7},{4,20},{5,1},{6,22},{7,3},{8,24},{9,13},... | collective-permute-start | bytes 516104 | tf_op jit(solution)/shard_map/ppermute | solution.py:52
  12.5 2.7 %collective-permute-start.6 = (bf16[32,1152]{1,0:T(8,128)(2,1)S(1)}, bf16[32,1152]{1,0:T(8,128)(2,1)S(1)}, u32[]{:S(2)}, u32[]{:S(2)}) collective-permute-start(bf16[32,1152]{1,0:T(8,128)(2,1)S(1)} %slice.51), channel_id=1, source_target_pairs={{0,32},{1,33},{2,34},{3,35},{4,36},{5,37},{6,38},{7,39},{8,40},{9,... | collective-permute-start | bytes 221192 | tf_op jit(solution)/shard_map/ppermute | solution.py:52
  17.2 1.5 collective-permute-start.4
  18.8 2.9 %collective-permute-done.4 = bf16[32,1152]{1,0:T(8,128)(2,1)S(1)} collective-permute-done((bf16[32,1152]{1,0:T(8,128)(2,1)S(1)}, bf16[32,1152]{1,0:T(8,128)(2,1)S(1)}, u32[]{:S(2)}, u32[]{:S(2)}) %collective-permute-start.4) | collective-permute-done | bytes 73760 | tf_op jit(solution)/shard_map/ppermute | solution.py:52
  21.8 1.9 collective-permute-start.9
  25.1 3.9 %collective-permute-start.12 = (bf16[128,1152]{1,0:T(8,128)(2,1)S(1)}, bf16[128,1152]{1,0:T(8,128)(2,1)S(1)}, u32[]{:S(2)}, u32[]{:S(2)}) collective-permute-start(bf16[128,1152]{1,0:T(8,128)(2,1)S(1)} %pad_maximum_fusion.1.refs_0_.refs_4_), channel_id=1, source_target_pairs={{0,16},{1,17},{2,18},{3,19},{4,20},{5,21},{6,22},{7,23},{8,24},{9,... | collective-permute-start | bytes 884744 | tf_op jit(solution)/shard_map/ppermute | solution.py:52
  29.5 3.7 %collective-permute-done.12.refs_3_.refs_7_ = bf16[128,1152]{1,0:T(8,128)(2,1)S(1)} collective-permute-done((bf16[128,1152]{1,0:T(8,128)(2,1)S(1)}, bf16[128,1152]{1,0:T(8,128)(2,1)S(1)}, u32[]{:S(2)}, u32[]{:S(2)}) %collective-permute-start.12) | collective-permute-done | bytes 294944 | tf_op jit(solution)/shard_map/ppermute | solution.py:52
  33.2 1.3 collective-permute-start.10
  34.5 5.6 %collective-permute-done.11.refs_2_.refs_6_ = bf16[128,1152]{1,0:T(8,128)(2,1)} collective-permute-done((bf16[128,1152]{1,0:T(8,128)(2,1)S(1)}, bf16[128,1152]{1,0:T(8,128)(2,1)}, u32[]{:S(2)}, u32[]{:S(2)}) %collective-permute-start.11) | collective-permute-done | bytes 294944 | tf_op jit(solution)/shard_map/ppermute | solution.py:52
  40.0 1.2 collective-permute-done.10.refs_1_.refs_5_
  41.3 13.9 %collective-permute-start.13 = (bf16[128,1152]{1,0:T(8,128)(2,1)S(1)}, bf16[128,1152]{1,0:T(8,128)(2,1)}, u32[]{:S(2)}, u32[]{:S(2)}) collective-permute-start(bf16[128,1152]{1,0:T(8,128)(2,1)S(1)} %pad_maximum_fusion.1.refs_0_.refs_4_), channel_id=1, source_target_pairs={{0,1},{1,0},{2,3},{3,2},{4,5},{5,4},{6,7},{7,6},{8,9},{9,8},{10,11... | collective-permute-start | bytes 884744 | tf_op jit(solution)/shard_map/ppermute | solution.py:60
  55.9 2.6 %shard_map.82 = (bf16[128,2560]{1,0:T(8,128)(2,1)S(1)}, bf16[128,2560]{1,0:T(8,128)(2,1)S(1)}, bf16[128,2560]{1,0:T(8,128)(2,1)S(1)}, bf16[128,2560]{1,0:T(8,128...) custom-call(s32[12]{0:T(128)S(1)} %concatenate.31.info, ...), custom_call_target="tpu_custom_call" | custom-call | flops 671088640 | bytes 5242880 | tf_op jit(solution)/shard_map/pallas_call | solution.py:126
  59.9 2.7 %collective-permute-start.18 = (bf16[128,2560]{1,0:T(8,128)(2,1)S(1)}, bf16[128,2560]{1,0:T(8,128)(2,1)S(1)}, u32[]{:S(2)}, u32[]{:S(2)}) collective-permute-start(bf16[128,2560]{1,0:T(8,128)(2,1)S(1)} %get-tuple-element.156), channel_id=1, source_target_pairs={{0,96},{1,25},{2,98},{3,27},{4,100},{5,29},{6,102},{7,31},{8,104},... | collective-permute-start | bytes 1966088 | tf_op jit(solution)/shard_map/ppermute | solution.py:64
  62.6 3.5 %shard_map.83 = (bf16[128,2048]{1,0:T(8,128)(2,1)S(1)}, bf16[128,2048]{1,0:T(8,128)(2,1)}, bf16[128,2048]{1,0:T(8,128)(2,1)S(1)}, bf16[128,2048]{1,0:T(8,128)(2,1)S(1)}) custom-call(s32[12]{0:T(128)S(1)} %concatenate.31.info, bf16[128,1152]{1,0:T(8,128)(2,1)S(1)} %pad_maximum_fusion.1.refs_0_.refs_4_, ...), custom_call_target="tpu_custom_call" | custom-call | flops 268435456 | bytes 4194304 | tf_op jit(solution)/shard_map/pallas_call | solution.py:126
  68.1 9.8 %collective-permute-done.17.refs_1_ = bf16[128,2560]{1,0:T(8,128)(2,1)S(1)} collective-permute-done((bf16[128,2560]{1,0:T(8,128)(2,1)S(1)}, bf16[128,2560]{1,0:T(8,128)(2,1)S(1)}, u32[]{:S(2)}, u32[]{:S(2)}) %collective-permute-start.17) | collective-permute-done | bytes 655392 | tf_op jit(solution)/shard_map/ppermute | solution.py:64
  78.0 2.2 %collective-permute-start.22 = (bf16[128,2560]{1,0:T(8,128)(2,1)S(1)}, bf16[128,2560]{1,0:T(8,128)(2,1)S(1)}, u32[]{:S(2)}, u32[]{:S(2)}) collective-permute-start(bf16[128,2560]{1,0:T(8,128)(2,1)S(1)} %get-tuple-element.166), channel_id=1, source_target_pairs={{0,97},{1,24},{2,99},{3,26},{4,101},{5,28},{6,103},{7,30},{8,105},... | collective-permute-start | bytes 1966088 | tf_op jit(solution)/shard_map/ppermute | solution.py:64
  80.2 2.2 %collective-permute-start.23 = (bf16[128,2560]{1,0:T(8,128)(2,1)S(1)}, bf16[128,2560]{1,0:T(8,128)(2,1)S(1)}, u32[]{:S(2)}, u32[]{:S(2)}) collective-permute-start(bf16[128,2560]{1,0:T(8,128)(2,1)S(1)} %get-tuple-element.167), channel_id=1, source_target_pairs={{0,33},{1,16},{2,35},{3,18},{4,37},{5,20},{6,39},{7,22},{8,41},{9,... | collective-permute-start | bytes 1966088 | tf_op jit(solution)/shard_map/ppermute | solution.py:64
  82.4 2.7 %collective-permute-start.25 = (bf16[128,2048]{1,0:T(8,128)(2,1)S(1)}, bf16[128,2048]{1,0:T(8,128)(2,1)}, u32[]{:S(2)}, u32[]{:S(2)}) collective-permute-start(bf16[128,2048]{1,0:T(8,128)(2,1)S(1)} %get-tuple-element.169), channel_id=1, source_target_pairs={{0,6},{1,7},{2,0},{3,1},{4,2},{5,3},{6,4},{7,5},{8,14},{9,15},{10,... | collective-permute-start | bytes 1572872 | tf_op jit(solution)/shard_map/ppermute | solution.py:64
  85.1 7.8 %shard_map.84.refs_0_ = f32[512,1024]{1,0:T(8,128)} custom-call(s32[12]{0:T(128)} %copy-done.4, bf16[128,2560]{1,0:T(8,128)(2,1)} %copy-done.2, bf16[128,2560]{1,0:T(8,128)(2,1)} %copy-done.6, bf16[128,2560]{1,0:T(8,128)(2,1)} %copy-done.7, bf16[128,2560]{1,0:T(8,128)(2,1)} %copy-done.8, bf16[7168,512]{1,0:T(8,128)(2,1)} %bitcast.4, bf16[7168,512]{1,0:T(8,128)(2,1)} %bitcast.6), custom_call_target="tpu_custom_call" | custom-call | flops 2684354560 | bytes 7864320 | tf_op jit(solution)/shard_map/pallas_call | solution.py:235
  92.9 3.6 %collective-permute-done.24.refs_6_ = bf16[128,2048]{1,0:T(8,128)(2,1)} collective-permute-done((bf16[128,2048]{1,0:T(8,128)(2,1)}, bf16[128,2048]{1,0:T(8,128)(2,1)}, u32[]{:S(2)}, u32[]{:S(2)}) %collective-permute-start.24) | collective-permute-done | bytes 524320 | tf_op jit(solution)/shard_map/ppermute | solution.py:64
  98.4 16.1 %shard_map.85 = (bf16[128,2560]{1,0:T(8,128)(2,1)}, bf16[128,2560]{1,0:T(8,128)(2,1)}, bf16[128,2560]{1,0:T(8,128)(2,1)}, bf16[128,2560]{1,0:T(8,128)(2,1)}, bf1...) custom-call(s32[12]{0:T(128)} %copy-done.4, ...), custom_call_target="tpu_custom_call" | custom-call | flops 7247757312 | bytes 23592960 | tf_op jit(solution)/shard_map/pallas_call | solution.py:334
  114.5 1.9 collective-permute-start.27
  116.4 1.3 collective-permute-start.29
  117.7 2.2 %collective-permute-start.30 = (bf16[128,2048]{1,0:T(8,128)(2,1)}, bf16[128,2048]{1,0:T(8,128)(2,1)S(1)}, u32[]{:S(2)}, u32[]{:S(2)}) collective-permute-start(bf16[128,2048]{1,0:T(8,128)(2,1)} %get-tuple-element.184), channel_id=1, source_target_pairs={{2,0},{3,1},{4,2},{5,3},{6,4},{7,5},{0,6},{1,7},{10,8},{11,9},{12,... | collective-permute-start | bytes 1572872 | tf_op jit(solution)/shard_map/ppermute | solution.py:64
  119.9 5.8 %shard_map.86 = (bf16[128,2560]{1,0:T(8,128)(2,1)}, bf16[128,2560]{1,0:T(8,128)(2,1)}, bf16[128,2560]{1,0:T(8,128)(2,1)}, bf16[128,2560]{1,0:T(8,128)(2,1)}) custom-call(s32[12]{0:T(128)} %copy-done.4, bf16[512,512]{1,0:T(8,128)(2,1)} %get-tuple-element.178.hidden, bf16[512,7168]{1,0:T(8,128)(2,1)} %bitcast.9), custom_call_target="tpu_custom_call" | custom-call | flops 1342177280 | bytes 5242880 | tf_op jit(solution)/shard_map/pallas_call | solution.py:375
  125.7 4.3 %collective-permute-done.30.refs_1_ = bf16[128,2048]{1,0:T(8,128)(2,1)S(1)} collective-permute-done((bf16[128,2048]{1,0:T(8,128)(2,1)}, bf16[128,2048]{1,0:T(8,128)(2,1)S(1)}, u32[]{:S(2)}, u32[]{:S(2)}) %collective-permute-start.30) | collective-permute-done | bytes 524320 | tf_op jit(solution)/shard_map/ppermute | solution.py:64
  130.1 3.0 %collective-permute-done.31.refs_2_ = bf16[128,2048]{1,0:T(8,128)(2,1)S(1)} collective-permute-done((bf16[128,2048]{1,0:T(8,128)(2,1)}, bf16[128,2048]{1,0:T(8,128)(2,1)S(1)}, u32[]{:S(2)}, u32[]{:S(2)}) %collective-permute-start.31) | collective-permute-done | bytes 524320 | tf_op jit(solution)/shard_map/ppermute | solution.py:64
  133.1 1.5 collective-permute-done.28.refs_2_
  134.6 3.4 %collective-permute-start.32 = (bf16[128,2560]{1,0:T(8,128)(2,1)}, bf16[128,2560]{1,0:T(8,128)(2,1)S(1)}, u32[]{:S(2)}, u32[]{:S(2)}) collective-permute-start(bf16[128,2560]{1,0:T(8,128)(2,1)} %get-tuple-element.196), channel_id=1, source_target_pairs={{65,0},{8,1},{67,2},{10,3},{69,4},{12,5},{71,6},{14,7},{73,8},{16,... | collective-permute-start | bytes 1966088 | tf_op jit(solution)/shard_map/ppermute | solution.py:64
  138.8 1.5 collective-permute-start.35
  140.3 14.7 %collective-permute-done.36.refs_3_ = bf16[128,2048]{1,0:T(8,128)(2,1)S(1)} collective-permute-done((bf16[128,2048]{1,0:T(8,128)(2,1)S(1)}, bf16[128,2048]{1,0:T(8,128)(2,1)S(1)}, u32[]{:S(2)}, u32[]{:S(2)}) %collective-permute-start.36) | collective-permute-done | bytes 524320 | tf_op jit(solution)/shard_map/ppermute | solution.py:64
  155.0 1.3 collective-permute-done.34.refs_7_
  156.4 2.4 %shard_map.88 = bf16[512,1024]{1,0:T(8,128)(2,1)S(1)} custom-call(s32[12]{0:T(128)S(1)} %copy-done.5, bf16[128,2048]{1,0:T(8,128)(2,1)S(1)} %copy-done, bf16[128,2048]{1,0:T(8,128)(2,1)S(1)} %collective-permute-done.30.refs_1_, bf16[128,2048]{1,0:T(8,128)(2,1)S(1)} %collective-permute-done.31.refs_2_, bf16[128,2048]{1,0:T(8,128)(2,1)S(1)} %collective-permute-done.36.refs_3_, ...), custom_call_target="tpu_custom_call" | custom-call | flops 268435456 | bytes 3145728 | tf_op jit(solution)/shard_map/pallas_call | solution.py:172
  158.9 3.0 %shard_map.87 = (bf16[128,2560]{1,0:T(8,128)(2,1)S(1)}, bf16[128,2560]{1,0:T(8,128)(2,1)S(1)}, bf16[128,2560]{1,0:T(8,128)(2,1)S(1)}, bf16[128,2560]{1,0:T(8,128)(2,1)S(1)}) custom-call(s32[12]{0:T(128)S(1)} %copy-done.5, bf16[128,2560]{1,0:T(8,128)(2,1)S(1)} %copy-done.1, bf16[128,2560]{1,0:T(8,128)(2,1)S(1)} %collective-permute-done.27.refs_1_, ...), custom_call_target="tpu_custom_call" | custom-call | flops 1342177280 | bytes 7864320 | tf_op jit(solution)/shard_map/pallas_call | solution.py:172
  163.4 2.6 %collective-permute-start.39 = (bf16[128,2560]{1,0:T(8,128)(2,1)S(1)}, bf16[128,2560]{1,0:T(8,128)(2,1)S(1)}, u32[]{:S(2)}, u32[]{:S(2)}) collective-permute-start(bf16[128,2560]{1,0:T(8,128)(2,1)S(1)} %get-tuple-element.208), channel_id=1, source_target_pairs={{4,0},{33,1},{6,2},{35,3},{0,4},{37,5},{2,6},{39,7},{12,8},{41,9},... | collective-permute-start | bytes 1966088 | tf_op jit(solution)/shard_map/ppermute | solution.py:56
  166.1 2.4 %shard_map.89 = (bf16[128,1024]{1,0:T(8,128)(2,1)S(1)}, bf16[128,1024]{1,0:T(8,128)(2,1)S(1)}, bf16[128,1024]{1,0:T(8,128)(2,1)S(1)}, bf16[128,1024]{1,0:T(8,128)(2,1)S(1)}) custom-call(s32[12]{0:T(128)S(1)} %copy-done.5, bf16[128,2048]{1,0:T(8,128)(2,1)S(1)} %copy-done, bf16[128,2048]{1,0:T(8,128)(2,1)S(1)} %collective-permute-done.30.refs_1_, ...), custom_call_target="tpu_custom_call" | custom-call | flops 268435456 | bytes 3145728 | tf_op jit(solution)/shard_map/pallas_call | solution.py:172
  170.0 1.7 collective-permute-done.37
  171.7 2.3 %collective-permute-start.43 = (bf16[128,1024]{1,0:T(8,128)(2,1)S(1)}, bf16[128,1024]{1,0:T(8,128)(2,1)S(1)}, u32[]{:S(2)}, u32[]{:S(2)}) collective-permute-start(bf16[128,1024]{1,0:T(8,128)(2,1)S(1)} %get-tuple-element.216), channel_id=1, source_target_pairs={{16,0},{17,1},{18,2},{19,3},{20,4},{21,5},{22,6},{23,7},{24,8},{25... | collective-permute-start | bytes 786440 | tf_op jit(solution)/shard_map/ppermute | solution.py:56
  174.0 7.4 %collective-permute-done.39 = bf16[128,2560]{1,0:T(8,128)(2,1)S(1)} collective-permute-done((bf16[128,2560]{1,0:T(8,128)(2,1)S(1)}, bf16[128,2560]{1,0:T(8,128)(2,1)S(1)}, u32[]{:S(2)}, u32[]{:S(2)}) %collective-permute-start.39) | collective-permute-done | bytes 655392 | tf_op jit(solution)/shard_map/ppermute | solution.py:56
  181.4 2.9 %collective-permute-done.42 = bf16[128,1024]{1,0:T(8,128)(2,1)S(1)} collective-permute-done((bf16[128,1024]{1,0:T(8,128)(2,1)S(1)}, bf16[128,1024]{1,0:T(8,128)(2,1)S(1)}, u32[]{:S(2)}, u32[]{:S(2)}) %collective-permute-start.42) | collective-permute-done | bytes 262176 | tf_op jit(solution)/shard_map/ppermute | solution.py:56
  184.8 3.5 %collective-permute-start.46 = (bf16[32,2560]{1,0:T(8,128)(2,1)S(1)}, bf16[32,2560]{1,0:T(8,128)(2,1)S(1)}, u32[]{:S(2)}, u32[]{:S(2)}) collective-permute-start(bf16[32,2560]{1,0:T(8,128)(2,1)S(1)} %get-tuple-element.235), channel_id=1, source_target_pairs={{16,0},{5,1},{18,2},{7,3},{20,4},{1,5},{22,6},{3,7},{24,8},{13,9},... | collective-permute-start | bytes 491528 | tf_op jit(solution)/shard_map/ppermute | solution.py:56
  188.3 2.7 %collective-permute-start.44 = (bf16[32,2560]{1,0:T(8,128)(2,1)S(1)}, bf16[32,2560]{1,0:T(8,128)(2,1)S(1)}, u32[]{:S(2)}, u32[]{:S(2)}) collective-permute-start(bf16[32,2560]{1,0:T(8,128)(2,1)S(1)} %get-tuple-element.237), channel_id=1, source_target_pairs={{8,0},{3,1},{10,2},{5,3},{12,4},{7,5},{14,6},{1,7},{16,8},{11,9},{... | collective-permute-start | bytes 491528 | tf_op jit(solution)/shard_map/ppermute | solution.py:56
  191.1 1.9 collective-permute-start.48
  193.1 2.8 %collective-permute-done.49 = bf16[32,1024]{1,0:T(8,128)(2,1)S(1)} collective-permute-done((bf16[32,1024]{1,0:T(8,128)(2,1)S(1)}, bf16[32,1024]{1,0:T(8,128)(2,1)S(1)}, u32[]{:S(2)}, u32[]{:S(2)}) %collective-permute-start.49) | collective-permute-done | bytes 65568 | tf_op jit(solution)/shard_map/ppermute | solution.py:56
  195.8 1.3 collective-permute-start.47
  197.1 1.8 collective-permute-done.47
  199.1 2.6 %collective-permute-start.50 = (bf16[16,3584]{1,0:T(8,128)(2,1)S(1)}, bf16[16,3584]{1,0:T(8,128)(2,1)S(1)}, u32[]{:S(2)}, u32[]{:S(2)}) collective-permute-start(bf16[16,3584]{1,0:T(8,128)(2,1)S(1)} %broadcast_select_fusion.4), channel_id=1, source_target_pairs={{0,1},{1,0},{2,3},{3,2},{4,5},{5,4},{6,7},{7,6},{8,9},{9,8},{10,11... | collective-permute-start | bytes 344072 | tf_op jit(solution)/shard_map/ppermute | solution.py:60
  (125 shorter events, 24.5 us)
Async XLA Ops:
  8.0 13.7 %collective-permute-start.3 = (bf16[32,2688]{1,0:T(8,128)(2,1)S(1)}, bf16[32,2688]{1,0:T(8,128)(2,1)S(1)}, u32[]{:S(2)}, u32[]{:S(2)}) collective-permute-start(bf16[32,2688]{1,0:T(8,128)(2,1)S(1)} %slice.50), channel_id=1, source_target_pairs={{0,16},{1,5},{2,18},{3,7},{4,20},{5,1},{6,22},{7,3},{8,24},{9,13},... | collective-permute-start | bytes 516104 | tf_op jit(solution)/shard_map/ppermute | solution.py:52
  11.1 10.6 %collective-permute-start.2 = (bf16[32,2688]{1,0:T(8,128)(2,1)S(1)}, bf16[32,2688]{1,0:T(8,128)(2,1)S(1)}, u32[]{:S(2)}, u32[]{:S(2)}) collective-permute-start(bf16[32,2688]{1,0:T(8,128)(2,1)S(1)} %slice.50), channel_id=1, source_target_pairs={{0,24},{1,7},{2,26},{3,1},{4,28},{5,3},{6,30},{7,5},{8,0},{9,15},{... | collective-permute-start | bytes 516104 | tf_op jit(solution)/shard_map/ppermute | solution.py:52
  11.8 9.8 %collective-permute-start.1 = (bf16[32,2688]{1,0:T(8,128)(2,1)S(1)}, bf16[32,2688]{1,0:T(8,128)(2,1)S(1)}, u32[]{:S(2)}, u32[]{:S(2)}) collective-permute-start(bf16[32,2688]{1,0:T(8,128)(2,1)S(1)} %slice.50), channel_id=1, source_target_pairs={{0,8},{1,3},{2,10},{3,5},{4,12},{5,7},{6,14},{7,1},{8,16},{9,11},{... | collective-permute-start | bytes 516104 | tf_op jit(solution)/shard_map/ppermute | solution.py:52
  12.5 4.7 %collective-permute-start.6 = (bf16[32,1152]{1,0:T(8,128)(2,1)S(1)}, bf16[32,1152]{1,0:T(8,128)(2,1)S(1)}, u32[]{:S(2)}, u32[]{:S(2)}) collective-permute-start(bf16[32,1152]{1,0:T(8,128)(2,1)S(1)} %slice.51), channel_id=1, source_target_pairs={{0,32},{1,33},{2,34},{3,35},{4,36},{5,37},{6,38},{7,39},{8,40},{9,... | collective-permute-start | bytes 221192 | tf_op jit(solution)/shard_map/ppermute | solution.py:52
  17.2 4.4 %collective-permute-start.4 = (bf16[32,1152]{1,0:T(8,128)(2,1)S(1)}, bf16[32,1152]{1,0:T(8,128)(2,1)S(1)}, u32[]{:S(2)}, u32[]{:S(2)}) collective-permute-start(bf16[32,1152]{1,0:T(8,128)(2,1)S(1)} %slice.51), channel_id=1, source_target_pairs={{0,64},{1,65},{2,66},{3,67},{4,68},{5,69},{6,70},{7,71},{8,72},{9,... | collective-permute-start | bytes 221192 | tf_op jit(solution)/shard_map/ppermute | solution.py:52
  21.8 19.5 %collective-permute-start.9 = (bf16[128,2688]{1,0:T(8,128)(2,1)S(1)}, bf16[128,2688]{1,0:T(8,128)(2,1)S(1)}, u32[]{:S(2)}, u32[]{:S(2)}) collective-permute-start(bf16[128,2688]{1,0:T(8,128)(2,1)S(1)} %pad_maximum_fusion.refs_0_.refs_8_), channel_id=1, source_target_pairs={{0,4},{1,33},{2,6},{3,35},{4,0},{5,37},{6,2},{7,39},{8,12},{9,41},... | collective-permute-start | bytes 2064392 | tf_op jit(solution)/shard_map/ppermute | solution.py:52
  23.7 17.6 %collective-permute-start.8 = (bf16[128,2688]{1,0:T(8,128)(2,1)S(1)}, bf16[128,2688]{1,0:T(8,128)(2,1)S(1)}, u32[]{:S(2)}, u32[]{:S(2)}) collective-permute-start(bf16[128,2688]{1,0:T(8,128)(2,1)S(1)} %pad_maximum_fusion.refs_0_.refs_8_), channel_id=1, source_target_pairs={{0,6},{1,97},{2,0},{3,99},{4,2},{5,101},{6,4},{7,103},{8,14},{9,10... | collective-permute-start | bytes 2064392 | tf_op jit(solution)/shard_map/ppermute | solution.py:52
  24.5 16.8 %collective-permute-start.7 = (bf16[128,2688]{1,0:T(8,128)(2,1)S(1)}, bf16[128,2688]{1,0:T(8,128)(2,1)S(1)}, u32[]{:S(2)}, u32[]{:S(2)}) collective-permute-start(bf16[128,2688]{1,0:T(8,128)(2,1)S(1)} %pad_maximum_fusion.refs_0_.refs_8_), channel_id=1, source_target_pairs={{0,2},{1,65},{2,4},{3,67},{4,6},{5,69},{6,0},{7,71},{8,10},{9,73},... | collective-permute-start | bytes 2064392 | tf_op jit(solution)/shard_map/ppermute | solution.py:52
  25.1 8.0 %collective-permute-start.12 = (bf16[128,1152]{1,0:T(8,128)(2,1)S(1)}, bf16[128,1152]{1,0:T(8,128)(2,1)S(1)}, u32[]{:S(2)}, u32[]{:S(2)}) collective-permute-start(bf16[128,1152]{1,0:T(8,128)(2,1)S(1)} %pad_maximum_fusion.1.refs_0_.refs_4_), channel_id=1, source_target_pairs={{0,16},{1,17},{2,18},{3,19},{4,20},{5,21},{6,22},{7,23},{8,24},{9,... | collective-permute-start | bytes 884744 | tf_op jit(solution)/shard_map/ppermute | solution.py:52
  29.1 11.0 %collective-permute-start.11 = (bf16[128,1152]{1,0:T(8,128)(2,1)S(1)}, bf16[128,1152]{1,0:T(8,128)(2,1)}, u32[]{:S(2)}, u32[]{:S(2)}) collective-permute-start(bf16[128,1152]{1,0:T(8,128)(2,1)S(1)} %pad_maximum_fusion.1.refs_0_.refs_4_), channel_id=1, source_target_pairs={{0,24},{1,25},{2,26},{3,27},{4,28},{5,29},{6,30},{7,31},{8,0},{9,1... | collective-permute-start | bytes 884744 | tf_op jit(solution)/shard_map/ppermute | solution.py:52
  33.2 8.1 %collective-permute-start.10 = (bf16[128,1152]{1,0:T(8,128)(2,1)S(1)}, bf16[128,1152]{1,0:T(8,128)(2,1)}, u32[]{:S(2)}, u32[]{:S(2)}) collective-permute-start(bf16[128,1152]{1,0:T(8,128)(2,1)S(1)} %pad_maximum_fusion.1.refs_0_.refs_4_), channel_id=1, source_target_pairs={{0,8},{1,9},{2,10},{3,11},{4,12},{5,13},{6,14},{7,15},{8,16},{9,17... | collective-permute-start | bytes 884744 | tf_op jit(solution)/shard_map/ppermute | solution.py:52
  41.3 18.5 %collective-permute-start.13 = (bf16[128,1152]{1,0:T(8,128)(2,1)S(1)}, bf16[128,1152]{1,0:T(8,128)(2,1)}, u32[]{:S(2)}, u32[]{:S(2)}) collective-permute-start(bf16[128,1152]{1,0:T(8,128)(2,1)S(1)} %pad_maximum_fusion.1.refs_0_.refs_4_), channel_id=1, source_target_pairs={{0,1},{1,0},{2,3},{3,2},{4,5},{5,4},{6,7},{7,6},{8,9},{9,8},{10,11... | collective-permute-start | bytes 884744 | tf_op jit(solution)/shard_map/ppermute | solution.py:60
  55.2 4.6 %collective-permute-start.14 = (bf16[128,1152]{1,0:T(8,128)(2,1)}, bf16[128,1152]{1,0:T(8,128)(2,1)}, u32[]{:S(2)}, u32[]{:S(2)}) collective-permute-start(bf16[128,1152]{1,0:T(8,128)(2,1)} %collective-permute-done.10.refs_1_.refs_5_), channel_id=1, source_target_pairs={{0,1},{1,0},{2,3},{3,2},{4,5},{5,4},{6,7},{7,6},{8,9},{9,8},{10,11... | collective-permute-start | bytes 884744 | tf_op jit(solution)/shard_map/ppermute | solution.py:60
  55.3 4.5 %collective-permute-start.15 = (bf16[128,1152]{1,0:T(8,128)(2,1)}, bf16[128,1152]{1,0:T(8,128)(2,1)}, u32[]{:S(2)}, u32[]{:S(2)}) collective-permute-start(bf16[128,1152]{1,0:T(8,128)(2,1)} %collective-permute-done.11.refs_2_.refs_6_), channel_id=1, source_target_pairs={{0,1},{1,0},{2,3},{3,2},{4,5},{5,4},{6,7},{7,6},{8,9},{9,8},{10,11... | collective-permute-start | bytes 884744 | tf_op jit(solution)/shard_map/ppermute | solution.py:60
  55.7 4.1 %collective-permute-start.16 = (bf16[128,1152]{1,0:T(8,128)(2,1)S(1)}, bf16[128,1152]{1,0:T(8,128)(2,1)}, u32[]{:S(2)}, u32[]{:S(2)}) collective-permute-start(bf16[128,1152]{1,0:T(8,128)(2,1)S(1)} %collective-permute-done.12.refs_3_.refs_7_), channel_id=1, source_target_pairs={{0,1},{1,0},{2,3},{3,2},{4,5},{5,4},{6,7},{7,6},{8,9},{9,8},{10,11... | collective-permute-start | bytes 884744 | tf_op jit(solution)/shard_map/ppermute | solution.py:60
  59.4 8.7 %collective-permute-start.20 = (bf16[128,2560]{1,0:T(8,128)(2,1)S(1)}, bf16[128,2560]{1,0:T(8,128)(2,1)S(1)}, u32[]{:S(2)}, u32[]{:S(2)}) collective-permute-start(bf16[128,2560]{1,0:T(8,128)(2,1)S(1)} %get-tuple-element.143), channel_id=1, source_target_pairs={{0,1},{1,0},{2,3},{3,2},{4,5},{5,4},{6,7},{7,6},{8,9},{9,8},{10,11... | collective-permute-start | bytes 1966088 | tf_op jit(solution)/shard_map/ppermute | solution.py:60
  59.9 18.0 %collective-permute-start.17 = (bf16[128,2560]{1,0:T(8,128)(2,1)S(1)}, bf16[128,2560]{1,0:T(8,128)(2,1)S(1)}, u32[]{:S(2)}, u32[]{:S(2)}) collective-permute-start(bf16[128,2560]{1,0:T(8,128)(2,1)S(1)} %get-tuple-element.155), channel_id=1, source_target_pairs={{0,64},{1,9},{2,66},{3,11},{4,68},{5,13},{6,70},{7,15},{8,72},{9,1... | collective-permute-start | bytes 1966088 | tf_op jit(solution)/shard_map/ppermute | solution.py:64
  59.9 18.0 %collective-permute-start.18 = (bf16[128,2560]{1,0:T(8,128)(2,1)S(1)}, bf16[128,2560]{1,0:T(8,128)(2,1)S(1)}, u32[]{:S(2)}, u32[]{:S(2)}) collective-permute-start(bf16[128,2560]{1,0:T(8,128)(2,1)S(1)} %get-tuple-element.156), channel_id=1, source_target_pairs={{0,96},{1,25},{2,98},{3,27},{4,100},{5,29},{6,102},{7,31},{8,104},... | collective-permute-start | bytes 1966088 | tf_op jit(solution)/shard_map/ppermute | solution.py:64
  62.6 15.3 %collective-permute-start.19 = (bf16[128,2560]{1,0:T(8,128)(2,1)S(1)}, bf16[128,2560]{1,0:T(8,128)(2,1)S(1)}, u32[]{:S(2)}, u32[]{:S(2)}) collective-permute-start(bf16[128,2560]{1,0:T(8,128)(2,1)S(1)} %get-tuple-element.157), channel_id=1, source_target_pairs={{0,32},{1,17},{2,34},{3,19},{4,36},{5,21},{6,38},{7,23},{8,40},{9,... | collective-permute-start | bytes 1966088 | tf_op jit(solution)/shard_map/ppermute | solution.py:64
  66.9 15.4 %collective-permute-start.26 = (bf16[128,2048]{1,0:T(8,128)(2,1)S(1)}, bf16[128,2048]{1,0:T(8,128)(2,1)S(1)}, u32[]{:S(2)}, u32[]{:S(2)}) collective-permute-start(bf16[128,2048]{1,0:T(8,128)(2,1)S(1)} %get-tuple-element.154), channel_id=1, source_target_pairs={{0,4},{1,5},{2,6},{3,7},{4,0},{5,1},{6,2},{7,3},{8,12},{9,13},{10,... | collective-permute-start | bytes 1572872 | tf_op jit(solution)/shard_map/ppermute | solution.py:64
  77.9 19.1 %collective-permute-start.21 = (bf16[128,2560]{1,0:T(8,128)(2,1)S(1)}, bf16[128,2560]{1,0:T(8,128)(2,1)S(1)}, u32[]{:S(2)}, u32[]{:S(2)}) collective-permute-start(bf16[128,2560]{1,0:T(8,128)(2,1)S(1)} %get-tuple-element.165), channel_id=1, source_target_pairs={{0,65},{1,8},{2,67},{3,10},{4,69},{5,12},{6,71},{7,14},{8,73},{9,1... | collective-permute-start | bytes 1966088 | tf_op jit(solution)/shard_map/ppermute | solution.py:64
  78.0 19.1 %collective-permute-start.22 = (bf16[128,2560]{1,0:T(8,128)(2,1)S(1)}, bf16[128,2560]{1,0:T(8,128)(2,1)S(1)}, u32[]{:S(2)}, u32[]{:S(2)}) collective-permute-start(bf16[128,2560]{1,0:T(8,128)(2,1)S(1)} %get-tuple-element.166), channel_id=1, source_target_pairs={{0,97},{1,24},{2,99},{3,26},{4,101},{5,28},{6,103},{7,30},{8,105},... | collective-permute-start | bytes 1966088 | tf_op jit(solution)/shard_map/ppermute | solution.py:64
  80.2 16.9 %collective-permute-start.23 = (bf16[128,2560]{1,0:T(8,128)(2,1)S(1)}, bf16[128,2560]{1,0:T(8,128)(2,1)S(1)}, u32[]{:S(2)}, u32[]{:S(2)}) collective-permute-start(bf16[128,2560]{1,0:T(8,128)(2,1)S(1)} %get-tuple-element.167), channel_id=1, source_target_pairs={{0,33},{1,16},{2,35},{3,18},{4,37},{5,20},{6,39},{7,22},{8,41},{9,... | collective-permute-start | bytes 1966088 | tf_op jit(solution)/shard_map/ppermute | solution.py:64
  82.4 14.1 %collective-permute-start.24 = (bf16[128,2048]{1,0:T(8,128)(2,1)}, bf16[128,2048]{1,0:T(8,128)(2,1)}, u32[]{:S(2)}, u32[]{:S(2)}) collective-permute-start(bf16[128,2048]{1,0:T(8,128)(2,1)} %get-tuple-element.168), channel_id=1, source_target_pairs={{0,2},{1,3},{2,4},{3,5},{4,6},{5,7},{6,0},{7,1},{8,10},{9,11},{10,... | collective-permute-start | bytes 1572872 | tf_op jit(solution)/shard_map/ppermute | solution.py:64
  82.4 14.1 %collective-permute-start.25 = (bf16[128,2048]{1,0:T(8,128)(2,1)S(1)}, bf16[128,2048]{1,0:T(8,128)(2,1)}, u32[]{:S(2)}, u32[]{:S(2)}) collective-permute-start(bf16[128,2048]{1,0:T(8,128)(2,1)S(1)} %get-tuple-element.169), channel_id=1, source_target_pairs={{0,6},{1,7},{2,0},{3,1},{4,2},{5,3},{6,4},{7,5},{8,14},{9,15},{10,... | collective-permute-start | bytes 1572872 | tf_op jit(solution)/shard_map/ppermute | solution.py:64
  114.5 18.6 %collective-permute-start.27 = (bf16[128,2560]{1,0:T(8,128)(2,1)}, bf16[128,2560]{1,0:T(8,128)(2,1)S(1)}, u32[]{:S(2)}, u32[]{:S(2)}) collective-permute-start(bf16[128,2560]{1,0:T(8,128)(2,1)} %get-tuple-element.187), channel_id=1, source_target_pairs={{64,0},{9,1},{66,2},{11,3},{68,4},{13,5},{70,6},{15,7},{72,8},{17,... | collective-permute-start | bytes 1966088 | tf_op jit(solution)/shard_map/ppermute | solution.py:64
  116.4 18.2 %collective-permute-start.28 = (bf16[128,2560]{1,0:T(8,128)(2,1)}, bf16[128,2560]{1,0:T(8,128)(2,1)S(1)}, u32[]{:S(2)}, u32[]{:S(2)}) collective-permute-start(bf16[128,2560]{1,0:T(8,128)(2,1)} %get-tuple-element.188), channel_id=1, source_target_pairs={{96,0},{25,1},{98,2},{27,3},{100,4},{29,5},{102,6},{31,7},{104,8},... | collective-permute-start | bytes 1966088 | tf_op jit(solution)/shard_map/ppermute | solution.py:64
  116.4 18.2 %collective-permute-start.29 = (bf16[128,2560]{1,0:T(8,128)(2,1)}, bf16[128,2560]{1,0:T(8,128)(2,1)S(1)}, u32[]{:S(2)}, u32[]{:S(2)}) collective-permute-start(bf16[128,2560]{1,0:T(8,128)(2,1)} %get-tuple-element.189), channel_id=1, source_target_pairs={{32,0},{17,1},{34,2},{19,3},{36,4},{21,5},{38,6},{23,7},{40,8},{25... | collective-permute-start | bytes 1966088 | tf_op jit(solution)/shard_map/ppermute | solution.py:64
  117.7 12.4 %collective-permute-start.30 = (bf16[128,2048]{1,0:T(8,128)(2,1)}, bf16[128,2048]{1,0:T(8,128)(2,1)S(1)}, u32[]{:S(2)}, u32[]{:S(2)}) collective-permute-start(bf16[128,2048]{1,0:T(8,128)(2,1)} %get-tuple-element.184), channel_id=1, source_target_pairs={{2,0},{3,1},{4,2},{5,3},{6,4},{7,5},{0,6},{1,7},{10,8},{11,9},{12,... | collective-permute-start | bytes 1572872 | tf_op jit(solution)/shard_map/ppermute | solution.py:64
  119.9 13.2 %collective-permute-start.31 = (bf16[128,2048]{1,0:T(8,128)(2,1)}, bf16[128,2048]{1,0:T(8,128)(2,1)S(1)}, u32[]{:S(2)}, u32[]{:S(2)}) collective-permute-start(bf16[128,2048]{1,0:T(8,128)(2,1)} %get-tuple-element.185), channel_id=1, source_target_pairs={{6,0},{7,1},{0,2},{1,3},{2,4},{3,5},{4,6},{5,7},{14,8},{15,9},{8,1... | collective-permute-start | bytes 1572872 | tf_op jit(solution)/shard_map/ppermute | solution.py:64
  134.6 20.5 %collective-permute-start.32 = (bf16[128,2560]{1,0:T(8,128)(2,1)}, bf16[128,2560]{1,0:T(8,128)(2,1)S(1)}, u32[]{:S(2)}, u32[]{:S(2)}) collective-permute-start(bf16[128,2560]{1,0:T(8,128)(2,1)} %get-tuple-element.196), channel_id=1, source_target_pairs={{65,0},{8,1},{67,2},{10,3},{69,4},{12,5},{71,6},{14,7},{73,8},{16,... | collective-permute-start | bytes 1966088 | tf_op jit(solution)/shard_map/ppermute | solution.py:64
  137.9 17.1 %collective-permute-start.33 = (bf16[128,2560]{1,0:T(8,128)(2,1)}, bf16[128,2560]{1,0:T(8,128)(2,1)S(1)}, u32[]{:S(2)}, u32[]{:S(2)}) collective-permute-start(bf16[128,2560]{1,0:T(8,128)(2,1)} %get-tuple-element.197), channel_id=1, source_target_pairs={{97,0},{24,1},{99,2},{26,3},{101,4},{28,5},{103,6},{30,7},{105,8},... | collective-permute-start | bytes 1966088 | tf_op jit(solution)/shard_map/ppermute | solution.py:64
  137.9 18.5 %collective-permute-start.34 = (bf16[128,2560]{1,0:T(8,128)(2,1)}, bf16[128,2560]{1,0:T(8,128)(2,1)S(1)}, u32[]{:S(2)}, u32[]{:S(2)}) collective-permute-start(bf16[128,2560]{1,0:T(8,128)(2,1)} %get-tuple-element.198), channel_id=1, source_target_pairs={{33,0},{16,1},{35,2},{18,3},{37,4},{20,5},{39,6},{22,7},{41,8},{24... | collective-permute-start | bytes 1966088 | tf_op jit(solution)/shard_map/ppermute | solution.py:64
  138.8 17.5 %collective-permute-start.35 = (bf16[128,2560]{1,0:T(8,128)(2,1)}, bf16[128,2560]{1,0:T(8,128)(2,1)S(1)}, u32[]{:S(2)}, u32[]{:S(2)}) collective-permute-start(bf16[128,2560]{1,0:T(8,128)(2,1)} %get-tuple-element.199), channel_id=1, source_target_pairs={{0,1},{1,0},{2,3},{3,2},{4,5},{5,4},{6,7},{7,6},{8,9},{9,8},{10,11... | collective-permute-start | bytes 1966088 | tf_op jit(solution)/shard_map/ppermute | solution.py:60
  140.3 14.7 %collective-permute-start.36 = (bf16[128,2048]{1,0:T(8,128)(2,1)S(1)}, bf16[128,2048]{1,0:T(8,128)(2,1)S(1)}, u32[]{:S(2)}, u32[]{:S(2)}) collective-permute-start(bf16[128,2048]{1,0:T(8,128)(2,1)S(1)} %copy-done.15), channel_id=1, source_target_pairs={{4,0},{5,1},{6,2},{7,3},{0,4},{1,5},{2,6},{3,7},{12,8},{13,9},{14,... | collective-permute-start | bytes 1572872 | tf_op jit(solution)/shard_map/ppermute | solution.py:64
  158.8 7.3 %collective-permute-start.40 = (bf16[512,1024]{1,0:T(8,128)(2,1)S(1)}, bf16[512,1024]{1,0:T(8,128)(2,1)S(1)}, u32[]{:S(2)}, u32[]{:S(2)}) collective-permute-start(bf16[512,1024]{1,0:T(8,128)(2,1)S(1)} %shard_map.88), channel_id=1, source_target_pairs={{0,1},{1,0},{2,3},{3,2},{4,5},{5,4},{6,7},{7,6},{8,9},{9,8},{10,11... | collective-permute-start | bytes 3145736 | tf_op jit(solution)/shard_map/ppermute | solution.py:60
  161.9 9.8 %collective-permute-start.37 = (bf16[128,2560]{1,0:T(8,128)(2,1)S(1)}, bf16[128,2560]{1,0:T(8,128)(2,1)S(1)}, u32[]{:S(2)}, u32[]{:S(2)}) collective-permute-start(bf16[128,2560]{1,0:T(8,128)(2,1)S(1)} %get-tuple-element.206), channel_id=1, source_target_pairs={{2,0},{65,1},{4,2},{67,3},{6,4},{69,5},{0,6},{71,7},{10,8},{73,9},... | collective-permute-start | bytes 1966088 | tf_op jit(solution)/shard_map/ppermute | solution.py:56
  162.5 11.5 %collective-permute-start.38 = (bf16[128,2560]{1,0:T(8,128)(2,1)S(1)}, bf16[128,2560]{1,0:T(8,128)(2,1)S(1)}, u32[]{:S(2)}, u32[]{:S(2)}) collective-permute-start(bf16[128,2560]{1,0:T(8,128)(2,1)S(1)} %get-tuple-element.207), channel_id=1, source_target_pairs={{6,0},{97,1},{0,2},{99,3},{2,4},{101,5},{4,6},{103,7},{14,8},{105,... | collective-permute-start | bytes 1966088 | tf_op jit(solution)/shard_map/ppermute | solution.py:56
  163.4 17.9 %collective-permute-start.39 = (bf16[128,2560]{1,0:T(8,128)(2,1)S(1)}, bf16[128,2560]{1,0:T(8,128)(2,1)S(1)}, u32[]{:S(2)}, u32[]{:S(2)}) collective-permute-start(bf16[128,2560]{1,0:T(8,128)(2,1)S(1)} %get-tuple-element.208), channel_id=1, source_target_pairs={{4,0},{33,1},{6,2},{35,3},{0,4},{37,5},{2,6},{39,7},{12,8},{41,9},... | collective-permute-start | bytes 1966088 | tf_op jit(solution)/shard_map/ppermute | solution.py:56
  168.5 12.9 %collective-permute-start.41 = (bf16[128,1024]{1,0:T(8,128)(2,1)S(1)}, bf16[128,1024]{1,0:T(8,128)(2,1)S(1)}, u32[]{:S(2)}, u32[]{:S(2)}) collective-permute-start(bf16[128,1024]{1,0:T(8,128)(2,1)S(1)} %get-tuple-element.214), channel_id=1, source_target_pairs={{8,0},{9,1},{10,2},{11,3},{12,4},{13,5},{14,6},{15,7},{16,8},{17,9... | collective-permute-start | bytes 786440 | tf_op jit(solution)/shard_map/ppermute | solution.py:56
  169.4 14.9 %collective-permute-start.42 = (bf16[128,1024]{1,0:T(8,128)(2,1)S(1)}, bf16[128,1024]{1,0:T(8,128)(2,1)S(1)}, u32[]{:S(2)}, u32[]{:S(2)}) collective-permute-start(bf16[128,1024]{1,0:T(8,128)(2,1)S(1)} %get-tuple-element.215), channel_id=1, source_target_pairs={{24,0},{25,1},{26,2},{27,3},{28,4},{29,5},{30,6},{31,7},{0,8},{1,9... | collective-permute-start | bytes 786440 | tf_op jit(solution)/shard_map/ppermute | solution.py:56
  171.7 12.6 %collective-permute-start.43 = (bf16[128,1024]{1,0:T(8,128)(2,1)S(1)}, bf16[128,1024]{1,0:T(8,128)(2,1)S(1)}, u32[]{:S(2)}, u32[]{:S(2)}) collective-permute-start(bf16[128,1024]{1,0:T(8,128)(2,1)S(1)} %get-tuple-element.216), channel_id=1, source_target_pairs={{16,0},{17,1},{18,2},{19,3},{20,4},{21,5},{22,6},{23,7},{24,8},{25... | collective-permute-start | bytes 786440 | tf_op jit(solution)/shard_map/ppermute | solution.py:56
  184.8 14.1 %collective-permute-start.46 = (bf16[32,2560]{1,0:T(8,128)(2,1)S(1)}, bf16[32,2560]{1,0:T(8,128)(2,1)S(1)}, u32[]{:S(2)}, u32[]{:S(2)}) collective-permute-start(bf16[32,2560]{1,0:T(8,128)(2,1)S(1)} %get-tuple-element.235), channel_id=1, source_target_pairs={{16,0},{5,1},{18,2},{7,3},{20,4},{1,5},{22,6},{3,7},{24,8},{13,9},... | collective-permute-start | bytes 491528 | tf_op jit(solution)/shard_map/ppermute | solution.py:56
  188.3 10.6 %collective-permute-start.45 = (bf16[32,2560]{1,0:T(8,128)(2,1)S(1)}, bf16[32,2560]{1,0:T(8,128)(2,1)S(1)}, u32[]{:S(2)}, u32[]{:S(2)}) collective-permute-start(bf16[32,2560]{1,0:T(8,128)(2,1)S(1)} %get-tuple-element.236), channel_id=1, source_target_pairs={{24,0},{7,1},{26,2},{1,3},{28,4},{3,5},{30,6},{5,7},{0,8},{15,9},{... | collective-permute-start | bytes 491528 | tf_op jit(solution)/shard_map/ppermute | solution.py:56
  188.3 10.6 %collective-permute-start.44 = (bf16[32,2560]{1,0:T(8,128)(2,1)S(1)}, bf16[32,2560]{1,0:T(8,128)(2,1)S(1)}, u32[]{:S(2)}, u32[]{:S(2)}) collective-permute-start(bf16[32,2560]{1,0:T(8,128)(2,1)S(1)} %get-tuple-element.237), channel_id=1, source_target_pairs={{8,0},{3,1},{10,2},{5,3},{12,4},{7,5},{14,6},{1,7},{16,8},{11,9},{... | collective-permute-start | bytes 491528 | tf_op jit(solution)/shard_map/ppermute | solution.py:56
  191.0 4.8 %collective-permute-start.49 = (bf16[32,1024]{1,0:T(8,128)(2,1)S(1)}, bf16[32,1024]{1,0:T(8,128)(2,1)S(1)}, u32[]{:S(2)}, u32[]{:S(2)}) collective-permute-start(bf16[32,1024]{1,0:T(8,128)(2,1)S(1)} %get-tuple-element.241), channel_id=1, source_target_pairs={{32,0},{33,1},{34,2},{35,3},{36,4},{37,5},{38,6},{39,7},{40,8},{41... | collective-permute-start | bytes 196616 | tf_op jit(solution)/shard_map/ppermute | solution.py:56
  191.1 6.0 %collective-permute-start.48 = (bf16[32,1024]{1,0:T(8,128)(2,1)S(1)}, bf16[32,1024]{1,0:T(8,128)(2,1)S(1)}, u32[]{:S(2)}, u32[]{:S(2)}) collective-permute-start(bf16[32,1024]{1,0:T(8,128)(2,1)S(1)} %get-tuple-element.242), channel_id=1, source_target_pairs={{96,0},{97,1},{98,2},{99,3},{100,4},{101,5},{102,6},{103,7},{104,8... | collective-permute-start | bytes 196616 | tf_op jit(solution)/shard_map/ppermute | solution.py:56
  199.1 3.6 %collective-permute-start.50 = (bf16[16,3584]{1,0:T(8,128)(2,1)S(1)}, bf16[16,3584]{1,0:T(8,128)(2,1)S(1)}, u32[]{:S(2)}, u32[]{:S(2)}) collective-permute-start(bf16[16,3584]{1,0:T(8,128)(2,1)S(1)} %broadcast_select_fusion.4), channel_id=1, source_target_pairs={{0,1},{1,0},{2,3},{3,2},{4,5},{5,4},{6,7},{7,6},{8,9},{9,8},{10,11... | collective-permute-start | bytes 344072 | tf_op jit(solution)/shard_map/ppermute | solution.py:60
  (19 other events, 227.5 us)
where the time goes:
time: 206 us; the launch traced here: 204 us
  starting transfers between devices  77.5 us (38%)
  waiting for transfers between devices  71.9 us (35%)
  Pallas kernels  43.7 us (21%)
  local copies, waits for them, and re-layouts  7.31 us (4%)
  other arithmetic  2.81 us (1%)
    ppermute x18, waiting for transfers between devices, hop(): lax.ppermute(blocks[r], ALL_AXES, perm(axes, SHIFTS[r], cross))  38.8 us
    ppermute x18, starting transfers between devices, hop(): lax.ppermute(blocks[r], ALL_AXES, perm(axes, SHIFTS[r], cross))  20.7 us
    ppermute x9, starting transfers between devices, other_core(): return lax.ppermute(value, 'c', [(0, 1), (1, 0)])  20.7 us
    ppermute x12, starting transfers between devices, gathered(): lax.ppermute(value, ALL_AXES, ring_perm(axes, s))  18.6 us
    ppermute x12, starting transfers between devices, scattered(): lax.ppermute(b, ALL_AXES, back_perm(axes, s))  17.5 us
    ppermute x12, waiting for transfers between devices, scattered(): lax.ppermute(b, ALL_AXES, back_perm(axes, s))  16.5 us
    pallas_call x1, Pallas kernels, expert(): pl.pallas_call(expert_kernel, out_shape=[block(MAIN)] * RING + [block(2 *...  16.1 us
    ppermute x12, waiting for transfers between devices, gathered(): lax.ppermute(value, ALL_AXES, ring_perm(axes, s))  14.5 us
  transfers between devices with their start and end apart: 51, of which 20 were waited for; matrix products, arithmetic and copies ran while one was open for 0% of the time, Pallas kernels for 12%

commit v1 on v0

v1 whole, which is shorter than its diff:
```python
import functools
import itertools

import jax
import jax.numpy as jnp
from jax import lax
from jax.experimental import pallas as pl
from jax.experimental.pallas import tpu as pltpu
from jax.sharding import Mesh, PartitionSpec as P

ALL_AXES = ("dp", "xh", "z", "y", "c")
RING = 4
CORES = 2
CAP = 4
TOP = 8
GROUP = 16
META = 128
HALF = 3584
BLOCK = 128
SHIFTS = (0, 1, 3, 2)
ROUTE = (("z", "y"), ("y", "x"), ("x", "z"))
SMALL_VMEM = 24 << 20
LARGE_VMEM = 56 << 20


def flat_index(x, z, y, c):
    return ((((x % 2) * 2 + x // 2) * RING + z) * RING + y) * CORES + c


def ring_perm(axes, shift, cross=False):
    pairs = []
    for x, z, y, c in itertools.product(range(RING), range(RING), range(RING), range(CORES)):
        there = {"x": x, "z": z, "y": y}
        there[axes[c]] = (there[axes[c]] + shift) % RING
        target = flat_index(there["x"], there["z"], there["y"], 1 - c if cross else c)
        pairs.append((flat_index(x, z, y, c), target))
    return pairs


def together(*values):
    return lax.optimization_barrier(values)


def back_perm(axes, shift, cross=False):
    return [(target, source) for source, target in ring_perm(axes, shift, cross)]


def gathered(value, axes):
    return [value] + [lax.ppermute(value, ALL_AXES, ring_perm(axes, s)) for s in SHIFTS[1:]]


def scattered(blocks, axes):
    return [blocks[0]] + [lax.ppermute(b, ALL_AXES, back_perm(axes, s)) for b, s in zip(blocks[1:], SHIFTS[1:])]


def other_core(value):
    return lax.ppermute(value, "c", [(0, 1), (1, 0)])


def hop(blocks, axes, perm, numbers, cross=False):
    return [other_core(blocks[r]) if r == 0 else lax.ppermute(blocks[r], ALL_AXES, perm(axes, SHIFTS[r], cross))
            for r in numbers]


def column_chunks(width):
    steps, start = [], 0
    while start < width:
        size = min(1792, width - start)
        steps.append((start, size))
        start += size
    return steps


def iota(shape, dim):
    return lax.broadcasted_iota(jnp.int32, shape, dim)


def slots_of(meta, experts):
    turned = jnp.transpose(meta.astype(jnp.float32))
    owner = turned[:TOP]
    match = [owner == e.astype(jnp.float32) for e in experts]
    hits = [jnp.max(jnp.where(m, 1.0, 0.0), axis=0, keepdims=True) for m in match]
    stacked = jnp.concatenate(hits * (8 // len(hits)), axis=0)
    row, col = iota((BLOCK, BLOCK), 0), iota((BLOCK, BLOCK), 1)
    before = jnp.where((row // GROUP == col // GROUP) & (row < col), 1.0, 0.0)
    rank = jnp.dot(stacked.astype(jnp.bfloat16), before.astype(jnp.bfloat16),
                   preferred_element_type=jnp.float32)
    base = (iota((1, BLOCK), 1) // GROUP * CAP).astype(jnp.float32)
    slot = iota((BLOCK // RING, BLOCK), 0).astype(jnp.float32)
    place = [slot == jnp.where(h > 0.5, base + rank[e:e + 1], -1.0) for e, h in enumerate(hits)]
    return place, match, turned


def experts_at(info):
    own = [info[4 + r] for r in range(RING)]
    return own + [e ^ 1 for e in own]


def pack_kernel(cross, info, *refs):
    blocks, outs = refs[:RING], refs[RING:]
    experts = experts_at(info)[RING * cross:RING * cross + RING]
    rows = BLOCK // RING
    for b in range(RING):
        place, _, _ = slots_of(blocks[b][:, HALF:HALF + META], experts)
        spread = jnp.concatenate([jnp.where(p, 1.0, 0.0) for p in place], axis=0).astype(jnp.bfloat16)
        for start, size in column_chunks(HALF):
            cols = slice(start, start + size)
            got = jnp.dot(spread, blocks[b][:, cols], preferred_element_type=jnp.float32).astype(jnp.bfloat16)
            for e, out in enumerate(outs):
                out[rows * b:rows * (b + 1), cols] = got[rows * e:rows * (e + 1)]


VMEM_SPEC = pl.BlockSpec(memory_space=pltpu.VMEM)
SMEM_SPEC = pl.BlockSpec(memory_space=pltpu.SMEM)
HBM_SPEC = pl.BlockSpec(memory_space=pltpu.HBM)


def pack(info, blocks, cross):
    return list(pl.pallas_call(
        functools.partial(pack_kernel, cross),
        out_shape=[jax.ShapeDtypeStruct((BLOCK, HALF), jnp.bfloat16)] * RING,
        in_specs=[SMEM_SPEC] + [VMEM_SPEC] * RING,
        out_specs=[VMEM_SPEC] * RING,
        compiler_params=pltpu.CompilerParams(vmem_limit_bytes=SMALL_VMEM),
        cost_estimate=pl.CostEstimate(
            flops=2 * RING * BLOCK * BLOCK * HALF, bytes_accessed=16 * BLOCK * HALF, transcendentals=0),
    )(info, *blocks))


def combine_kernel(info, *refs):
    blocks, metas, outs = refs[:2 * RING], refs[2 * RING:3 * RING], refs[3 * RING:]
    experts = experts_at(info)
    rows = BLOCK // RING
    for b in range(RING):
        place, match, turned = slots_of(metas[b][...], experts)
        parts = []
        for offset in (TOP, 2 * TOP):
            mix = turned[offset:offset + TOP]
            picked = [jnp.sum(jnp.where(m, mix, 0.0), axis=0, keepdims=True) for m in match]
            weight = jnp.concatenate([jnp.where(p, w, 0.0) for p, w in zip(place, picked)], axis=0)
            parts.append(jnp.transpose(weight))
        mixer = jnp.concatenate(parts, axis=0).astype(jnp.bfloat16)
        for start, size in column_chunks(HALF):
            cols = slice(start, start + size)
            data = jnp.concatenate([block[rows * b:rows * (b + 1), cols] for block in blocks], axis=0)
            got = jnp.dot(mixer, data, preferred_element_type=jnp.float32)
            outs[b][:, cols] = (got[:BLOCK] + got[BLOCK:]).astype(jnp.bfloat16)


def combine(info, blocks, metas):
    meta_spec = pl.BlockSpec((BLOCK, META), lambda i: (0, HALF // META))
    return list(pl.pallas_call(
        combine_kernel,
        grid=(1,),
        out_shape=[jax.ShapeDtypeStruct((BLOCK, HALF), jnp.bfloat16)] * RING,
        in_specs=[SMEM_SPEC] + [VMEM_SPEC] * (2 * RING) + [meta_spec] * RING,
        out_specs=[VMEM_SPEC] * RING,
        compiler_params=pltpu.CompilerParams(vmem_limit_bytes=SMALL_VMEM),
        cost_estimate=pl.CostEstimate(
            flops=8 * RING * BLOCK * BLOCK * HALF, bytes_accessed=24 * BLOCK * HALF, transcendentals=0),
    )(info, *blocks, *metas))


def weight_copies(chunks, gate_hbm, up_hbm, w_in, in_sem):
    half = w_in.shape[1] // 2
    copies, at = [], 0
    for i, (col, size) in enumerate(chunks):
        col = pl.multiple_of(col, BLOCK)
        copies.append((
            pltpu.make_async_copy(gate_hbm.at[pl.ds(col, size)], w_in.at[pl.ds(at, size), pl.ds(0, half)],
                                  in_sem.at[2 * i]),
            pltpu.make_async_copy(up_hbm.at[pl.ds(col, size)], w_in.at[pl.ds(at, size), pl.ds(half, half)],
                                  in_sem.at[2 * i + 1])))
        at += size
    return copies


def block_copies(blocks, target, sems, first):
    return [pltpu.make_async_copy(blocks[r], target.at[pl.ds(r * BLOCK, BLOCK)], sems.at[first + r])
            for r in range(RING)]


def start_all(copies):
    for copy in copies:
        copy.start()


def wait_all(copies):
    for copy in copies:
        copy.wait()


def begin_kernel(info, pairs, tokens, picks, mix, mine, theirs):
    slot = picks[...]
    moved = slot < 0
    for i in range(pairs.shape[0]):
        for j in range(pairs.shape[1]):
            moved = moved | (slot == pairs[i, j])
    owner = jnp.where(moved, slot ^ 32, slot).astype(jnp.bfloat16)
    high = mix[...].astype(jnp.bfloat16)
    low = (mix[...] - high.astype(jnp.float32)).astype(jnp.bfloat16)
    meta = jnp.zeros((GROUP, META), jnp.float32)
    for i, part in enumerate((owner, high, low)):
        lane = iota((TOP, META), 1) == iota((TOP, META), 0) + i * TOP
        lane = jnp.where(lane, 1.0, 0.0).astype(jnp.bfloat16)
        meta += lax.dot_general(part, lane, (((0,), (0,)), ((), ())), preferred_element_type=jnp.float32)
    meta = meta.astype(jnp.bfloat16)
    mine[:, HALF:] = meta
    theirs[:, HALF:] = meta
    for core in range(CORES):
        @pl.when(info[0] == core)
        def _():
            mine[:, :HALF] = tokens[:, HALF * core:HALF * (core + 1)]
            theirs[:, :HALF] = tokens[:, HALF * (1 - core):HALF * (2 - core)]


def begin(info, pairs, tokens, picks, mix):
    out = jax.ShapeDtypeStruct((GROUP, HALF + META), jnp.bfloat16)
    return pl.pallas_call(
        begin_kernel,
        out_shape=[out, out],
        in_specs=[SMEM_SPEC, SMEM_SPEC] + [VMEM_SPEC] * 3,
        out_specs=[VMEM_SPEC, VMEM_SPEC],
        compiler_params=pltpu.CompilerParams(vmem_limit_bytes=SMALL_VMEM),
    )(info, pairs.T, tokens, picks.T, mix.T)


def project_kernel(info, *refs):
    blocks, (gate_hbm, up_hbm, total, x, w_in, x_sem, in_sem) = refs[:RING], refs[RING:]
    base = info[0] * HALF
    steps = column_chunks(HALF)
    x_copies = block_copies(blocks, x, x_sem, 0)
    in_copies = weight_copies([(base + start, size) for start, size in steps], gate_hbm, up_hbm, w_in, in_sem)
    start_all(x_copies)
    for pair in in_copies:
        start_all(pair)
    wait_all(x_copies)
    for (start, size), pair in zip(steps, in_copies):
        wait_all(pair)
        cols = slice(start, start + size)
        got = jnp.dot(x[:, cols], w_in[cols, :], preferred_element_type=jnp.float32)
        if start == 0:
            total[...] = got
        else:
            total[...] += got


def project(info, blocks, gate_w, up_w):
    rows, hid = RING * BLOCK, gate_w.shape[1]
    return pl.pallas_call(
        project_kernel,
        out_shape=jax.ShapeDtypeStruct((rows, 2 * hid), jnp.float32),
        in_specs=[SMEM_SPEC] + [HBM_SPEC] * 6,
        out_specs=VMEM_SPEC,
        scratch_shapes=[
            pltpu.VMEM((rows, HALF), jnp.bfloat16), pltpu.VMEM((HALF, 2 * hid), jnp.bfloat16),
            pltpu.SemaphoreType.DMA((RING,)), pltpu.SemaphoreType.DMA((2 * len(column_chunks(HALF)),)),
        ],
        compiler_params=pltpu.CompilerParams(vmem_limit_bytes=LARGE_VMEM),
        cost_estimate=pl.CostEstimate(
            flops=4 * rows * HALF * hid, bytes_accessed=2 * (2 * HALF * hid + rows * HALF), transcendentals=0),
    )(info, *blocks, gate_w, up_w)


def expert_kernel(info, *refs):
    near, far = refs[0], refs[1:1 + RING]
    gate_hbm, up_hbm, down_hbm = refs[5:8]
    main_outs, hidden_far = refs[8:12], refs[12]
    x, w_in, w_out, a1, a2, h1, h2, o, x_sem, in_sem, down_sem, out_sem = refs[13:]
    core = info[0]
    first = core == 0
    half = w_in.shape[1] // 2
    at_near, at_far = core * HALF, (1 - core) * HALF
    steps = column_chunks(HALF)
    far_copies = block_copies(far, x, x_sem, 0)
    near_copy = pltpu.make_async_copy(near, a1, x_sem.at[RING])
    in_copies = weight_copies([(at_far + start, size) for start, size in steps], gate_hbm, up_hbm, w_in, in_sem)
    down_copies = [pltpu.make_async_copy(
        down_hbm.at[:, pl.ds(pl.multiple_of(at_near + start, BLOCK), size)], w_out.at[:, pl.ds(start, size)],
        down_sem.at[i]) for i, (start, size) in enumerate(steps)]
    start_all(far_copies)
    for pair in in_copies:
        start_all(pair)
    near_copy.start()
    start_all(down_copies)

    wait_all(far_copies)
    for (start, size), pair in zip(steps, in_copies):
        wait_all(pair)
        cols = slice(start, start + size)
        got = jnp.dot(x[:, cols], w_in[cols, :], preferred_element_type=jnp.float32)
        if start == 0:
            a2[...] = got
        else:
            a2[...] += got
    near_copy.wait()

    def activate(i, carry):
        x, y, z = i // 16, i // 4 % 4, i % 4
        left, right = i, z * 16 + x * 4 + y
        i1 = pl.multiple_of(jnp.where(first, left, right) * 8, 8)
        i2 = pl.multiple_of(jnp.where(first, right, left) * 8, 8)
        both = a1[pl.ds(i1, 8)] + a2[pl.ds(i2, 8)]
        gate, up = both[:, :half], both[:, half:]
        value = gate / (1.0 + jnp.exp(-gate)) * up
        h1[pl.ds(i1, 8)] = value
        h2[pl.ds(i2, 8)] = value
        return carry

    lax.fori_loop(0, RING ** 3, activate, 0, unroll=4)
    hidden_far[...] = h2[...].astype(jnp.bfloat16)
    hidden = h1[...].astype(jnp.bfloat16)
    out_copies = []
    for i, ((start, size), copy) in enumerate(zip(steps, down_copies)):
        copy.wait()
        got = jnp.dot(hidden, w_out[:, start:start + size], preferred_element_type=jnp.float32)
        o[:, start:start + size] = got.astype(jnp.bfloat16)
        for r in range(RING):
            out_copies.append(pltpu.make_async_copy(
                o.at[pl.ds(r * BLOCK, BLOCK), pl.ds(start, size)],
                main_outs[r].at[:, pl.ds(start, size)], out_sem.at[RING * i + r]))
            out_copies[-1].start()
    wait_all(out_copies)


def expert(info, near, far, gate_w, up_w, down_w):
    rows, (width, hid) = RING * BLOCK, gate_w.shape
    steps = len(column_chunks(HALF))
    bf, f32 = jnp.bfloat16, jnp.float32
    out = pl.pallas_call(
        expert_kernel,
        out_shape=[jax.ShapeDtypeStruct((BLOCK, HALF), bf)] * RING + [jax.ShapeDtypeStruct((rows, hid), bf)],
        in_specs=[SMEM_SPEC] + [HBM_SPEC] * 8,
        out_specs=[HBM_SPEC] * RING + [VMEM_SPEC],
        scratch_shapes=[
            pltpu.VMEM((rows, HALF), bf), pltpu.VMEM((HALF, 2 * hid), bf), pltpu.VMEM((hid, HALF), bf),
            pltpu.VMEM((rows, 2 * hid), f32), pltpu.VMEM((rows, 2 * hid), f32),
            pltpu.VMEM((rows, hid), f32), pltpu.VMEM((rows, hid), f32),
            pltpu.VMEM((rows, HALF), bf),
            pltpu.SemaphoreType.DMA((RING + 1,)), pltpu.SemaphoreType.DMA((2 * steps,)),
            pltpu.SemaphoreType.DMA((steps,)), pltpu.SemaphoreType.DMA((RING * steps,)),
        ],
        compiler_params=pltpu.CompilerParams(vmem_limit_bytes=LARGE_VMEM),
        cost_estimate=pl.CostEstimate(
            flops=6 * rows * HALF * hid, bytes_accessed=2 * (3 * HALF * hid + 2 * rows * HALF),
            transcendentals=rows * hid),
    )(info, near, *far, gate_w, up_w, down_w)
    return list(out[:RING]), out[RING]


def spread_kernel(info, hidden, down_hbm, *refs):
    outs, (w_out, down_sem) = refs[:RING], refs[RING:]
    base = (1 - info[0]) * HALF
    steps = column_chunks(HALF)
    copies = [pltpu.make_async_copy(
        down_hbm.at[:, pl.ds(pl.multiple_of(base + start, BLOCK), size)], w_out.at[:, pl.ds(start, size)],
        down_sem.at[i]) for i, (start, size) in enumerate(steps)]
    start_all(copies)
    for (start, size), copy in zip(steps, copies):
        copy.wait()
        cols = slice(start, start + size)
        got = jnp.dot(hidden[...], w_out[:, cols], preferred_element_type=jnp.float32).astype(jnp.bfloat16)
        for r in range(RING):
            outs[r][:, cols] = got[BLOCK * r:BLOCK * (r + 1)]


def spread(info, hidden, down_w):
    rows, hid = hidden.shape
    out = pl.pallas_call(
        spread_kernel,
        out_shape=[jax.ShapeDtypeStruct((BLOCK, HALF), jnp.bfloat16)] * RING,
        in_specs=[SMEM_SPEC, VMEM_SPEC, HBM_SPEC],
        out_specs=[VMEM_SPEC] * RING,
        scratch_shapes=[
            pltpu.VMEM((hid, HALF), jnp.bfloat16), pltpu.SemaphoreType.DMA((len(column_chunks(HALF)),))],
        compiler_params=pltpu.CompilerParams(vmem_limit_bytes=LARGE_VMEM),
        cost_estimate=pl.CostEstimate(
            flops=2 * rows * HALF * hid, bytes_accessed=2 * HALF * (hid + rows), transcendentals=0),
    )(info, hidden, down_w)
    return list(out)


def summed(blocks):
    return sum(b.astype(jnp.float32) for b in blocks).astype(jnp.bfloat16)


def split_rows(value):
    return list(value.reshape(RING, -1, value.shape[-1]))


def per_device(tokens, picks, mix_weights, pairs, gate_weight, up_weight, down_weight):
    tok_rows, width = tokens.shape
    c = lax.axis_index("c")
    x = lax.axis_index("xh") * 2 + lax.axis_index("dp")
    z = lax.axis_index("z")
    y = lax.axis_index("y")
    first = c == 0

    shifts = jnp.array(SHIFTS, jnp.int32)
    place = lambda x, z, y: ((x // 2 * RING + z) * RING + y) * CORES + c + 0 * shifts
    along_x = place((x + shifts) % RING, z, y)
    along_z = place(x, (z + shifts) % RING, y)
    info = jnp.concatenate([jnp.stack([c, c, c, c]), jnp.where(first, along_x, along_z)]).astype(jnp.int32)

    mine, theirs = begin(info, pairs, tokens, picks, mix_weights)
    theirs = other_core(theirs)
    pool = jnp.where(first, jnp.concatenate([mine, theirs]), jnp.concatenate([theirs, mine]))
    pool = jnp.concatenate(gathered(pool, ROUTE[0]), axis=0)
    pool = gathered(pool, ROUTE[1])

    own, far = pack(info, pool, 0), pack(info, pool, 1)
    own = own[:1] + hop(own, ROUTE[2], ring_perm, (1, 2, 3))
    far = hop(far, ROUTE[2], ring_perm, (0, 1, 2, 3), cross=True)
    gate_w, up_w, down_w = gate_weight[0], up_weight[0], down_weight[0]
    near = project(info, own, gate_w, up_w)
    own, hidden = expert(info, near, far, gate_w, up_w, down_w)
    far = spread(info, hidden, down_w)
    own = own[:1] + hop(own, ROUTE[2], back_perm, (1, 2, 3))
    far = hop(far, ROUTE[2], back_perm, (0, 1, 2, 3), cross=True)
    sums = combine(info, own + far, pool)
    sums = summed(scattered(sums, ROUTE[1]))
    done = summed(scattered(split_rows(sums), ROUTE[0]))
    own = jnp.where(first, done[:tok_rows], done[tok_rows:])
    rest = other_core(jnp.where(first, done[tok_rows:], done[:tok_rows]))
    return jnp.where(first, jnp.concatenate([own, rest], axis=1), jnp.concatenate([rest, own], axis=1))


def solution(mesh):
    fine = Mesh(mesh.devices.reshape(2, 2, RING, RING, CORES), ALL_AXES)
    experts = ("xh", "z", "y", "c")
    return jax.shard_map(
        per_device,
        mesh=fine,
        in_specs=(
            P(ALL_AXES, None),
            P(ALL_AXES, None),
            P(ALL_AXES, None),
            P(),
            P(experts, None, "dp"),
            P(experts, None, "dp"),
            P(experts, "dp", None),
        ),
        out_specs=P(ALL_AXES, None),
        check_vma=False,
    )
```

time: 206 us -> 197 us (0.956); the launches traced: 204 us -> 197 us
  waiting for transfers between devices: 71.9 us -> 106 us
  starting transfers between devices: 77.5 us -> 44 us
  Pallas kernels: 43.7 us -> 40.1 us
  local copies, waits for them, and re-layouts: 7.31 us -> 4.09 us
    ppermute x12 -> x6, waiting for transfers between devices: 16.5 us -> 30.4 us  [scattered(): lax.ppermute(b, ALL_AXES, back_perm(axes, s))]
    ppermute x9 -> x4, starting transfers between devices: 20.7 us -> 7.41 us  [other_core(): return lax.ppermute(value, 'c', [(0, 1), (1, 0)])]
    ppermute x12 -> x6, waiting for transfers between devices: 14.5 us -> 26.3 us  [gathered(): lax.ppermute(value, ALL_AXES, ring_perm(axes, s))]
    ppermute x12 -> x6, starting transfers between devices: 17.5 us -> 6.44 us  [scattered(): lax.ppermute(b, ALL_AXES, back_perm(axes, s))]
    ppermute x12 -> x6, starting transfers between devices: 18.6 us -> 8.83 us  [gathered(): lax.ppermute(value, ALL_AXES, ring_perm(axes, s))]
    ppermute x18 -> x12, waiting for transfers between devices: 38.8 us -> 47.6 us  [hop(): lax.ppermute(blocks[r], ALL_AXES, perm(axes, SHIFTS[r], cross))]
    pallas_call x7 -> x6, Pallas kernels: 35.9 us -> 30.4 us  [the longest x1 13.8 us: expert(): pl.pallas_call(expert_kernel, out_shape=[jax.ShapeDtypeStruct((BLOCK, HAL...]
    unnamed x35 -> x22, local copies, waits for them, and re-layouts: 5.26 us -> 3.96 us
  transfers between devices with their start and end apart: 51 -> 28, of which waited for: 20 -> 21; matrix products, arithmetic and copies ran while one was open for 0% -> 0% of each run, Pallas kernels for 12% -> 10%
where the time goes in v1:
time: 197 us
  waiting for transfers between devices  106 us (54%)
  starting transfers between devices  44 us (22%)
  Pallas kernels  40.1 us (20%)
  local copies, waits for them, and re-layouts  4.09 us (2%)
  other arithmetic  2.2 us (1%)
    ppermute x12, waiting for transfers between devices, hop(): lax.ppermute(blocks[r], ALL_AXES, perm(axes, SHIFTS[r], cross))  47.6 us
    ppermute x6, waiting for transfers between devices, scattered(): lax.ppermute(b, ALL_AXES, back_perm(axes, s))  30.4 us
    ppermute x6, waiting for transfers between devices, gathered(): lax.ppermute(value, ALL_AXES, ring_perm(axes, s))  26.3 us
    ppermute x12, starting transfers between devices, hop(): lax.ppermute(blocks[r], ALL_AXES, perm(axes, SHIFTS[r], cross))  21.3 us
    pallas_call x1, Pallas kernels, expert(): pl.pallas_call(expert_kernel, out_shape=[jax.ShapeDtypeStruct((BLOCK, HAL...  13.8 us
    pallas_call x1, Pallas kernels, project(): pl.pallas_call(project_kernel, out_shape=jax.ShapeDtypeStruct((rows, 2 *...  9.7 us
    ppermute x6, starting transfers between devices, gathered(): lax.ppermute(value, ALL_AXES, ring_perm(axes, s))  8.83 us
    ppermute x4, starting transfers between devices, other_core(): return lax.ppermute(value, 'c', [(0, 1), (1, 0)])  7.41 us
  transfers between devices with their start and end apart: 28, of which 21 were waited for; matrix products, arithmetic and copies ran while one was open for 0% of the time, Pallas kernels for 10%

profile of v1, /device:TPU:1, one launch (start us, length us, event | category | flops | bytes accessed | tf_op | source)
XLA Modules:
  0.0 196.7 jit_solution(15082641627017702836)
XLA Ops:
  0.8 0.9 copy-done.2
  3.8 0.8 shard_map.82
  4.5 1.4 collective-permute-start
  5.9 1.0 collective-permute-done
  7.0 3.1 %collective-permute-start.3 = (bf16[32,3712]{1,0:T(8,128)(2,1)S(1)}, bf16[32,3712]{1,0:T(8,128)(2,1)S(1)}, u32[]{:S(2)}, u32[]{:S(2)}) collective-permute-start(bf16[32,3712]{1,0:T(8,128)(2,1)S(1)} %maximum_select_fusion), channel_id=1, source_target_pairs={{0,16},{1,5},{2,18},{3,7},{4,20},{5,1},{6,22},{7,3},{8,24},{9,13},... | collective-permute-start | bytes 712712 | tf_op jit(solution)/shard_map/ppermute | solution.py:49
  10.0 0.8 collective-permute-start.2
  11.5 2.3 %collective-permute-done.3 = bf16[32,3712]{1,0:T(8,128)(2,1)S(1)} collective-permute-done((bf16[32,3712]{1,0:T(8,128)(2,1)S(1)}, bf16[32,3712]{1,0:T(8,128)(2,1)S(1)}, u32[]{:S(2)}, u32[]{:S(2)}) %collective-permute-start.3) | collective-permute-done | bytes 237600 | tf_op jit(solution)/shard_map/ppermute | solution.py:49
  13.8 3.0 %collective-permute-done.2 = bf16[32,3712]{1,0:T(8,128)(2,1)S(1)} collective-permute-done((bf16[32,3712]{1,0:T(8,128)(2,1)S(1)}, bf16[32,3712]{1,0:T(8,128)(2,1)S(1)}, u32[]{:S(2)}, u32[]{:S(2)}) %collective-permute-start.2) | collective-permute-done | bytes 237600 | tf_op jit(solution)/shard_map/ppermute | solution.py:49
  17.4 2.8 %collective-permute-start.6 = (bf16[128,3712]{1,0:T(8,128)(2,1)S(1)}, bf16[128,3712]{1,0:T(8,128)(2,1)S(1)}, u32[]{:S(2)}, u32[]{:S(2)}) collective-permute-start(bf16[128,3712]{1,0:T(8,128)(2,1)S(1)} %pad_maximum_fusion.refs_0_.refs_8_), channel_id=1, source_target_pairs={{0,4},{1,33},{2,6},{3,35},{4,0},{5,37},{6,2},{7,39},{8,12},{9,41},... | collective-permute-start | bytes 2850824 | tf_op jit(solution)/shard_map/ppermute | solution.py:49
  20.2 0.9 collective-permute-start.5
  21.6 10.2 %collective-permute-done.6.refs_3_.refs_11_ = bf16[128,3712]{1,0:T(8,128)(2,1)S(1)} collective-permute-done((bf16[128,3712]{1,0:T(8,128)(2,1)S(1)}, bf16[128,3712]{1,0:T(8,128)(2,1)S(1)}, u32[]{:S(2)}, u32[]{:S(2)}) %collective-permute-start.6) | collective-permute-done | bytes 950304 | tf_op jit(solution)/shard_map/ppermute | solution.py:49
  31.9 10.3 %collective-permute-done.5.refs_2_.refs_10_ = bf16[128,3712]{1,0:T(8,128)(2,1)S(1)} collective-permute-done((bf16[128,3712]{1,0:T(8,128)(2,1)S(1)}, bf16[128,3712]{1,0:T(8,128)(2,1)S(1)}, u32[]{:S(2)}, u32[]{:S(2)}) %collective-permute-start.5) | collective-permute-done | bytes 950304 | tf_op jit(solution)/shard_map/ppermute | solution.py:49
  42.1 2.2 %shard_map.83 = (bf16[128,3584]{1,0:T(8,128)(2,1)S(1)}, bf16[128,3584]{1,0:T(8,128)(2,1)S(1)}, bf16[128,3584]{1,0:T(8,128)(2,1)S(1)}, bf16[128,3584]{1,0:T(8,128)(2,1)S(1)}) custom-call(s32[8]{0:T(128)S(1)} %concatenate.18.info, bf16[128,3712]{1,0:T(8,128)(2,1)S(1)} %pad_maximum_fusion.refs_0_.refs_8_, ...), custom_call_target="tpu_custom_call" | custom-call | flops 469762048 | bytes 7340032 | tf_op jit(solution)/shard_map/pallas_call | solution.py:119
  44.4 1.4 collective-permute-start.7
  45.8 2.5 %collective-permute-start.8 = (bf16[128,3584]{1,0:T(8,128)(2,1)S(1)}, bf16[128,3584]{1,0:T(8,128)(2,1)S(1)}, u32[]{:S(2)}, u32[]{:S(2)}) collective-permute-start(bf16[128,3584]{1,0:T(8,128)(2,1)S(1)} %get-tuple-element.32), channel_id=1, source_target_pairs={{0,96},{1,25},{2,98},{3,27},{4,100},{5,29},{6,102},{7,31},{8,104},... | collective-permute-start | bytes 2752520 | tf_op jit(solution)/shard_map/ppermute | solution.py:61
  48.3 1.1 collective-permute-start.9
  49.4 3.2 %shard_map.85 = (bf16[128,3584]{1,0:T(8,128)(2,1)}, bf16[128,3584]{1,0:T(8,128)(2,1)S(1)}, bf16[128,3584]{1,0:T(8,128)(2,1)S(1)}, bf16[128,3584]{1,0:T(8,128)(2,1)S(1)}) custom-call(s32[8]{0:T(128)S(1)} %concatenate.18.info, bf16[128,3712]{1,0:T(8,128)(2,1)S(1)} %pad_maximum_fusion.refs_0_.refs_8_, ...), custom_call_target="tpu_custom_call" | custom-call | flops 469762048 | bytes 7340032 | tf_op jit(solution)/shard_map/pallas_call | solution.py:119
  52.5 3.4 %collective-permute-start.10 = (bf16[128,3584]{1,0:T(8,128)(2,1)}, bf16[128,3584]{1,0:T(8,128)(2,1)}, u32[]{:S(2)}, u32[]{:S(2)}) collective-permute-start(bf16[128,3584]{1,0:T(8,128)(2,1)} %get-tuple-element.34), channel_id=1, source_target_pairs={{0,1},{1,0},{2,3},{3,2},{4,5},{5,4},{6,7},{7,6},{8,9},{9,8},{10,11... | collective-permute-start | bytes 2752520 | tf_op jit(solution)/shard_map/ppermute | solution.py:57
  56.1 3.1 %collective-permute-done.7.refs_1_ = bf16[128,3584]{1,0:T(8,128)(2,1)S(1)} collective-permute-done((bf16[128,3584]{1,0:T(8,128)(2,1)S(1)}, bf16[128,3584]{1,0:T(8,128)(2,1)S(1)}, u32[]{:S(2)}, u32[]{:S(2)}) %collective-permute-start.7) | collective-permute-done | bytes 917536 | tf_op jit(solution)/shard_map/ppermute | solution.py:61
  59.3 4.9 %collective-permute-start.12 = (bf16[128,3584]{1,0:T(8,128)(2,1)S(1)}, bf16[128,3584]{1,0:T(8,128)(2,1)}, u32[]{:S(2)}, u32[]{:S(2)}) collective-permute-start(bf16[128,3584]{1,0:T(8,128)(2,1)S(1)} %get-tuple-element.36), channel_id=1, source_target_pairs={{0,97},{1,24},{2,99},{3,26},{4,101},{5,28},{6,103},{7,30},{8,105},... | collective-permute-start | bytes 2752520 | tf_op jit(solution)/shard_map/ppermute | solution.py:61
  64.2 4.2 %collective-permute-done.8.refs_2_ = bf16[128,3584]{1,0:T(8,128)(2,1)S(1)} collective-permute-done((bf16[128,3584]{1,0:T(8,128)(2,1)S(1)}, bf16[128,3584]{1,0:T(8,128)(2,1)S(1)}, u32[]{:S(2)}, u32[]{:S(2)}) %collective-permute-start.8) | collective-permute-done | bytes 917536 | tf_op jit(solution)/shard_map/ppermute | solution.py:61
  68.4 5.0 %collective-permute-start.13 = (bf16[128,3584]{1,0:T(8,128)(2,1)S(1)}, bf16[128,3584]{1,0:T(8,128)(2,1)}, u32[]{:S(2)}, u32[]{:S(2)}) collective-permute-start(bf16[128,3584]{1,0:T(8,128)(2,1)S(1)} %get-tuple-element.37), channel_id=1, source_target_pairs={{0,33},{1,16},{2,35},{3,18},{4,37},{5,20},{6,39},{7,22},{8,41},{9,... | collective-permute-start | bytes 2752520 | tf_op jit(solution)/shard_map/ppermute | solution.py:61
  73.4 0.9 copy-done.10
  74.4 9.7 %shard_map.84.refs_0_ = f32[512,1024]{1,0:T(8,128)} custom-call(s32[8]{0:T(128)} %copy-done.3, bf16[128,3584]{1,0:T(8,128)(2,1)} %copy-done.1, bf16[128,3584]{1,0:T(8,128)(2,1)} %copy-done.8, bf16[128,3584]{1,0:T(8,128)(2,1)} %copy-done.9, bf16[128,3584]{1,0:T(8,128)(2,1)} %copy-done.10, bf16[7168,512]{1,0:T(8,128)(2,1)} %bitcast.10, bf16[7168,512]{1,0:T(8,128)(2,1)} %bitcast.12), custom_call_target="tpu_custom_call" | custom-call | flops 3758096384 | bytes 11010048 | tf_op jit(solution)/shard_map/pallas_call | solution.py:250
  84.1 4.0 %collective-permute-done.12.refs_3_ = bf16[128,3584]{1,0:T(8,128)(2,1)} collective-permute-done((bf16[128,3584]{1,0:T(8,128)(2,1)S(1)}, bf16[128,3584]{1,0:T(8,128)(2,1)}, u32[]{:S(2)}, u32[]{:S(2)}) %collective-permute-start.12) | collective-permute-done | bytes 917536 | tf_op jit(solution)/shard_map/ppermute | solution.py:61
  88.1 4.1 %collective-permute-done.13.refs_4_ = bf16[128,3584]{1,0:T(8,128)(2,1)} collective-permute-done((bf16[128,3584]{1,0:T(8,128)(2,1)S(1)}, bf16[128,3584]{1,0:T(8,128)(2,1)}, u32[]{:S(2)}, u32[]{:S(2)}) %collective-permute-start.13) | collective-permute-done | bytes 917536 | tf_op jit(solution)/shard_map/ppermute | solution.py:61
  92.2 13.8 %shard_map.86 = (bf16[128,3584]{1,0:T(8,128)(2,1)}, bf16[128,3584]{1,0:T(8,128)(2,1)}, bf16[128,3584]{1,0:T(8,128)(2,1)}, bf16[128,3584]{1,0:T(8,128)(2,1)}, bf16[512,512]{1,0:T(8,128)(2,1)}) custom-call(s32[8]{0:T(128)} %copy-done.3, f32[512,1024]{1,0:T(8,128)} %shard_map.84.refs_0_, bf16[128,3584]{1,0:T(8,128)(2,1)} %collective-permute-done.10.refs_1_, ...), custom_call_target="tpu_custom_call" | custom-call | flops 5637144576 | bytes 18350080 | tf_op jit(solution)/shard_map/pallas_call | solution.py:330
  106.1 2.1 %collective-permute-start.14 = (bf16[128,3584]{1,0:T(8,128)(2,1)}, bf16[128,3584]{1,0:T(8,128)(2,1)S(1)}, u32[]{:S(2)}, u32[]{:S(2)}) collective-permute-start(bf16[128,3584]{1,0:T(8,128)(2,1)} %get-tuple-element.39), channel_id=1, source_target_pairs={{64,0},{9,1},{66,2},{11,3},{68,4},{13,5},{70,6},{15,7},{72,8},{17,... | collective-permute-start | bytes 2752520 | tf_op jit(solution)/shard_map/ppermute | solution.py:61
  108.1 1.3 collective-permute-start.16
  109.5 6.9 %shard_map.87 = (bf16[128,3584]{1,0:T(8,128)(2,1)}, bf16[128,3584]{1,0:T(8,128)(2,1)}, bf16[128,3584]{1,0:T(8,128)(2,1)}, bf16[128,3584]{1,0:T(8,128)(2,1)}) custom-call(s32[8]{0:T(128)} %copy-done.3, bf16[512,512]{1,0:T(8,128)(2,1)} %get-tuple-element.42.hidden, bf16[512,7168]{1,0:T(8,128)(2,1)} %bitcast.15), custom_call_target="tpu_custom_call" | custom-call | flops 1879048192 | bytes 7340032 | tf_op jit(solution)/shard_map/pallas_call | solution.py:369
  116.4 2.8 %collective-permute-start.18 = (bf16[128,3584]{1,0:T(8,128)(2,1)}, bf16[128,3584]{1,0:T(8,128)(2,1)S(1)}, u32[]{:S(2)}, u32[]{:S(2)}) collective-permute-start(bf16[128,3584]{1,0:T(8,128)(2,1)} %get-tuple-element.44), channel_id=1, source_target_pairs={{65,0},{8,1},{67,2},{10,3},{69,4},{12,5},{71,6},{14,7},{73,8},{16,... | collective-permute-start | bytes 2752520 | tf_op jit(solution)/shard_map/ppermute | solution.py:61
  119.2 2.8 %collective-permute-done.14.refs_1_ = bf16[128,3584]{1,0:T(8,128)(2,1)S(1)} collective-permute-done((bf16[128,3584]{1,0:T(8,128)(2,1)}, bf16[128,3584]{1,0:T(8,128)(2,1)S(1)}, u32[]{:S(2)}, u32[]{:S(2)}) %collective-permute-start.14) | collective-permute-done | bytes 917536 | tf_op jit(solution)/shard_map/ppermute | solution.py:61
  122.0 11.1 %collective-permute-done.15.refs_2_ = bf16[128,3584]{1,0:T(8,128)(2,1)S(1)} collective-permute-done((bf16[128,3584]{1,0:T(8,128)(2,1)}, bf16[128,3584]{1,0:T(8,128)(2,1)S(1)}, u32[]{:S(2)}, u32[]{:S(2)}) %collective-permute-start.15) | collective-permute-done | bytes 917536 | tf_op jit(solution)/shard_map/ppermute | solution.py:61
  133.1 1.0 collective-permute-done.16.refs_3_
  134.2 13.2 %collective-permute-done.18.refs_5_ = bf16[128,3584]{1,0:T(8,128)(2,1)S(1)} collective-permute-done((bf16[128,3584]{1,0:T(8,128)(2,1)}, bf16[128,3584]{1,0:T(8,128)(2,1)S(1)}, u32[]{:S(2)}, u32[]{:S(2)}) %collective-permute-start.18) | collective-permute-done | bytes 917536 | tf_op jit(solution)/shard_map/ppermute | solution.py:61
  147.4 3.9 %collective-permute-done.19.refs_6_ = bf16[128,3584]{1,0:T(8,128)(2,1)S(1)} collective-permute-done((bf16[128,3584]{1,0:T(8,128)(2,1)}, bf16[128,3584]{1,0:T(8,128)(2,1)S(1)}, u32[]{:S(2)}, u32[]{:S(2)}) %collective-permute-start.19) | collective-permute-done | bytes 917536 | tf_op jit(solution)/shard_map/ppermute | solution.py:61
  151.3 3.5 %shard_map.88 = (bf16[128,3584]{1,0:T(8,128)(2,1)S(1)}, bf16[128,3584]{1,0:T(8,128)(2,1)S(1)}, bf16[128,3584]{1,0:T(8,128)(2,1)S(1)}, bf16[128,3584]{1,0:T(8,128)(2,1)S(1)}) custom-call(s32[8]{0:T(128)S(1)} %copy-done.4, bf16[128,3584]{1,0:T(8,128)(2,1)S(1)} %copy-done, bf16[128,3584]{1,0:T(8,128)(2,1)S(1)} %collective-permute-done.14.refs_1_, ...), custom_call_target="tpu_custom_call" | custom-call | flops 1879048192 | bytes 11010048 | tf_op jit(solution)/shard_map/pallas_call | solution.py:152
  154.8 2.0 %collective-permute-start.21 = (bf16[128,3584]{1,0:T(8,128)(2,1)S(1)}, bf16[128,3584]{1,0:T(8,128)(2,1)S(1)}, u32[]{:S(2)}, u32[]{:S(2)}) collective-permute-start(bf16[128,3584]{1,0:T(8,128)(2,1)S(1)} %get-tuple-element.48), channel_id=1, source_target_pairs={{2,0},{65,1},{4,2},{67,3},{6,4},{69,5},{0,6},{71,7},{10,8},{73,9},... | collective-permute-start | bytes 2752520 | tf_op jit(solution)/shard_map/ppermute | solution.py:53
  156.8 1.3 collective-permute-start.23
  158.1 18.9 %collective-permute-done.21 = bf16[128,3584]{1,0:T(8,128)(2,1)S(1)} collective-permute-done((bf16[128,3584]{1,0:T(8,128)(2,1)S(1)}, bf16[128,3584]{1,0:T(8,128)(2,1)S(1)}, u32[]{:S(2)}, u32[]{:S(2)}) %collective-permute-start.21) | collective-permute-done | bytes 917536 | tf_op jit(solution)/shard_map/ppermute | solution.py:53
  177.0 3.4 %collective-permute-done.22 = bf16[128,3584]{1,0:T(8,128)(2,1)S(1)} collective-permute-done((bf16[128,3584]{1,0:T(8,128)(2,1)S(1)}, bf16[128,3584]{1,0:T(8,128)(2,1)S(1)}, u32[]{:S(2)}, u32[]{:S(2)}) %collective-permute-start.22) | collective-permute-done | bytes 917536 | tf_op jit(solution)/shard_map/ppermute | solution.py:53
  181.0 2.1 %collective-permute-start.24 = (bf16[32,3584]{1,0:T(8,128)(2,1)S(1)}, bf16[32,3584]{1,0:T(8,128)(2,1)S(1)}, u32[]{:S(2)}, u32[]{:S(2)}) collective-permute-start(bf16[32,3584]{1,0:T(8,128)(2,1)S(1)} %get-tuple-element.51), channel_id=1, source_target_pairs={{8,0},{3,1},{10,2},{5,3},{12,4},{7,5},{14,6},{1,7},{16,8},{11,9},{... | collective-permute-start | bytes 688136 | tf_op jit(solution)/shard_map/ppermute | solution.py:53
  184.2 4.4 %collective-permute-done.24 = bf16[32,3584]{1,0:T(8,128)(2,1)S(1)} collective-permute-done((bf16[32,3584]{1,0:T(8,128)(2,1)S(1)}, bf16[32,3584]{1,0:T(8,128)(2,1)S(1)}, u32[]{:S(2)}, u32[]{:S(2)}) %collective-permute-start.24) | collective-permute-done | bytes 229408 | tf_op jit(solution)/shard_map/ppermute | solution.py:53
  188.5 1.3 collective-permute-done.26
  189.8 2.4 %collective-permute-done.25 = bf16[32,3584]{1,0:T(8,128)(2,1)S(1)} collective-permute-done((bf16[32,3584]{1,0:T(8,128)(2,1)S(1)}, bf16[32,3584]{1,0:T(8,128)(2,1)S(1)}, u32[]{:S(2)}, u32[]{:S(2)}) %collective-permute-start.25) | collective-permute-done | bytes 229408 | tf_op jit(solution)/shard_map/ppermute | solution.py:53
  192.4 2.5 %collective-permute-start.27 = (bf16[16,3584]{1,0:T(8,128)(2,1)S(1)}, bf16[16,3584]{1,0:T(8,128)(2,1)S(1)}, u32[]{:S(2)}, u32[]{:S(2)}) collective-permute-start(bf16[16,3584]{1,0:T(8,128)(2,1)S(1)} %get-tuple-element.55), channel_id=1, source_target_pairs={{0,1},{1,0},{2,3},{3,2},{4,5},{5,4},{6,7},{7,6},{8,9},{9,8},{10,11... | collective-permute-start | bytes 344072 | tf_op jit(solution)/shard_map/ppermute | solution.py:57
  194.9 1.0 collective-permute-done.27
  195.9 0.7 maximum_select_fusion.1
  (46 shorter events, 6.8 us)
Async XLA Ops:
  0.8 48.6 %copy-start.3 = (s32[8]{0:T(128)}, s32[8]{0:T(128)S(1)}, u32[]{:S(2)}) copy-start(s32[8]{0:T(128)S(1)} %concatenate.18.info) | copy-start | bytes 100
  0.8 0.9 copy-start.2
  1.7 0.7 copy-start.5
  2.4 0.7 copy-start.6
  3.1 0.7 copy-start.7
  4.5 2.4 %collective-permute-start = (bf16[16,3712]{1,0:T(8,128)(2,1)S(1)}, bf16[16,3712]{1,0:T(8,128)(2,1)S(1)}, u32[]{:S(2)}, u32[]{:S(2)}) collective-permute-start(bf16[16,3712]{1,0:T(8,128)(2,1)S(1)} %get-tuple-element.29), channel_id=1, source_target_pairs={{0,1},{1,0},{2,3},{3,2},{4,5},{5,4},{6,7},{7,6},{8,9},{9,8},{10,11... | collective-permute-start | bytes 356360 | tf_op jit(solution)/shard_map/ppermute | solution.py:57
  7.0 6.9 %collective-permute-start.3 = (bf16[32,3712]{1,0:T(8,128)(2,1)S(1)}, bf16[32,3712]{1,0:T(8,128)(2,1)S(1)}, u32[]{:S(2)}, u32[]{:S(2)}) collective-permute-start(bf16[32,3712]{1,0:T(8,128)(2,1)S(1)} %maximum_select_fusion), channel_id=1, source_target_pairs={{0,16},{1,5},{2,18},{3,7},{4,20},{5,1},{6,22},{7,3},{8,24},{9,13},... | collective-permute-start | bytes 712712 | tf_op jit(solution)/shard_map/ppermute | solution.py:49
  10.0 6.8 %collective-permute-start.2 = (bf16[32,3712]{1,0:T(8,128)(2,1)S(1)}, bf16[32,3712]{1,0:T(8,128)(2,1)S(1)}, u32[]{:S(2)}, u32[]{:S(2)}) collective-permute-start(bf16[32,3712]{1,0:T(8,128)(2,1)S(1)} %maximum_select_fusion), channel_id=1, source_target_pairs={{0,24},{1,7},{2,26},{3,1},{4,28},{5,3},{6,30},{7,5},{8,0},{9,15},{... | collective-permute-start | bytes 712712 | tf_op jit(solution)/shard_map/ppermute | solution.py:49
  10.8 6.5 %collective-permute-start.1 = (bf16[32,3712]{1,0:T(8,128)(2,1)S(1)}, bf16[32,3712]{1,0:T(8,128)(2,1)S(1)}, u32[]{:S(2)}, u32[]{:S(2)}) collective-permute-start(bf16[32,3712]{1,0:T(8,128)(2,1)S(1)} %maximum_select_fusion), channel_id=1, source_target_pairs={{0,8},{1,3},{2,10},{3,5},{4,12},{5,7},{6,14},{7,1},{8,16},{9,11},{... | collective-permute-start | bytes 712712 | tf_op jit(solution)/shard_map/ppermute | solution.py:49
  17.4 14.5 %collective-permute-start.6 = (bf16[128,3712]{1,0:T(8,128)(2,1)S(1)}, bf16[128,3712]{1,0:T(8,128)(2,1)S(1)}, u32[]{:S(2)}, u32[]{:S(2)}) collective-permute-start(bf16[128,3712]{1,0:T(8,128)(2,1)S(1)} %pad_maximum_fusion.refs_0_.refs_8_), channel_id=1, source_target_pairs={{0,4},{1,33},{2,6},{3,35},{4,0},{5,37},{6,2},{7,39},{8,12},{9,41},... | collective-permute-start | bytes 2850824 | tf_op jit(solution)/shard_map/ppermute | solution.py:49
  20.2 22.0 %collective-permute-start.5 = (bf16[128,3712]{1,0:T(8,128)(2,1)S(1)}, bf16[128,3712]{1,0:T(8,128)(2,1)S(1)}, u32[]{:S(2)}, u32[]{:S(2)}) collective-permute-start(bf16[128,3712]{1,0:T(8,128)(2,1)S(1)} %pad_maximum_fusion.refs_0_.refs_8_), channel_id=1, source_target_pairs={{0,6},{1,97},{2,0},{3,99},{4,2},{5,101},{6,4},{7,103},{8,14},{9,10... | collective-permute-start | bytes 2850824 | tf_op jit(solution)/shard_map/ppermute | solution.py:49
  21.0 21.1 %collective-permute-start.4 = (bf16[128,3712]{1,0:T(8,128)(2,1)S(1)}, bf16[128,3712]{1,0:T(8,128)(2,1)S(1)}, u32[]{:S(2)}, u32[]{:S(2)}) collective-permute-start(bf16[128,3712]{1,0:T(8,128)(2,1)S(1)} %pad_maximum_fusion.refs_0_.refs_8_), channel_id=1, source_target_pairs={{0,2},{1,65},{2,4},{3,67},{4,6},{5,69},{6,0},{7,71},{8,10},{9,73},... | collective-permute-start | bytes 2850824 | tf_op jit(solution)/shard_map/ppermute | solution.py:49
  44.4 8.2 %copy-start.1 = (bf16[128,3584]{1,0:T(8,128)(2,1)}, bf16[128,3584]{1,0:T(8,128)(2,1)S(1)}, u32[]{:S(2)}) copy-start(bf16[128,3584]{1,0:T(8,128)(2,1)S(1)} %get-tuple-element.30.refs_0_) | copy-start | bytes 2752516
  44.4 14.9 %collective-permute-start.7 = (bf16[128,3584]{1,0:T(8,128)(2,1)S(1)}, bf16[128,3584]{1,0:T(8,128)(2,1)S(1)}, u32[]{:S(2)}, u32[]{:S(2)}) collective-permute-start(bf16[128,3584]{1,0:T(8,128)(2,1)S(1)} %get-tuple-element.31), channel_id=1, source_target_pairs={{0,64},{1,9},{2,66},{3,11},{4,68},{5,13},{6,70},{7,15},{8,72},{9,1... | collective-permute-start | bytes 2752520 | tf_op jit(solution)/shard_map/ppermute | solution.py:61
  45.8 22.6 %collective-permute-start.8 = (bf16[128,3584]{1,0:T(8,128)(2,1)S(1)}, bf16[128,3584]{1,0:T(8,128)(2,1)S(1)}, u32[]{:S(2)}, u32[]{:S(2)}) collective-permute-start(bf16[128,3584]{1,0:T(8,128)(2,1)S(1)} %get-tuple-element.32), channel_id=1, source_target_pairs={{0,96},{1,25},{2,98},{3,27},{4,100},{5,29},{6,102},{7,31},{8,104},... | collective-permute-start | bytes 2752520 | tf_op jit(solution)/shard_map/ppermute | solution.py:61
  48.3 25.2 %collective-permute-start.9 = (bf16[128,3584]{1,0:T(8,128)(2,1)S(1)}, bf16[128,3584]{1,0:T(8,128)(2,1)S(1)}, u32[]{:S(2)}, u32[]{:S(2)}) collective-permute-start(bf16[128,3584]{1,0:T(8,128)(2,1)S(1)} %get-tuple-element.33), channel_id=1, source_target_pairs={{0,32},{1,17},{2,34},{3,19},{4,36},{5,21},{6,38},{7,23},{8,40},{9,... | collective-permute-start | bytes 2752520 | tf_op jit(solution)/shard_map/ppermute | solution.py:61
  52.5 31.6 %collective-permute-start.10 = (bf16[128,3584]{1,0:T(8,128)(2,1)}, bf16[128,3584]{1,0:T(8,128)(2,1)}, u32[]{:S(2)}, u32[]{:S(2)}) collective-permute-start(bf16[128,3584]{1,0:T(8,128)(2,1)} %get-tuple-element.34), channel_id=1, source_target_pairs={{0,1},{1,0},{2,3},{3,2},{4,5},{5,4},{6,7},{7,6},{8,9},{9,8},{10,11... | collective-permute-start | bytes 2752520 | tf_op jit(solution)/shard_map/ppermute | solution.py:57
  55.9 28.2 %collective-permute-start.11 = (bf16[128,3584]{1,0:T(8,128)(2,1)S(1)}, bf16[128,3584]{1,0:T(8,128)(2,1)}, u32[]{:S(2)}, u32[]{:S(2)}) collective-permute-start(bf16[128,3584]{1,0:T(8,128)(2,1)S(1)} %get-tuple-element.35), channel_id=1, source_target_pairs={{0,65},{1,8},{2,67},{3,10},{4,69},{5,12},{6,71},{7,14},{8,73},{9,1... | collective-permute-start | bytes 2752520 | tf_op jit(solution)/shard_map/ppermute | solution.py:61
  59.3 14.2 %copy-start.8 = (bf16[128,3584]{1,0:T(8,128)(2,1)}, bf16[128,3584]{1,0:T(8,128)(2,1)S(1)}, u32[]{:S(2)}) copy-start(bf16[128,3584]{1,0:T(8,128)(2,1)S(1)} %collective-permute-done.7.refs_1_) | copy-start | bytes 2752516
  59.3 28.8 %collective-permute-start.12 = (bf16[128,3584]{1,0:T(8,128)(2,1)S(1)}, bf16[128,3584]{1,0:T(8,128)(2,1)}, u32[]{:S(2)}, u32[]{:S(2)}) collective-permute-start(bf16[128,3584]{1,0:T(8,128)(2,1)S(1)} %get-tuple-element.36), channel_id=1, source_target_pairs={{0,97},{1,24},{2,99},{3,26},{4,101},{5,28},{6,103},{7,30},{8,105},... | collective-permute-start | bytes 2752520 | tf_op jit(solution)/shard_map/ppermute | solution.py:61
  68.4 5.0 %copy-start.9 = (bf16[128,3584]{1,0:T(8,128)(2,1)}, bf16[128,3584]{1,0:T(8,128)(2,1)S(1)}, u32[]{:S(2)}) copy-start(bf16[128,3584]{1,0:T(8,128)(2,1)S(1)} %collective-permute-done.8.refs_2_) | copy-start | bytes 2752516
  68.4 23.8 %collective-permute-start.13 = (bf16[128,3584]{1,0:T(8,128)(2,1)S(1)}, bf16[128,3584]{1,0:T(8,128)(2,1)}, u32[]{:S(2)}, u32[]{:S(2)}) collective-permute-start(bf16[128,3584]{1,0:T(8,128)(2,1)S(1)} %get-tuple-element.37), channel_id=1, source_target_pairs={{0,33},{1,16},{2,35},{3,18},{4,37},{5,20},{6,39},{7,22},{8,41},{9,... | collective-permute-start | bytes 2752520 | tf_op jit(solution)/shard_map/ppermute | solution.py:61
  73.4 0.9 copy-start.10
  106.1 15.9 %collective-permute-start.14 = (bf16[128,3584]{1,0:T(8,128)(2,1)}, bf16[128,3584]{1,0:T(8,128)(2,1)S(1)}, u32[]{:S(2)}, u32[]{:S(2)}) collective-permute-start(bf16[128,3584]{1,0:T(8,128)(2,1)} %get-tuple-element.39), channel_id=1, source_target_pairs={{64,0},{9,1},{66,2},{11,3},{68,4},{13,5},{70,6},{15,7},{72,8},{17,... | collective-permute-start | bytes 2752520 | tf_op jit(solution)/shard_map/ppermute | solution.py:61
  108.1 25.0 %collective-permute-start.15 = (bf16[128,3584]{1,0:T(8,128)(2,1)}, bf16[128,3584]{1,0:T(8,128)(2,1)S(1)}, u32[]{:S(2)}, u32[]{:S(2)}) collective-permute-start(bf16[128,3584]{1,0:T(8,128)(2,1)} %get-tuple-element.40), channel_id=1, source_target_pairs={{96,0},{25,1},{98,2},{27,3},{100,4},{29,5},{102,6},{31,7},{104,8},... | collective-permute-start | bytes 2752520 | tf_op jit(solution)/shard_map/ppermute | solution.py:61
  108.1 26.0 %collective-permute-start.16 = (bf16[128,3584]{1,0:T(8,128)(2,1)}, bf16[128,3584]{1,0:T(8,128)(2,1)S(1)}, u32[]{:S(2)}, u32[]{:S(2)}) collective-permute-start(bf16[128,3584]{1,0:T(8,128)(2,1)} %get-tuple-element.41), channel_id=1, source_target_pairs={{32,0},{17,1},{34,2},{19,3},{36,4},{21,5},{38,6},{23,7},{40,8},{25... | collective-permute-start | bytes 2752520 | tf_op jit(solution)/shard_map/ppermute | solution.py:61
  109.4 41.9 %copy-start = (bf16[128,3584]{1,0:T(8,128)(2,1)S(1)}, bf16[128,3584]{1,0:T(8,128)(2,1)}, u32[]{:S(2)}) copy-start(bf16[128,3584]{1,0:T(8,128)(2,1)} %get-tuple-element.38.refs_0_) | copy-start | bytes 2752516
  109.5 41.9 %copy-start.4 = (s32[8]{0:T(128)S(1)}, s32[8]{0:T(128)}, u32[]{:S(2)}) copy-start(s32[8]{0:T(128)} %copy-done.3) | copy-start | bytes 100
  116.3 17.8 %collective-permute-start.17 = (bf16[128,3584]{1,0:T(8,128)(2,1)}, bf16[128,3584]{1,0:T(8,128)(2,1)S(1)}, u32[]{:S(2)}, u32[]{:S(2)}) collective-permute-start(bf16[128,3584]{1,0:T(8,128)(2,1)} %get-tuple-element.43), channel_id=1, source_target_pairs={{0,1},{1,0},{2,3},{3,2},{4,5},{5,4},{6,7},{7,6},{8,9},{9,8},{10,11... | collective-permute-start | bytes 2752520 | tf_op jit(solution)/shard_map/ppermute | solution.py:57
  116.4 30.9 %collective-permute-start.18 = (bf16[128,3584]{1,0:T(8,128)(2,1)}, bf16[128,3584]{1,0:T(8,128)(2,1)S(1)}, u32[]{:S(2)}, u32[]{:S(2)}) collective-permute-start(bf16[128,3584]{1,0:T(8,128)(2,1)} %get-tuple-element.44), channel_id=1, source_target_pairs={{65,0},{8,1},{67,2},{10,3},{69,4},{12,5},{71,6},{14,7},{73,8},{16,... | collective-permute-start | bytes 2752520 | tf_op jit(solution)/shard_map/ppermute | solution.py:61
  122.0 29.3 %collective-permute-start.19 = (bf16[128,3584]{1,0:T(8,128)(2,1)}, bf16[128,3584]{1,0:T(8,128)(2,1)S(1)}, u32[]{:S(2)}, u32[]{:S(2)}) collective-permute-start(bf16[128,3584]{1,0:T(8,128)(2,1)} %get-tuple-element.45), channel_id=1, source_target_pairs={{97,0},{24,1},{99,2},{26,3},{101,4},{28,5},{103,6},{30,7},{105,8},... | collective-permute-start | bytes 2752520 | tf_op jit(solution)/shard_map/ppermute | solution.py:61
  133.1 18.2 %collective-permute-start.20 = (bf16[128,3584]{1,0:T(8,128)(2,1)}, bf16[128,3584]{1,0:T(8,128)(2,1)S(1)}, u32[]{:S(2)}, u32[]{:S(2)}) collective-permute-start(bf16[128,3584]{1,0:T(8,128)(2,1)} %get-tuple-element.46), channel_id=1, source_target_pairs={{33,0},{16,1},{35,2},{18,3},{37,4},{20,5},{39,6},{22,7},{41,8},{24... | collective-permute-start | bytes 2752520 | tf_op jit(solution)/shard_map/ppermute | solution.py:61
  154.8 22.2 %collective-permute-start.21 = (bf16[128,3584]{1,0:T(8,128)(2,1)S(1)}, bf16[128,3584]{1,0:T(8,128)(2,1)S(1)}, u32[]{:S(2)}, u32[]{:S(2)}) collective-permute-start(bf16[128,3584]{1,0:T(8,128)(2,1)S(1)} %get-tuple-element.48), channel_id=1, source_target_pairs={{2,0},{65,1},{4,2},{67,3},{6,4},{69,5},{0,6},{71,7},{10,8},{73,9},... | collective-permute-start | bytes 2752520 | tf_op jit(solution)/shard_map/ppermute | solution.py:53
  156.8 23.6 %collective-permute-start.22 = (bf16[128,3584]{1,0:T(8,128)(2,1)S(1)}, bf16[128,3584]{1,0:T(8,128)(2,1)S(1)}, u32[]{:S(2)}, u32[]{:S(2)}) collective-permute-start(bf16[128,3584]{1,0:T(8,128)(2,1)S(1)} %get-tuple-element.49), channel_id=1, source_target_pairs={{6,0},{97,1},{0,2},{99,3},{2,4},{101,5},{4,6},{103,7},{14,8},{105,... | collective-permute-start | bytes 2752520 | tf_op jit(solution)/shard_map/ppermute | solution.py:53
  156.8 23.6 %collective-permute-start.23 = (bf16[128,3584]{1,0:T(8,128)(2,1)S(1)}, bf16[128,3584]{1,0:T(8,128)(2,1)S(1)}, u32[]{:S(2)}, u32[]{:S(2)}) collective-permute-start(bf16[128,3584]{1,0:T(8,128)(2,1)S(1)} %get-tuple-element.50), channel_id=1, source_target_pairs={{4,0},{33,1},{6,2},{35,3},{0,4},{37,5},{2,6},{39,7},{12,8},{41,9},... | collective-permute-start | bytes 2752520 | tf_op jit(solution)/shard_map/ppermute | solution.py:53
  181.0 7.6 %collective-permute-start.24 = (bf16[32,3584]{1,0:T(8,128)(2,1)S(1)}, bf16[32,3584]{1,0:T(8,128)(2,1)S(1)}, u32[]{:S(2)}, u32[]{:S(2)}) collective-permute-start(bf16[32,3584]{1,0:T(8,128)(2,1)S(1)} %get-tuple-element.51), channel_id=1, source_target_pairs={{8,0},{3,1},{10,2},{5,3},{12,4},{7,5},{14,6},{1,7},{16,8},{11,9},{... | collective-permute-start | bytes 688136 | tf_op jit(solution)/shard_map/ppermute | solution.py:53
  183.1 6.7 %collective-permute-start.26 = (bf16[32,3584]{1,0:T(8,128)(2,1)S(1)}, bf16[32,3584]{1,0:T(8,128)(2,1)S(1)}, u32[]{:S(2)}, u32[]{:S(2)}) collective-permute-start(bf16[32,3584]{1,0:T(8,128)(2,1)S(1)} %get-tuple-element.52), channel_id=1, source_target_pairs={{16,0},{5,1},{18,2},{7,3},{20,4},{1,5},{22,6},{3,7},{24,8},{13,9},... | collective-permute-start | bytes 688136 | tf_op jit(solution)/shard_map/ppermute | solution.py:53
  183.6 8.6 %collective-permute-start.25 = (bf16[32,3584]{1,0:T(8,128)(2,1)S(1)}, bf16[32,3584]{1,0:T(8,128)(2,1)S(1)}, u32[]{:S(2)}, u32[]{:S(2)}) collective-permute-start(bf16[32,3584]{1,0:T(8,128)(2,1)S(1)} %get-tuple-element.53), channel_id=1, source_target_pairs={{24,0},{7,1},{26,2},{1,3},{28,4},{3,5},{30,6},{5,7},{0,8},{15,9},{... | collective-permute-start | bytes 688136 | tf_op jit(solution)/shard_map/ppermute | solution.py:53
  192.4 3.5 %collective-permute-start.27 = (bf16[16,3584]{1,0:T(8,128)(2,1)S(1)}, bf16[16,3584]{1,0:T(8,128)(2,1)S(1)}, u32[]{:S(2)}, u32[]{:S(2)}) collective-permute-start(bf16[16,3584]{1,0:T(8,128)(2,1)S(1)} %get-tuple-element.55), channel_id=1, source_target_pairs={{0,1},{1,0},{2,3},{3,2},{4,5},{5,4},{6,7},{7,6},{8,9},{9,8},{10,11... | collective-permute-start | bytes 344072 | tf_op jit(solution)/shard_map/ppermute | solution.py:57

commit v2 on v1

--- a/solution.py
+++ b/solution.py
@@ -18,9 +18,11 @@
 HALF = 3584
 BLOCK = 128
 SHIFTS = (0, 1, 3, 2)
-ROUTE = (("z", "y"), ("y", "x"), ("x", "z"))
+ROUTE = (("y", "y"), ("z", "x"), ("x", "z"))
 SMALL_VMEM = 24 << 20
 LARGE_VMEM = 56 << 20
+PROJECT_VMEM = 30 << 20
+EXPERT_VMEM = 18 << 20
 
 
 def flat_index(x, z, y, c):
@@ -226,14 +228,20 @@
 
 
 def project_kernel(info, *refs):
-    blocks, (gate_hbm, up_hbm, total, x, w_in, x_sem, in_sem) = refs[:RING], refs[RING:]
-    base = info[0] * HALF
+    blocks, (gate_hbm, up_hbm, down_hbm), (total, w_far, w_out) = refs[:RING], refs[RING:RING + 3], refs[RING + 3:RING + 6]
+    x, w_in, x_sem, in_sem, far_sem, down_sem = refs[RING + 6:]
+    at_near, at_far = info[0] * HALF, (1 - info[0]) * HALF
     steps = column_chunks(HALF)
     x_copies = block_copies(blocks, x, x_sem, 0)
-    in_copies = weight_copies([(base + start, size) for start, size in steps], gate_hbm, up_hbm, w_in, in_sem)
+    in_copies = weight_copies([(at_near + start, size) for start, size in steps], gate_hbm, up_hbm, w_in, in_sem)
+    far_copies = weight_copies([(at_far, HALF)], gate_hbm, up_hbm, w_far, far_sem)[0]
+    down_copy = pltpu.make_async_copy(
+        down_hbm.at[:, pl.ds(pl.multiple_of(at_near, BLOCK), HALF)], w_out, down_sem)
     start_all(x_copies)
     for pair in in_copies:
         start_all(pair)
+    start_all(far_copies)
+    down_copy.start()
     wait_all(x_copies)
     for (start, size), pair in zip(steps, in_copies):
         wait_all(pair)
@@ -243,76 +251,70 @@
             total[...] = got
         else:
             total[...] += got
-
-
-def project(info, blocks, gate_w, up_w):
+    wait_all(far_copies)
+    down_copy.wait()
+
+
+def project(info, blocks, gate_w, up_w, down_w):
     rows, hid = RING * BLOCK, gate_w.shape[1]
+    bf = jnp.bfloat16
     return pl.pallas_call(
         project_kernel,
-        out_shape=jax.ShapeDtypeStruct((rows, 2 * hid), jnp.float32),
-        in_specs=[SMEM_SPEC] + [HBM_SPEC] * 6,
-        out_specs=VMEM_SPEC,
+        out_shape=[jax.ShapeDtypeStruct((rows, 2 * hid), jnp.float32),
+                   jax.ShapeDtypeStruct((HALF, 2 * hid), bf), jax.ShapeDtypeStruct((hid, HALF), bf)],
+        in_specs=[SMEM_SPEC] + [HBM_SPEC] * 7,
+        out_specs=[VMEM_SPEC] * 3,
         scratch_shapes=[
-            pltpu.VMEM((rows, HALF), jnp.bfloat16), pltpu.VMEM((HALF, 2 * hid), jnp.bfloat16),
+            pltpu.VMEM((rows, HALF), bf), pltpu.VMEM((HALF, 2 * hid), bf),
             pltpu.SemaphoreType.DMA((RING,)), pltpu.SemaphoreType.DMA((2 * len(column_chunks(HALF)),)),
+            pltpu.SemaphoreType.DMA((2,)), pltpu.SemaphoreType.DMA,
         ],
-        compiler_params=pltpu.CompilerParams(vmem_limit_bytes=LARGE_VMEM),
+        compiler_params=pltpu.CompilerParams(vmem_limit_bytes=PROJECT_VMEM),
         cost_estimate=pl.CostEstimate(
-            flops=4 * rows * HALF * hid, bytes_accessed=2 * (2 * HALF * hid + rows * HALF), transcendentals=0),
-    )(info, *blocks, gate_w, up_w)
-
-
-def expert_kernel(info, *refs):
-    near, far = refs[0], refs[1:1 + RING]
-    gate_hbm, up_hbm, down_hbm = refs[5:8]
-    main_outs, hidden_far = refs[8:12], refs[12]
-    x, w_in, w_out, a1, a2, h1, h2, o, x_sem, in_sem, down_sem, out_sem = refs[13:]
-    core = info[0]
-    first = core == 0
+            flops=4 * rows * HALF * hid, bytes_accessed=2 * (5 * HALF * hid + rows * HALF), transcendentals=0),
+    )(info, *blocks, gate_w, up_w, down_w)
+
+
+def expert_kernel(info, near, w_in, w_out, *refs):
+    far, main_outs, hidden_far = refs[:RING], refs[RING:2 * RING], refs[2 * RING]
+    x, a2, h1, h2, o, x_sem, out_sem = refs[2 * RING + 1:]
+    first = info[0] == 0
     half = w_in.shape[1] // 2
-    at_near, at_far = core * HALF, (1 - core) * HALF
     steps = column_chunks(HALF)
-    far_copies = block_copies(far, x, x_sem, 0)
-    near_copy = pltpu.make_async_copy(near, a1, x_sem.at[RING])
-    in_copies = weight_copies([(at_far + start, size) for start, size in steps], gate_hbm, up_hbm, w_in, in_sem)
-    down_copies = [pltpu.make_async_copy(
-        down_hbm.at[:, pl.ds(pl.multiple_of(at_near + start, BLOCK), size)], w_out.at[:, pl.ds(start, size)],
-        down_sem.at[i]) for i, (start, size) in enumerate(steps)]
-    start_all(far_copies)
-    for pair in in_copies:
-        start_all(pair)
-    near_copy.start()
-    start_all(down_copies)
-
-    wait_all(far_copies)
-    for (start, size), pair in zip(steps, in_copies):
-        wait_all(pair)
+    far_copies = [
+        [pltpu.make_async_copy(
+            far[r].at[:, pl.ds(start, size)], x.at[pl.ds(r * BLOCK, BLOCK), pl.ds(start, size)],
+            x_sem.at[RING * i + r]) for r in range(RING)]
+        for i, (start, size) in enumerate(steps)]
+    for copies in far_copies:
+        start_all(copies)
+    for (start, size), copies in zip(steps, far_copies):
+        wait_all(copies)
         cols = slice(start, start + size)
         got = jnp.dot(x[:, cols], w_in[cols, :], preferred_element_type=jnp.float32)
         if start == 0:
             a2[...] = got
         else:
             a2[...] += got
-    near_copy.wait()
+
+    rows = BLOCK // RING
 
     def activate(i, carry):
-        x, y, z = i // 16, i // 4 % 4, i % 4
-        left, right = i, z * 16 + x * 4 + y
-        i1 = pl.multiple_of(jnp.where(first, left, right) * 8, 8)
-        i2 = pl.multiple_of(jnp.where(first, right, left) * 8, 8)
-        both = a1[pl.ds(i1, 8)] + a2[pl.ds(i2, 8)]
+        left, right = i, i % RING * RING + i // RING
+        i1 = pl.multiple_of(jnp.where(first, left, right) * rows, rows)
+        i2 = pl.multiple_of(jnp.where(first, right, left) * rows, rows)
+        both = near[pl.ds(i1, rows)] + a2[pl.ds(i2, rows)]
         gate, up = both[:, :half], both[:, half:]
         value = gate / (1.0 + jnp.exp(-gate)) * up
-        h1[pl.ds(i1, 8)] = value
-        h2[pl.ds(i2, 8)] = value
+        h1[pl.ds(i1, rows)] = value
+        h2[pl.ds(i2, rows)] = value
         return carry
 
-    lax.fori_loop(0, RING ** 3, activate, 0, unroll=4)
+    lax.fori_loop(0, RING ** 2, activate, 0)
     hidden_far[...] = h2[...].astype(jnp.bfloat16)
     hidden = h1[...].astype(jnp.bfloat16)
     out_copies = []
-    for i, ((start, size), copy) in enumerate(zip(steps, down_copies)):
-        copy.wait()
+    for i, (start, size) in enumerate(steps):
         got = jnp.dot(hidden, w_out[:, start:start + size], preferred_element_type=jnp.float32)
         o[:, start:start + size] = got.astype(jnp.bfloat16)
         for r in range(RING):
@@ -323,28 +325,24 @@
     wait_all(out_copies)
 
 
-def expert(info, near, far, gate_w, up_w, down_w):
-    rows, (width, hid) = RING * BLOCK, gate_w.shape
+def expert(info, near, w_in, w_out, far):
+    rows, hid = RING * BLOCK, w_out.shape[0]
     steps = len(column_chunks(HALF))
     bf, f32 = jnp.bfloat16, jnp.float32
     out = pl.pallas_call(
         expert_kernel,
         out_shape=[jax.ShapeDtypeStruct((BLOCK, HALF), bf)] * RING + [jax.ShapeDtypeStruct((rows, hid), bf)],
-        in_specs=[SMEM_SPEC] + [HBM_SPEC] * 8,
+        in_specs=[SMEM_SPEC] + [VMEM_SPEC] * 3 + [HBM_SPEC] * RING,
         out_specs=[HBM_SPEC] * RING + [VMEM_SPEC],
         scratch_shapes=[
-            pltpu.VMEM((rows, HALF), bf), pltpu.VMEM((HALF, 2 * hid), bf), pltpu.VMEM((hid, HALF), bf),
-            pltpu.VMEM((rows, 2 * hid), f32), pltpu.VMEM((rows, 2 * hid), f32),
-            pltpu.VMEM((rows, hid), f32), pltpu.VMEM((rows, hid), f32),
-            pltpu.VMEM((rows, HALF), bf),
-            pltpu.SemaphoreType.DMA((RING + 1,)), pltpu.SemaphoreType.DMA((2 * steps,)),
-            pltpu.SemaphoreType.DMA((steps,)), pltpu.SemaphoreType.DMA((RING * steps,)),
+            pltpu.VMEM((rows, HALF), bf), pltpu.VMEM((rows, 2 * hid), f32),
+            pltpu.VMEM((rows, hid), f32), pltpu.VMEM((rows, hid), f32), pltpu.VMEM((rows, HALF), bf),
+            pltpu.SemaphoreType.DMA((RING * steps,)), pltpu.SemaphoreType.DMA((RING * steps,)),
         ],
-        compiler_params=pltpu.CompilerParams(vmem_limit_bytes=LARGE_VMEM),
+        compiler_params=pltpu.CompilerParams(vmem_limit_bytes=EXPERT_VMEM),
         cost_estimate=pl.CostEstimate(
-            flops=6 * rows * HALF * hid, bytes_accessed=2 * (3 * HALF * hid + 2 * rows * HALF),
-            transcendentals=rows * hid),
-    )(info, near, *far, gate_w, up_w, down_w)
+            flops=6 * rows * HALF * hid, bytes_accessed=4 * rows * HALF, transcendentals=rows * hid),
+    )(info, near, w_in, w_out, *far)
     return list(out[:RING]), out[RING]
 
 
@@ -405,21 +403,26 @@
     mine, theirs = begin(info, pairs, tokens, picks, mix_weights)
     theirs = other_core(theirs)
     pool = jnp.where(first, jnp.concatenate([mine, theirs]), jnp.concatenate([theirs, mine]))
-    pool = jnp.concatenate(gathered(pool, ROUTE[0]), axis=0)
-    pool = gathered(pool, ROUTE[1])
+    line, part = together(gathered(pool, ROUTE[0]), lax.ppermute(pool, ALL_AXES, ring_perm(ROUTE[1], SHIFTS[3])))
+    line = jnp.concatenate(line, axis=0)
+    ahead, part = together(hop([line] * RING, ROUTE[1], ring_perm, (1, 2)), gathered(part, ROUTE[0]))
+    pool = [line] + ahead + [jnp.concatenate(part, axis=0)]
 
     own, far = pack(info, pool, 0), pack(info, pool, 1)
     own = own[:1] + hop(own, ROUTE[2], ring_perm, (1, 2, 3))
     far = hop(far, ROUTE[2], ring_perm, (0, 1, 2, 3), cross=True)
     gate_w, up_w, down_w = gate_weight[0], up_weight[0], down_weight[0]
-    near = project(info, own, gate_w, up_w)
-    own, hidden = expert(info, near, far, gate_w, up_w, down_w)
+    near, w_in, w_out = project(info, own, gate_w, up_w, down_w)
+    own, hidden = expert(info, near, w_in, w_out, far)
     far = spread(info, hidden, down_w)
     own = own[:1] + hop(own, ROUTE[2], back_perm, (1, 2, 3))
     far = hop(far, ROUTE[2], back_perm, (0, 1, 2, 3), cross=True)
     sums = combine(info, own + far, pool)
-    sums = summed(scattered(sums, ROUTE[1]))
-    done = summed(scattered(split_rows(sums), ROUTE[0]))
+    ahead, part = together(hop(sums, ROUTE[1], back_perm, (1, 2)), scattered(split_rows(sums[3]), ROUTE[0]))
+    line, part = summed(sums[:1] + ahead), summed(part)
+    line, part = together(
+        scattered(split_rows(line), ROUTE[0]), lax.ppermute(part, ALL_AXES, back_perm(ROUTE[1], SHIFTS[3])))
+    done = summed(line + [part])
     own = jnp.where(first, done[:tok_rows], done[tok_rows:])
     rest = other_core(jnp.where(first, done[tok_rows:], done[:tok_rows]))
     return jnp.where(first, jnp.concatenate([own, rest], axis=1), jnp.concatenate([rest, own], axis=1))

time: 197 us -> 184 us (0.934)
  waiting for transfers between devices: 106 us -> 90.4 us
  starting transfers between devices: 44 us -> 52.5 us
  Pallas kernels: 40.1 us -> 34.4 us
    ppermute x6, waiting for transfers between devices: 30.4 us -> 17.2 us  [scattered(): lax.ppermute(b, ALL_AXES, back_perm(axes, s))]
    ppermute x6, waiting for transfers between devices: 26.3 us -> 18.5 us  [gathered(): lax.ppermute(value, ALL_AXES, ring_perm(axes, s))]
    ppermute x0 -> x2, starting transfers between devices: none -> 4.25 us  [the longest x1 2.91 us: per_device(): lax.ppermute(pool, ALL_AXES, ring_perm(ROUTE[1], SHIFTS[3]))]
    ppermute x12 -> x16, starting transfers between devices: 21.3 us -> 25.1 us  [hop(): lax.ppermute(blocks[r], ALL_AXES, perm(axes, SHIFTS[r], cross))]
    ppermute x12 -> x16, waiting for transfers between devices: 47.6 us -> 51.3 us  [hop(): lax.ppermute(blocks[r], ALL_AXES, perm(axes, SHIFTS[r], cross))]
    pallas_call x1, Pallas kernels: 13.8 us -> 10.2 us  [expert(): pl.pallas_call(expert_kernel, out_shape=[jax.ShapeDtypeStruct((BLOCK, HAL...]
    ppermute x4, starting transfers between devices: 7.41 us -> 4.37 us  [other_core(): return lax.ppermute(value, 'c', [(0, 1), (1, 0)])]
    ppermute x6, starting transfers between devices: 6.44 us -> 9.31 us  [scattered(): lax.ppermute(b, ALL_AXES, back_perm(axes, s))]
  transfers between devices with their start and end apart: 28 -> 34, of which waited for: 21 -> 21; matrix products, arithmetic and copies ran while one was open for 0% -> 0% of each run, Pallas kernels for 10% -> 10%
where the time goes in v2:
time: 184 us
  waiting for transfers between devices  90.4 us (49%)
  starting transfers between devices  52.5 us (29%)
  Pallas kernels  34.4 us (19%)
  local copies, waits for them, and re-layouts  4.18 us (2%)
  other arithmetic  2.08 us (1%)
    ppermute x16, waiting for transfers between devices, hop(): lax.ppermute(blocks[r], ALL_AXES, perm(axes, SHIFTS[r], cross))  51.3 us
    ppermute x16, starting transfers between devices, hop(): lax.ppermute(blocks[r], ALL_AXES, perm(axes, SHIFTS[r], cross))  25.1 us
    ppermute x6, waiting for transfers between devices, gathered(): lax.ppermute(value, ALL_AXES, ring_perm(axes, s))  18.5 us
    ppermute x6, waiting for transfers between devices, scattered(): lax.ppermute(b, ALL_AXES, back_perm(axes, s))  17.2 us
    pallas_call x1, Pallas kernels, expert(): pl.pallas_call(expert_kernel, out_shape=[jax.ShapeDtypeStruct((BLOCK, HAL...  10.2 us
    ppermute x6, starting transfers between devices, gathered(): lax.ppermute(value, ALL_AXES, ring_perm(axes, s))  9.43 us
    ppermute x6, starting transfers between devices, scattered(): lax.ppermute(b, ALL_AXES, back_perm(axes, s))  9.31 us
    pallas_call x1, Pallas kernels, project(): pl.pallas_call(project_kernel, out_shape=[jax.ShapeDtypeStruct((rows, 2 *...  7.33 us
  transfers between devices with their start and end apart: 34, of which 21 were waited for; matrix products, arithmetic and copies ran while one was open for 0% of the time, Pallas kernels for 10%

profile of v2, /device:TPU:1, one launch (start us, length us, event | category | flops | bytes accessed | tf_op | source)
XLA Modules:
  0.0 183.7 jit_solution(10496663996801124650)
XLA Ops:
  0.8 0.9 copy-done.2
  4.5 1.4 collective-permute-start
  5.9 1.0 collective-permute-done
  7.0 2.9 %collective-permute-start.4 = (bf16[32,3712]{1,0:T(8,128)(2,1)S(1)}, bf16[32,3712]{1,0:T(8,128)(2,1)S(1)}, u32[]{:S(2)}, u32[]{:S(2)}) collective-permute-start(bf16[32,3712]{1,0:T(8,128)(2,1)S(1)} %maximum_select_fusion), channel_id=1, source_target_pairs={{0,16},{1,33},{2,18},{3,35},{4,20},{5,37},{6,22},{7,39},{8,24},{9,... | collective-permute-start | bytes 712712 | tf_op jit(solution)/shard_map/ppermute | solution.py:406
  9.9 2.9 %collective-permute-start.3 = (bf16[32,3712]{1,0:T(8,128)(2,1)S(1)}, bf16[32,3712]{1,0:T(8,128)(2,1)S(1)}, u32[]{:S(2)}, u32[]{:S(2)}) collective-permute-start(bf16[32,3712]{1,0:T(8,128)(2,1)S(1)} %maximum_select_fusion), channel_id=1, source_target_pairs={{0,4},{1,5},{2,6},{3,7},{4,0},{5,1},{6,2},{7,3},{8,12},{9,13},{10,... | collective-permute-start | bytes 712712 | tf_op jit(solution)/shard_map/ppermute | solution.py:51
  14.2 2.9 %collective-permute-done.3 = bf16[32,3712]{1,0:T(8,128)(2,1)S(1)} collective-permute-done((bf16[32,3712]{1,0:T(8,128)(2,1)S(1)}, bf16[32,3712]{1,0:T(8,128)(2,1)S(1)}, u32[]{:S(2)}, u32[]{:S(2)}) %collective-permute-start.3) | collective-permute-done | bytes 237600 | tf_op jit(solution)/shard_map/ppermute | solution.py:51
  17.1 6.3 %collective-permute-done.2 = bf16[32,3712]{1,0:T(8,128)(2,1)S(1)} collective-permute-done((bf16[32,3712]{1,0:T(8,128)(2,1)S(1)}, bf16[32,3712]{1,0:T(8,128)(2,1)S(1)}, u32[]{:S(2)}, u32[]{:S(2)}) %collective-permute-start.2) | collective-permute-done | bytes 237600 | tf_op jit(solution)/shard_map/ppermute | solution.py:51
  24.3 0.8 collective-permute-start.5
  25.1 3.6 %collective-permute-start.9 = (bf16[32,3712]{1,0:T(8,128)(2,1)S(1)}, bf16[32,3712]{1,0:T(8,128)(2,1)S(1)}, u32[]{:S(2)}, u32[]{:S(2)}) collective-permute-start(bf16[32,3712]{1,0:T(8,128)(2,1)S(1)} %collective-permute-done.4), channel_id=1, source_target_pairs={{0,4},{1,5},{2,6},{3,7},{4,0},{5,1},{6,2},{7,3},{8,12},{9,13},{10,... | collective-permute-start | bytes 712712 | tf_op jit(solution)/shard_map/ppermute | solution.py:51
  28.7 0.8 collective-permute-start.8
  30.2 2.8 %collective-permute-done.9 = bf16[32,3712]{1,0:T(8,128)(2,1)S(1)} collective-permute-done((bf16[32,3712]{1,0:T(8,128)(2,1)S(1)}, bf16[32,3712]{1,0:T(8,128)(2,1)S(1)}, u32[]{:S(2)}, u32[]{:S(2)}) %collective-permute-start.9) | collective-permute-done | bytes 237600 | tf_op jit(solution)/shard_map/ppermute | solution.py:51
  33.0 6.4 %collective-permute-done.8 = bf16[32,3712]{1,0:T(8,128)(2,1)S(1)} collective-permute-done((bf16[32,3712]{1,0:T(8,128)(2,1)S(1)}, bf16[32,3712]{1,0:T(8,128)(2,1)S(1)}, u32[]{:S(2)}, u32[]{:S(2)}) %collective-permute-start.8) | collective-permute-done | bytes 237600 | tf_op jit(solution)/shard_map/ppermute | solution.py:51
  39.6 2.2 %shard_map.83 = (bf16[128,3584]{1,0:T(8,128)(2,1)S(1)}, bf16[128,3584]{1,0:T(8,128)(2,1)S(1)}, bf16[128,3584]{1,0:T(8,128)(2,1)S(1)}, bf16[128,3584]{1,0:T(8,128)(2,1)S(1)}) custom-call(s32[8]{0:T(128)S(1)} %concatenate.21.info, bf16[128,3712]{1,0:T(8,128)(2,1)S(1)} %constant_dynamic-update-slice_fusion.refs_0_.refs_8_, ...), custom_call_target="tpu_custom_call" | custom-call | flops 469762048 | bytes 7340032 | tf_op jit(solution)/shard_map/pallas_call | solution.py:121
  41.8 1.7 collective-permute-start.10
  43.5 2.3 %collective-permute-start.11 = (bf16[128,3584]{1,0:T(8,128)(2,1)S(1)}, bf16[128,3584]{1,0:T(8,128)(2,1)S(1)}, u32[]{:S(2)}, u32[]{:S(2)}) collective-permute-start(bf16[128,3584]{1,0:T(8,128)(2,1)S(1)} %get-tuple-element.68), channel_id=1, source_target_pairs={{0,96},{1,25},{2,98},{3,27},{4,100},{5,29},{6,102},{7,31},{8,104},... | collective-permute-start | bytes 2752520 | tf_op jit(solution)/shard_map/ppermute | solution.py:63
  45.8 1.2 collective-permute-start.12
  47.1 3.5 %shard_map.85 = (bf16[128,3584]{1,0:T(8,128)(2,1)}, bf16[128,3584]{1,0:T(8,128)(2,1)}, bf16[128,3584]{1,0:T(8,128)(2,1)S(1)}, bf16[128,3584]{1,0:T(8,128)(2,1)S(1)}) custom-call(s32[8]{0:T(128)S(1)} %concatenate.21.info, bf16[128,3712]{1,0:T(8,128)(2,1)S(1)} %constant_dynamic-update-slice_fusion.refs_0_.refs_8_, ...), custom_call_target="tpu_custom_call" | custom-call | flops 469762048 | bytes 7340032 | tf_op jit(solution)/shard_map/pallas_call | solution.py:121
  50.6 2.2 %collective-permute-start.13 = (bf16[128,3584]{1,0:T(8,128)(2,1)}, bf16[128,3584]{1,0:T(8,128)(2,1)S(1)}, u32[]{:S(2)}, u32[]{:S(2)}) collective-permute-start(bf16[128,3584]{1,0:T(8,128)(2,1)} %get-tuple-element.73), channel_id=1, source_target_pairs={{0,1},{1,0},{2,3},{3,2},{4,5},{5,4},{6,7},{7,6},{8,9},{9,8},{10,11... | collective-permute-start | bytes 2752520 | tf_op jit(solution)/shard_map/ppermute | solution.py:59
  52.7 4.1 %collective-permute-done.10.refs_1_ = bf16[128,3584]{1,0:T(8,128)(2,1)S(1)} collective-permute-done((bf16[128,3584]{1,0:T(8,128)(2,1)S(1)}, bf16[128,3584]{1,0:T(8,128)(2,1)S(1)}, u32[]{:S(2)}, u32[]{:S(2)}) %collective-permute-start.10) | collective-permute-done | bytes 917536 | tf_op jit(solution)/shard_map/ppermute | solution.py:63
  56.8 4.3 %collective-permute-start.15 = (bf16[128,3584]{1,0:T(8,128)(2,1)S(1)}, bf16[128,3584]{1,0:T(8,128)(2,1)S(1)}, u32[]{:S(2)}, u32[]{:S(2)}) collective-permute-start(bf16[128,3584]{1,0:T(8,128)(2,1)S(1)} %get-tuple-element.75), channel_id=1, source_target_pairs={{0,97},{1,24},{2,99},{3,26},{4,101},{5,28},{6,103},{7,30},{8,105},... | collective-permute-start | bytes 2752520 | tf_op jit(solution)/shard_map/ppermute | solution.py:63
  61.1 4.9 %collective-permute-done.11.refs_2_ = bf16[128,3584]{1,0:T(8,128)(2,1)S(1)} collective-permute-done((bf16[128,3584]{1,0:T(8,128)(2,1)S(1)}, bf16[128,3584]{1,0:T(8,128)(2,1)S(1)}, u32[]{:S(2)}, u32[]{:S(2)}) %collective-permute-start.11) | collective-permute-done | bytes 917536 | tf_op jit(solution)/shard_map/ppermute | solution.py:63
  66.0 5.0 %collective-permute-start.16 = (bf16[128,3584]{1,0:T(8,128)(2,1)S(1)}, bf16[128,3584]{1,0:T(8,128)(2,1)}, u32[]{:S(2)}, u32[]{:S(2)}) collective-permute-start(bf16[128,3584]{1,0:T(8,128)(2,1)S(1)} %get-tuple-element.76), channel_id=1, source_target_pairs={{0,33},{1,16},{2,35},{3,18},{4,37},{5,20},{6,39},{7,22},{8,41},{9,... | collective-permute-start | bytes 2752520 | tf_op jit(solution)/shard_map/ppermute | solution.py:63
  71.0 7.3 %shard_map.84 = (f32[512,1024]{1,0:T(8,128)S(1)}, bf16[3584,1024]{1,0:T(8,128)(2,1)S(1)}, bf16[512,3584]{1,0:T(8,128)(2,1)S(1)}) custom-call(s32[8]{0:T(128)S(1)} %concatenate.21.info, bf16[128,3584]{1,0:T(8,128)(2,1)S(1)} %get-tuple-element.66.refs_0_, bf16[128,3584]{1,0:T(8,128)(2,1)S(1)} %collective-permute-done.10.refs_1_, ...), custom_call_target="tpu_custom_call" | custom-call | flops 3758096384 | bytes 22020096 | tf_op jit(solution)/shard_map/pallas_call | solution.py:261
  79.2 10.4 %collective-permute-done.16.refs_3_ = bf16[128,3584]{1,0:T(8,128)(2,1)} collective-permute-done((bf16[128,3584]{1,0:T(8,128)(2,1)S(1)}, bf16[128,3584]{1,0:T(8,128)(2,1)}, u32[]{:S(2)}, u32[]{:S(2)}) %collective-permute-start.16) | collective-permute-done | bytes 917536 | tf_op jit(solution)/shard_map/ppermute | solution.py:63
  89.6 10.2 %shard_map.86 = (bf16[128,3584]{1,0:T(8,128)(2,1)S(1)}, bf16[128,3584]{1,0:T(8,128)(2,1)}, bf16[128,3584]{1,0:T(8,128)(2,1)}, bf16[128,3584]{1,0:T(8,128)(2,1)}, bf16[512,512]{1,0:T(8,128)(2,1)S(1)}) custom-call(s32[8]{0:T(128)S(1)} %concatenate.21.info, f32[512,1024]{1,0:T(8,128)S(1)} %get-tuple-element.70.near, ...), custom_call_target="tpu_custom_call" | custom-call | flops 5637144576 | bytes 7340032 | tf_op jit(solution)/shard_map/pallas_call | solution.py:332
  100.6 1.8 collective-permute-start.17
  102.4 1.2 collective-permute-start.19
  103.6 6.8 %shard_map.87 = (bf16[128,3584]{1,0:T(8,128)(2,1)}, bf16[128,3584]{1,0:T(8,128)(2,1)}, bf16[128,3584]{1,0:T(8,128)(2,1)}, bf16[128,3584]{1,0:T(8,128)(2,1)}) custom-call(s32[8]{0:T(128)} %copy-done.3, bf16[512,512]{1,0:T(8,128)(2,1)} %copy-done.1, bf16[512,7168]{1,0:T(8,128)(2,1)} %bitcast.12), custom_call_target="tpu_custom_call" | custom-call | flops 1879048192 | bytes 7340032 | tf_op jit(solution)/shard_map/pallas_call | solution.py:367
  110.5 3.9 %collective-permute-start.21 = (bf16[128,3584]{1,0:T(8,128)(2,1)}, bf16[128,3584]{1,0:T(8,128)(2,1)S(1)}, u32[]{:S(2)}, u32[]{:S(2)}) collective-permute-start(bf16[128,3584]{1,0:T(8,128)(2,1)} %get-tuple-element.83), channel_id=1, source_target_pairs={{65,0},{8,1},{67,2},{10,3},{69,4},{12,5},{71,6},{14,7},{73,8},{16,... | collective-permute-start | bytes 2752520 | tf_op jit(solution)/shard_map/ppermute | solution.py:63
  114.4 1.0 collective-permute-done.17.refs_1_
  115.4 12.1 %collective-permute-done.18.refs_2_ = bf16[128,3584]{1,0:T(8,128)(2,1)S(1)} collective-permute-done((bf16[128,3584]{1,0:T(8,128)(2,1)}, bf16[128,3584]{1,0:T(8,128)(2,1)S(1)}, u32[]{:S(2)}, u32[]{:S(2)}) %collective-permute-start.18) | collective-permute-done | bytes 917536 | tf_op jit(solution)/shard_map/ppermute | solution.py:63
  127.5 2.2 %collective-permute-done.19.refs_3_ = bf16[128,3584]{1,0:T(8,128)(2,1)S(1)} collective-permute-done((bf16[128,3584]{1,0:T(8,128)(2,1)}, bf16[128,3584]{1,0:T(8,128)(2,1)S(1)}, u32[]{:S(2)}, u32[]{:S(2)}) %collective-permute-start.19) | collective-permute-done | bytes 917536 | tf_op jit(solution)/shard_map/ppermute | solution.py:63
  129.7 12.3 %collective-permute-done.21.refs_5_ = bf16[128,3584]{1,0:T(8,128)(2,1)S(1)} collective-permute-done((bf16[128,3584]{1,0:T(8,128)(2,1)}, bf16[128,3584]{1,0:T(8,128)(2,1)S(1)}, u32[]{:S(2)}, u32[]{:S(2)}) %collective-permute-start.21) | collective-permute-done | bytes 917536 | tf_op jit(solution)/shard_map/ppermute | solution.py:63
  142.0 3.5 %collective-permute-done.22.refs_6_ = bf16[128,3584]{1,0:T(8,128)(2,1)S(1)} collective-permute-done((bf16[128,3584]{1,0:T(8,128)(2,1)}, bf16[128,3584]{1,0:T(8,128)(2,1)S(1)}, u32[]{:S(2)}, u32[]{:S(2)}) %collective-permute-start.22) | collective-permute-done | bytes 917536 | tf_op jit(solution)/shard_map/ppermute | solution.py:63
  145.6 3.5 %shard_map.88 = (bf16[128,3584]{1,0:T(8,128)(2,1)S(1)}, bf16[128,3584]{1,0:T(8,128)(2,1)S(1)}, bf16[128,3584]{1,0:T(8,128)(2,1)S(1)}, bf16[128,3584]{1,0:T(8,128)(2,1)S(1)}) custom-call(s32[8]{0:T(128)S(1)} %copy-done.4, bf16[128,3584]{1,0:T(8,128)(2,1)S(1)} %get-tuple-element.77.refs_0_, bf16[128,3584]{1,0:T(8,128)(2,1)S(1)} %collective-permute-done.17.refs_1_, ...), custom_call_target="tpu_custom_call" | custom-call | flops 1879048192 | bytes 11010048 | tf_op jit(solution)/shard_map/pallas_call | solution.py:154
  149.1 2.1 %collective-permute-start.24 = (bf16[128,3584]{1,0:T(8,128)(2,1)S(1)}, bf16[128,3584]{1,0:T(8,128)(2,1)S(1)}, u32[]{:S(2)}, u32[]{:S(2)}) collective-permute-start(bf16[128,3584]{1,0:T(8,128)(2,1)S(1)} %get-tuple-element.87), channel_id=1, source_target_pairs={{8,0},{65,1},{10,2},{67,3},{12,4},{69,5},{14,6},{71,7},{16,8},{73,... | collective-permute-start | bytes 2752520 | tf_op jit(solution)/shard_map/ppermute | solution.py:63
  151.3 2.7 %collective-permute-start.28 = (bf16[32,3584]{1,0:T(8,128)(2,1)S(1)}, bf16[32,3584]{1,0:T(8,128)(2,1)S(1)}, u32[]{:S(2)}, u32[]{:S(2)}) collective-permute-start(bf16[32,3584]{1,0:T(8,128)(2,1)S(1)} %get-tuple-element.105), channel_id=1, source_target_pairs={{4,0},{5,1},{6,2},{7,3},{0,4},{1,5},{2,6},{3,7},{12,8},{13,9},{14,... | collective-permute-start | bytes 688136 | tf_op jit(solution)/shard_map/ppermute | solution.py:55
  154.4 2.2 %collective-permute-start.26 = (bf16[32,3584]{1,0:T(8,128)(2,1)S(1)}, bf16[32,3584]{1,0:T(8,128)(2,1)S(1)}, u32[]{:S(2)}, u32[]{:S(2)}) collective-permute-start(bf16[32,3584]{1,0:T(8,128)(2,1)S(1)} %get-tuple-element.107), channel_id=1, source_target_pairs={{2,0},{3,1},{4,2},{5,3},{6,4},{7,5},{0,6},{1,7},{10,8},{11,9},{12,... | collective-permute-start | bytes 688136 | tf_op jit(solution)/shard_map/ppermute | solution.py:55
  156.6 3.1 %collective-permute-done.28 = bf16[32,3584]{1,0:T(8,128)(2,1)S(1)} collective-permute-done((bf16[32,3584]{1,0:T(8,128)(2,1)S(1)}, bf16[32,3584]{1,0:T(8,128)(2,1)S(1)}, u32[]{:S(2)}, u32[]{:S(2)}) %collective-permute-start.28) | collective-permute-done | bytes 229408 | tf_op jit(solution)/shard_map/ppermute | solution.py:55
  159.7 5.6 %collective-permute-done.27 = bf16[32,3584]{1,0:T(8,128)(2,1)S(1)} collective-permute-done((bf16[32,3584]{1,0:T(8,128)(2,1)S(1)}, bf16[32,3584]{1,0:T(8,128)(2,1)S(1)}, u32[]{:S(2)}, u32[]{:S(2)}) %collective-permute-start.27) | collective-permute-done | bytes 229408 | tf_op jit(solution)/shard_map/ppermute | solution.py:55
  165.8 1.3 collective-permute-start.32
  167.2 1.3 collective-permute-start.31
  168.5 1.8 collective-permute-start.30
  170.2 0.9 collective-permute-start.29
  171.1 1.4 collective-permute-done.32
  172.6 2.2 %collective-permute-done.31 = bf16[32,3584]{1,0:T(8,128)(2,1)S(1)} collective-permute-done((bf16[32,3584]{1,0:T(8,128)(2,1)S(1)}, bf16[32,3584]{1,0:T(8,128)(2,1)S(1)}, u32[]{:S(2)}, u32[]{:S(2)}) %collective-permute-start.31) | collective-permute-done | bytes 229408 | tf_op jit(solution)/shard_map/ppermute | solution.py:55
  174.8 6.4 %collective-permute-done.30 = bf16[32,3584]{1,0:T(8,128)(2,1)S(1)} collective-permute-done((bf16[32,3584]{1,0:T(8,128)(2,1)S(1)}, bf16[32,3584]{1,0:T(8,128)(2,1)S(1)}, u32[]{:S(2)}, u32[]{:S(2)}) %collective-permute-start.30) | collective-permute-done | bytes 229408 | tf_op jit(solution)/shard_map/ppermute | solution.py:55
  182.0 1.0 collective-permute-done.33
  (61 shorter events, 11.0 us)
Async XLA Ops:
  0.8 88.8 %copy-start.3 = (s32[8]{0:T(128)}, s32[8]{0:T(128)S(1)}, u32[]{:S(2)}) copy-start(s32[8]{0:T(128)S(1)} %concatenate.21.info) | copy-start | bytes 100
  0.8 0.9 copy-start.2
  1.7 0.7 copy-start.5
  2.4 0.7 copy-start.6
  3.1 0.7 copy-start.7
  4.5 2.4 %collective-permute-start = (bf16[16,3712]{1,0:T(8,128)(2,1)S(1)}, bf16[16,3712]{1,0:T(8,128)(2,1)S(1)}, u32[]{:S(2)}, u32[]{:S(2)}) collective-permute-start(bf16[16,3712]{1,0:T(8,128)(2,1)S(1)} %get-tuple-element.54), channel_id=1, source_target_pairs={{0,1},{1,0},{2,3},{3,2},{4,5},{5,4},{6,7},{7,6},{8,9},{9,8},{10,11... | collective-permute-start | bytes 356360 | tf_op jit(solution)/shard_map/ppermute | solution.py:59
  7.0 7.3 %collective-permute-start.4 = (bf16[32,3712]{1,0:T(8,128)(2,1)S(1)}, bf16[32,3712]{1,0:T(8,128)(2,1)S(1)}, u32[]{:S(2)}, u32[]{:S(2)}) collective-permute-start(bf16[32,3712]{1,0:T(8,128)(2,1)S(1)} %maximum_select_fusion), channel_id=1, source_target_pairs={{0,16},{1,33},{2,18},{3,35},{4,20},{5,37},{6,22},{7,39},{8,24},{9,... | collective-permute-start | bytes 712712 | tf_op jit(solution)/shard_map/ppermute | solution.py:406
  9.9 7.3 %collective-permute-start.3 = (bf16[32,3712]{1,0:T(8,128)(2,1)S(1)}, bf16[32,3712]{1,0:T(8,128)(2,1)S(1)}, u32[]{:S(2)}, u32[]{:S(2)}) collective-permute-start(bf16[32,3712]{1,0:T(8,128)(2,1)S(1)} %maximum_select_fusion), channel_id=1, source_target_pairs={{0,4},{1,5},{2,6},{3,7},{4,0},{5,1},{6,2},{7,3},{8,12},{9,13},{10,... | collective-permute-start | bytes 712712 | tf_op jit(solution)/shard_map/ppermute | solution.py:51
  12.8 10.7 %collective-permute-start.2 = (bf16[32,3712]{1,0:T(8,128)(2,1)S(1)}, bf16[32,3712]{1,0:T(8,128)(2,1)S(1)}, u32[]{:S(2)}, u32[]{:S(2)}) collective-permute-start(bf16[32,3712]{1,0:T(8,128)(2,1)S(1)} %maximum_select_fusion), channel_id=1, source_target_pairs={{0,6},{1,7},{2,0},{3,1},{4,2},{5,3},{6,4},{7,5},{8,14},{9,15},{10,... | collective-permute-start | bytes 712712 | tf_op jit(solution)/shard_map/ppermute | solution.py:51
  13.6 9.9 %collective-permute-start.1 = (bf16[32,3712]{1,0:T(8,128)(2,1)S(1)}, bf16[32,3712]{1,0:T(8,128)(2,1)S(1)}, u32[]{:S(2)}, u32[]{:S(2)}) collective-permute-start(bf16[32,3712]{1,0:T(8,128)(2,1)S(1)} %maximum_select_fusion), channel_id=1, source_target_pairs={{0,2},{1,3},{2,4},{3,5},{4,6},{5,7},{6,0},{7,1},{8,10},{9,11},{10,... | collective-permute-start | bytes 712712 | tf_op jit(solution)/shard_map/ppermute | solution.py:51
  23.6 15.8 %collective-permute-start.6 = (bf16[128,3712]{1,0:T(8,128)(2,1)S(1)}, bf16[128,3712]{1,0:T(8,128)(2,1)S(1)}, u32[]{:S(2)}, u32[]{:S(2)}) collective-permute-start(bf16[128,3712]{1,0:T(8,128)(2,1)S(1)} %constant_dynamic-update-slice_fusion.refs_0_.refs_8_), channel_id=1, source_target_pairs={{0,24},{1,97},{2,26},{3,99},{4,28},{5,101},{6,30},{7,103},{8,0},{9... | collective-permute-start | bytes 2850824 | tf_op jit(solution)/shard_map/ppermute | solution.py:63
  24.3 15.2 %collective-permute-start.5 = (bf16[128,3712]{1,0:T(8,128)(2,1)S(1)}, bf16[128,3712]{1,0:T(8,128)(2,1)S(1)}, u32[]{:S(2)}, u32[]{:S(2)}) collective-permute-start(bf16[128,3712]{1,0:T(8,128)(2,1)S(1)} %constant_dynamic-update-slice_fusion.refs_0_.refs_8_), channel_id=1, source_target_pairs={{0,8},{1,65},{2,10},{3,67},{4,12},{5,69},{6,14},{7,71},{8,16},{9,7... | collective-permute-start | bytes 2850824 | tf_op jit(solution)/shard_map/ppermute | solution.py:63
  25.1 7.9 %collective-permute-start.9 = (bf16[32,3712]{1,0:T(8,128)(2,1)S(1)}, bf16[32,3712]{1,0:T(8,128)(2,1)S(1)}, u32[]{:S(2)}, u32[]{:S(2)}) collective-permute-start(bf16[32,3712]{1,0:T(8,128)(2,1)S(1)} %collective-permute-done.4), channel_id=1, source_target_pairs={{0,4},{1,5},{2,6},{3,7},{4,0},{5,1},{6,2},{7,3},{8,12},{9,13},{10,... | collective-permute-start | bytes 712712 | tf_op jit(solution)/shard_map/ppermute | solution.py:51
  28.7 10.7 %collective-permute-start.8 = (bf16[32,3712]{1,0:T(8,128)(2,1)S(1)}, bf16[32,3712]{1,0:T(8,128)(2,1)S(1)}, u32[]{:S(2)}, u32[]{:S(2)}) collective-permute-start(bf16[32,3712]{1,0:T(8,128)(2,1)S(1)} %collective-permute-done.4), channel_id=1, source_target_pairs={{0,6},{1,7},{2,0},{3,1},{4,2},{5,3},{6,4},{7,5},{8,14},{9,15},{10,... | collective-permute-start | bytes 712712 | tf_op jit(solution)/shard_map/ppermute | solution.py:51
  29.5 9.9 %collective-permute-start.7 = (bf16[32,3712]{1,0:T(8,128)(2,1)S(1)}, bf16[32,3712]{1,0:T(8,128)(2,1)S(1)}, u32[]{:S(2)}, u32[]{:S(2)}) collective-permute-start(bf16[32,3712]{1,0:T(8,128)(2,1)S(1)} %collective-permute-done.4), channel_id=1, source_target_pairs={{0,2},{1,3},{2,4},{3,5},{4,6},{5,7},{6,0},{7,1},{8,10},{9,11},{10,... | collective-permute-start | bytes 712712 | tf_op jit(solution)/shard_map/ppermute | solution.py:51
  39.5 31.5 %copy-start = (bf16[1,7168,512]{2,1,0:T(8,128)(2,1)S(1)}, bf16[1,7168,512]{2,1,0:T(8,128)(2,1)}, u32[]{:S(2)}) copy-start(bf16[1,7168,512]{2,1,0:T(8,128)(2,1)} %param.12) | copy-start | bytes 22020100
  41.8 15.0 %collective-permute-start.10 = (bf16[128,3584]{1,0:T(8,128)(2,1)S(1)}, bf16[128,3584]{1,0:T(8,128)(2,1)S(1)}, u32[]{:S(2)}, u32[]{:S(2)}) collective-permute-start(bf16[128,3584]{1,0:T(8,128)(2,1)S(1)} %get-tuple-element.67), channel_id=1, source_target_pairs={{0,64},{1,9},{2,66},{3,11},{4,68},{5,13},{6,70},{7,15},{8,72},{9,1... | collective-permute-start | bytes 2752520 | tf_op jit(solution)/shard_map/ppermute | solution.py:63
  43.5 22.5 %collective-permute-start.11 = (bf16[128,3584]{1,0:T(8,128)(2,1)S(1)}, bf16[128,3584]{1,0:T(8,128)(2,1)S(1)}, u32[]{:S(2)}, u32[]{:S(2)}) collective-permute-start(bf16[128,3584]{1,0:T(8,128)(2,1)S(1)} %get-tuple-element.68), channel_id=1, source_target_pairs={{0,96},{1,25},{2,98},{3,27},{4,100},{5,29},{6,102},{7,31},{8,104},... | collective-permute-start | bytes 2752520 | tf_op jit(solution)/shard_map/ppermute | solution.py:63
  45.8 25.2 %collective-permute-start.12 = (bf16[128,3584]{1,0:T(8,128)(2,1)S(1)}, bf16[128,3584]{1,0:T(8,128)(2,1)S(1)}, u32[]{:S(2)}, u32[]{:S(2)}) collective-permute-start(bf16[128,3584]{1,0:T(8,128)(2,1)S(1)} %get-tuple-element.69), channel_id=1, source_target_pairs={{0,32},{1,17},{2,34},{3,19},{4,36},{5,21},{6,38},{7,23},{8,40},{9,... | collective-permute-start | bytes 2752520 | tf_op jit(solution)/shard_map/ppermute | solution.py:63
  50.6 27.8 %collective-permute-start.13 = (bf16[128,3584]{1,0:T(8,128)(2,1)}, bf16[128,3584]{1,0:T(8,128)(2,1)S(1)}, u32[]{:S(2)}, u32[]{:S(2)}) collective-permute-start(bf16[128,3584]{1,0:T(8,128)(2,1)} %get-tuple-element.73), channel_id=1, source_target_pairs={{0,1},{1,0},{2,3},{3,2},{4,5},{5,4},{6,7},{7,6},{8,9},{9,8},{10,11... | collective-permute-start | bytes 2752520 | tf_op jit(solution)/shard_map/ppermute | solution.py:59
  52.7 25.9 %collective-permute-start.14 = (bf16[128,3584]{1,0:T(8,128)(2,1)}, bf16[128,3584]{1,0:T(8,128)(2,1)S(1)}, u32[]{:S(2)}, u32[]{:S(2)}) collective-permute-start(bf16[128,3584]{1,0:T(8,128)(2,1)} %get-tuple-element.74), channel_id=1, source_target_pairs={{0,65},{1,8},{2,67},{3,10},{4,69},{5,12},{6,71},{7,14},{8,73},{9,1... | collective-permute-start | bytes 2752520 | tf_op jit(solution)/shard_map/ppermute | solution.py:63
  56.8 22.4 %collective-permute-start.15 = (bf16[128,3584]{1,0:T(8,128)(2,1)S(1)}, bf16[128,3584]{1,0:T(8,128)(2,1)S(1)}, u32[]{:S(2)}, u32[]{:S(2)}) collective-permute-start(bf16[128,3584]{1,0:T(8,128)(2,1)S(1)} %get-tuple-element.75), channel_id=1, source_target_pairs={{0,97},{1,24},{2,99},{3,26},{4,101},{5,28},{6,103},{7,30},{8,105},... | collective-permute-start | bytes 2752520 | tf_op jit(solution)/shard_map/ppermute | solution.py:63
  66.0 23.6 %collective-permute-start.16 = (bf16[128,3584]{1,0:T(8,128)(2,1)S(1)}, bf16[128,3584]{1,0:T(8,128)(2,1)}, u32[]{:S(2)}, u32[]{:S(2)}) collective-permute-start(bf16[128,3584]{1,0:T(8,128)(2,1)S(1)} %get-tuple-element.76), channel_id=1, source_target_pairs={{0,33},{1,16},{2,35},{3,18},{4,37},{5,20},{6,39},{7,22},{8,41},{9,... | collective-permute-start | bytes 2752520 | tf_op jit(solution)/shard_map/ppermute | solution.py:63
  99.8 0.8 copy-start.1
  100.6 14.8 %collective-permute-start.17 = (bf16[128,3584]{1,0:T(8,128)(2,1)}, bf16[128,3584]{1,0:T(8,128)(2,1)S(1)}, u32[]{:S(2)}, u32[]{:S(2)}) collective-permute-start(bf16[128,3584]{1,0:T(8,128)(2,1)} %get-tuple-element.78), channel_id=1, source_target_pairs={{64,0},{9,1},{66,2},{11,3},{68,4},{13,5},{70,6},{15,7},{72,8},{17,... | collective-permute-start | bytes 2752520 | tf_op jit(solution)/shard_map/ppermute | solution.py:63
  102.4 25.1 %collective-permute-start.18 = (bf16[128,3584]{1,0:T(8,128)(2,1)}, bf16[128,3584]{1,0:T(8,128)(2,1)S(1)}, u32[]{:S(2)}, u32[]{:S(2)}) collective-permute-start(bf16[128,3584]{1,0:T(8,128)(2,1)} %get-tuple-element.79), channel_id=1, source_target_pairs={{96,0},{25,1},{98,2},{27,3},{100,4},{29,5},{102,6},{31,7},{104,8},... | collective-permute-start | bytes 2752520 | tf_op jit(solution)/shard_map/ppermute | solution.py:63
  102.4 27.3 %collective-permute-start.19 = (bf16[128,3584]{1,0:T(8,128)(2,1)}, bf16[128,3584]{1,0:T(8,128)(2,1)S(1)}, u32[]{:S(2)}, u32[]{:S(2)}) collective-permute-start(bf16[128,3584]{1,0:T(8,128)(2,1)} %get-tuple-element.80), channel_id=1, source_target_pairs={{32,0},{17,1},{34,2},{19,3},{36,4},{21,5},{38,6},{23,7},{40,8},{25... | collective-permute-start | bytes 2752520 | tf_op jit(solution)/shard_map/ppermute | solution.py:63
  103.6 42.0 %copy-start.4 = (s32[8]{0:T(128)S(1)}, s32[8]{0:T(128)}, u32[]{:S(2)}) copy-start(s32[8]{0:T(128)} %copy-done.3) | copy-start | bytes 100
  110.4 19.3 %collective-permute-start.20 = (bf16[128,3584]{1,0:T(8,128)(2,1)}, bf16[128,3584]{1,0:T(8,128)(2,1)S(1)}, u32[]{:S(2)}, u32[]{:S(2)}) collective-permute-start(bf16[128,3584]{1,0:T(8,128)(2,1)} %get-tuple-element.82), channel_id=1, source_target_pairs={{0,1},{1,0},{2,3},{3,2},{4,5},{5,4},{6,7},{7,6},{8,9},{9,8},{10,11... | collective-permute-start | bytes 2752520 | tf_op jit(solution)/shard_map/ppermute | solution.py:59
  110.5 31.5 %collective-permute-start.21 = (bf16[128,3584]{1,0:T(8,128)(2,1)}, bf16[128,3584]{1,0:T(8,128)(2,1)S(1)}, u32[]{:S(2)}, u32[]{:S(2)}) collective-permute-start(bf16[128,3584]{1,0:T(8,128)(2,1)} %get-tuple-element.83), channel_id=1, source_target_pairs={{65,0},{8,1},{67,2},{10,3},{69,4},{12,5},{71,6},{14,7},{73,8},{16,... | collective-permute-start | bytes 2752520 | tf_op jit(solution)/shard_map/ppermute | solution.py:63
  115.4 30.1 %collective-permute-start.22 = (bf16[128,3584]{1,0:T(8,128)(2,1)}, bf16[128,3584]{1,0:T(8,128)(2,1)S(1)}, u32[]{:S(2)}, u32[]{:S(2)}) collective-permute-start(bf16[128,3584]{1,0:T(8,128)(2,1)} %get-tuple-element.84), channel_id=1, source_target_pairs={{97,0},{24,1},{99,2},{26,3},{101,4},{28,5},{103,6},{30,7},{105,8},... | collective-permute-start | bytes 2752520 | tf_op jit(solution)/shard_map/ppermute | solution.py:63
  127.5 18.0 %collective-permute-start.23 = (bf16[128,3584]{1,0:T(8,128)(2,1)}, bf16[128,3584]{1,0:T(8,128)(2,1)S(1)}, u32[]{:S(2)}, u32[]{:S(2)}) collective-permute-start(bf16[128,3584]{1,0:T(8,128)(2,1)} %get-tuple-element.85), channel_id=1, source_target_pairs={{33,0},{16,1},{35,2},{18,3},{37,4},{20,5},{39,6},{22,7},{41,8},{24... | collective-permute-start | bytes 2752520 | tf_op jit(solution)/shard_map/ppermute | solution.py:63
  149.1 16.2 %collective-permute-start.24 = (bf16[128,3584]{1,0:T(8,128)(2,1)S(1)}, bf16[128,3584]{1,0:T(8,128)(2,1)S(1)}, u32[]{:S(2)}, u32[]{:S(2)}) collective-permute-start(bf16[128,3584]{1,0:T(8,128)(2,1)S(1)} %get-tuple-element.87), channel_id=1, source_target_pairs={{8,0},{65,1},{10,2},{67,3},{12,4},{69,5},{14,6},{71,7},{16,8},{73,... | collective-permute-start | bytes 2752520 | tf_op jit(solution)/shard_map/ppermute | solution.py:63
  151.2 14.1 %collective-permute-start.25 = (bf16[128,3584]{1,0:T(8,128)(2,1)S(1)}, bf16[128,3584]{1,0:T(8,128)(2,1)S(1)}, u32[]{:S(2)}, u32[]{:S(2)}) collective-permute-start(bf16[128,3584]{1,0:T(8,128)(2,1)S(1)} %get-tuple-element.88), channel_id=1, source_target_pairs={{24,0},{97,1},{26,2},{99,3},{28,4},{101,5},{30,6},{103,7},{0,8},{1... | collective-permute-start | bytes 2752520 | tf_op jit(solution)/shard_map/ppermute | solution.py:63
  151.3 8.4 %collective-permute-start.28 = (bf16[32,3584]{1,0:T(8,128)(2,1)S(1)}, bf16[32,3584]{1,0:T(8,128)(2,1)S(1)}, u32[]{:S(2)}, u32[]{:S(2)}) collective-permute-start(bf16[32,3584]{1,0:T(8,128)(2,1)S(1)} %get-tuple-element.105), channel_id=1, source_target_pairs={{4,0},{5,1},{6,2},{7,3},{0,4},{1,5},{2,6},{3,7},{12,8},{13,9},{14,... | collective-permute-start | bytes 688136 | tf_op jit(solution)/shard_map/ppermute | solution.py:55
  153.9 11.4 %collective-permute-start.27 = (bf16[32,3584]{1,0:T(8,128)(2,1)S(1)}, bf16[32,3584]{1,0:T(8,128)(2,1)S(1)}, u32[]{:S(2)}, u32[]{:S(2)}) collective-permute-start(bf16[32,3584]{1,0:T(8,128)(2,1)S(1)} %get-tuple-element.106), channel_id=1, source_target_pairs={{6,0},{7,1},{0,2},{1,3},{2,4},{3,5},{4,6},{5,7},{14,8},{15,9},{8,1... | collective-permute-start | bytes 688136 | tf_op jit(solution)/shard_map/ppermute | solution.py:55
  154.4 10.9 %collective-permute-start.26 = (bf16[32,3584]{1,0:T(8,128)(2,1)S(1)}, bf16[32,3584]{1,0:T(8,128)(2,1)S(1)}, u32[]{:S(2)}, u32[]{:S(2)}) collective-permute-start(bf16[32,3584]{1,0:T(8,128)(2,1)S(1)} %get-tuple-element.107), channel_id=1, source_target_pairs={{2,0},{3,1},{4,2},{5,3},{6,4},{7,5},{0,6},{1,7},{10,8},{11,9},{12,... | collective-permute-start | bytes 688136 | tf_op jit(solution)/shard_map/ppermute | solution.py:55
  165.8 6.8 %collective-permute-start.32 = (bf16[32,3584]{1,0:T(8,128)(2,1)S(1)}, bf16[32,3584]{1,0:T(8,128)(2,1)S(1)}, u32[]{:S(2)}, u32[]{:S(2)}) collective-permute-start(bf16[32,3584]{1,0:T(8,128)(2,1)S(1)} %add_convert_fusion.2), channel_id=1, source_target_pairs={{16,0},{33,1},{18,2},{35,3},{20,4},{37,5},{22,6},{39,7},{24,8},{41... | collective-permute-start | bytes 688136 | tf_op jit(solution)/shard_map/ppermute | solution.py:424
  167.2 7.6 %collective-permute-start.31 = (bf16[32,3584]{1,0:T(8,128)(2,1)S(1)}, bf16[32,3584]{1,0:T(8,128)(2,1)S(1)}, u32[]{:S(2)}, u32[]{:S(2)}) collective-permute-start(bf16[32,3584]{1,0:T(8,128)(2,1)S(1)} %get-tuple-element.101), channel_id=1, source_target_pairs={{4,0},{5,1},{6,2},{7,3},{0,4},{1,5},{2,6},{3,7},{12,8},{13,9},{14,... | collective-permute-start | bytes 688136 | tf_op jit(solution)/shard_map/ppermute | solution.py:55
  168.5 12.7 %collective-permute-start.30 = (bf16[32,3584]{1,0:T(8,128)(2,1)S(1)}, bf16[32,3584]{1,0:T(8,128)(2,1)S(1)}, u32[]{:S(2)}, u32[]{:S(2)}) collective-permute-start(bf16[32,3584]{1,0:T(8,128)(2,1)S(1)} %get-tuple-element.102), channel_id=1, source_target_pairs={{6,0},{7,1},{0,2},{1,3},{2,4},{3,5},{4,6},{5,7},{14,8},{15,9},{8,1... | collective-permute-start | bytes 688136 | tf_op jit(solution)/shard_map/ppermute | solution.py:55
  170.2 10.9 %collective-permute-start.29 = (bf16[32,3584]{1,0:T(8,128)(2,1)S(1)}, bf16[32,3584]{1,0:T(8,128)(2,1)S(1)}, u32[]{:S(2)}, u32[]{:S(2)}) collective-permute-start(bf16[32,3584]{1,0:T(8,128)(2,1)S(1)} %get-tuple-element.103), channel_id=1, source_target_pairs={{2,0},{3,1},{4,2},{5,3},{6,4},{7,5},{0,6},{1,7},{10,8},{11,9},{12,... | collective-permute-start | bytes 688136 | tf_op jit(solution)/shard_map/ppermute | solution.py:55
  181.3 1.7 collective-permute-start.33

commit v3 on v2

--- a/solution.py
+++ b/solution.py
@@ -403,7 +403,7 @@
     mine, theirs = begin(info, pairs, tokens, picks, mix_weights)
     theirs = other_core(theirs)
     pool = jnp.where(first, jnp.concatenate([mine, theirs]), jnp.concatenate([theirs, mine]))
-    line, part = together(gathered(pool, ROUTE[0]), lax.ppermute(pool, ALL_AXES, ring_perm(ROUTE[1], SHIFTS[3])))
+    part, line = together(lax.ppermute(pool, ALL_AXES, ring_perm(ROUTE[1], SHIFTS[3])), gathered(pool, ROUTE[0]))
     line = jnp.concatenate(line, axis=0)
     ahead, part = together(hop([line] * RING, ROUTE[1], ring_perm, (1, 2)), gathered(part, ROUTE[0]))
     pool = [line] + ahead + [jnp.concatenate(part, axis=0)]
@@ -420,8 +420,8 @@
     sums = combine(info, own + far, pool)
     ahead, part = together(hop(sums, ROUTE[1], back_perm, (1, 2)), scattered(split_rows(sums[3]), ROUTE[0]))
     line, part = summed(sums[:1] + ahead), summed(part)
-    line, part = together(
-        scattered(split_rows(line), ROUTE[0]), lax.ppermute(part, ALL_AXES, back_perm(ROUTE[1], SHIFTS[3])))
+    part, line = together(
+        lax.ppermute(part, ALL_AXES, back_perm(ROUTE[1], SHIFTS[3])), scattered(split_rows(line), ROUTE[0]))
     done = summed(line + [part])
     own = jnp.where(first, done[:tok_rows], done[tok_rows:])
     rest = other_core(jnp.where(first, done[tok_rows:], done[:tok_rows]))

time: 184 us -> 182 us (0.989)
  waiting for transfers between devices: 90.4 us -> 84.6 us
  starting transfers between devices: 52.5 us -> 56.3 us
    ppermute x6, waiting for transfers between devices: 18.5 us -> 15.9 us  [gathered(): lax.ppermute(value, ALL_AXES, ring_perm(axes, s))]
    ppermute x16, starting transfers between devices: 25.1 us -> 27.4 us  [hop(): lax.ppermute(blocks[r], ALL_AXES, perm(axes, SHIFTS[r], cross))]
  transfers between devices with their start and end apart: 34 -> 34, of which waited for: 21 -> 23; matrix products, arithmetic and copies ran while one was open for 0% -> 0% of each run, Pallas kernels for 10% -> 10%
where the time goes in v3:
time: 182 us
  waiting for transfers between devices  84.6 us (46%)
  starting transfers between devices  56.3 us (31%)
  Pallas kernels  34.4 us (19%)
  local copies, waits for them, and re-layouts  4.18 us (2%)
  other arithmetic  2.08 us (1%)
    ppermute x16, waiting for transfers between devices, hop(): lax.ppermute(blocks[r], ALL_AXES, perm(axes, SHIFTS[r], cross))  50.2 us
    ppermute x16, starting transfers between devices, hop(): lax.ppermute(blocks[r], ALL_AXES, perm(axes, SHIFTS[r], cross))  27.4 us
    ppermute x6, waiting for transfers between devices, scattered(): lax.ppermute(b, ALL_AXES, back_perm(axes, s))  16.5 us
    ppermute x6, waiting for transfers between devices, gathered(): lax.ppermute(value, ALL_AXES, ring_perm(axes, s))  15.9 us
    ppermute x6, starting transfers between devices, scattered(): lax.ppermute(b, ALL_AXES, back_perm(axes, s))  10.5 us
    pallas_call x1, Pallas kernels, expert(): pl.pallas_call(expert_kernel, out_shape=[jax.ShapeDtypeStruct((BLOCK, HAL...  10.2 us
    ppermute x6, starting transfers between devices, gathered(): lax.ppermute(value, ALL_AXES, ring_perm(axes, s))  9.06 us
    pallas_call x1, Pallas kernels, project(): pl.pallas_call(project_kernel, out_shape=[jax.ShapeDtypeStruct((rows, 2 *...  7.33 us
  transfers between devices with their start and end apart: 34, of which 23 were waited for; matrix products, arithmetic and copies ran while one was open for 0% of the time, Pallas kernels for 10%

profile of v3, /device:TPU:1, one launch (start us, length us, event | category | flops | bytes accessed | tf_op | source)
XLA Modules:
  0.0 181.6 jit_solution(18047761068135495226)
XLA Ops:
  0.8 0.9 copy-done.2
  3.8 0.8 shard_map.82
  4.5 1.4 collective-permute-start
  5.9 1.0 collective-permute-done
  7.0 3.1 %collective-permute-start.4 = (bf16[32,3712]{1,0:T(8,128)(2,1)S(1)}, bf16[32,3712]{1,0:T(8,128)(2,1)S(1)}, u32[]{:S(2)}, u32[]{:S(2)}) collective-permute-start(bf16[32,3712]{1,0:T(8,128)(2,1)S(1)} %maximum_select_fusion), channel_id=1, source_target_pairs={{0,4},{1,5},{2,6},{3,7},{4,0},{5,1},{6,2},{7,3},{8,12},{9,13},{10,... | collective-permute-start | bytes 712712 | tf_op jit(solution)/shard_map/ppermute | solution.py:51
  10.0 0.8 collective-permute-start.3
  11.5 2.7 %collective-permute-start.1 = (bf16[32,3712]{1,0:T(8,128)(2,1)S(1)}, bf16[32,3712]{1,0:T(8,128)(2,1)S(1)}, u32[]{:S(2)}, u32[]{:S(2)}) collective-permute-start(bf16[32,3712]{1,0:T(8,128)(2,1)S(1)} %maximum_select_fusion), channel_id=1, source_target_pairs={{0,16},{1,33},{2,18},{3,35},{4,20},{5,37},{6,22},{7,39},{8,24},{9,... | collective-permute-start | bytes 712712 | tf_op jit(solution)/shard_map/ppermute | solution.py:406
  14.2 1.4 collective-permute-done.4
  15.6 5.5 %collective-permute-done.3 = bf16[32,3712]{1,0:T(8,128)(2,1)S(1)} collective-permute-done((bf16[32,3712]{1,0:T(8,128)(2,1)S(1)}, bf16[32,3712]{1,0:T(8,128)(2,1)S(1)}, u32[]{:S(2)}, u32[]{:S(2)}) %collective-permute-start.3) | collective-permute-done | bytes 237600 | tf_op jit(solution)/shard_map/ppermute | solution.py:51
  21.3 2.6 %collective-permute-start.6 = (bf16[128,3712]{1,0:T(8,128)(2,1)S(1)}, bf16[128,3712]{1,0:T(8,128)(2,1)S(1)}, u32[]{:S(2)}, u32[]{:S(2)}) collective-permute-start(bf16[128,3712]{1,0:T(8,128)(2,1)S(1)} %constant_dynamic-update-slice_fusion.refs_0_.refs_8_), channel_id=1, source_target_pairs={{0,24},{1,97},{2,26},{3,99},{4,28},{5,101},{6,30},{7,103},{8,0},{9... | collective-permute-start | bytes 2850824 | tf_op jit(solution)/shard_map/ppermute | solution.py:63
  23.9 3.1 %collective-permute-start.9 = (bf16[32,3712]{1,0:T(8,128)(2,1)S(1)}, bf16[32,3712]{1,0:T(8,128)(2,1)S(1)}, u32[]{:S(2)}, u32[]{:S(2)}) collective-permute-start(bf16[32,3712]{1,0:T(8,128)(2,1)S(1)} %collective-permute-done.1), channel_id=1, source_target_pairs={{0,4},{1,5},{2,6},{3,7},{4,0},{5,1},{6,2},{7,3},{8,12},{9,13},{10,... | collective-permute-start | bytes 712712 | tf_op jit(solution)/shard_map/ppermute | solution.py:51
  27.0 0.8 collective-permute-start.8
  28.5 2.0 %collective-permute-done.9 = bf16[32,3712]{1,0:T(8,128)(2,1)S(1)} collective-permute-done((bf16[32,3712]{1,0:T(8,128)(2,1)S(1)}, bf16[32,3712]{1,0:T(8,128)(2,1)S(1)}, u32[]{:S(2)}, u32[]{:S(2)}) %collective-permute-start.9) | collective-permute-done | bytes 237600 | tf_op jit(solution)/shard_map/ppermute | solution.py:51
  30.5 6.7 %collective-permute-done.8 = bf16[32,3712]{1,0:T(8,128)(2,1)S(1)} collective-permute-done((bf16[32,3712]{1,0:T(8,128)(2,1)S(1)}, bf16[32,3712]{1,0:T(8,128)(2,1)S(1)}, u32[]{:S(2)}, u32[]{:S(2)}) %collective-permute-start.8) | collective-permute-done | bytes 237600 | tf_op jit(solution)/shard_map/ppermute | solution.py:51
  38.2 2.2 %shard_map.83 = (bf16[128,3584]{1,0:T(8,128)(2,1)S(1)}, bf16[128,3584]{1,0:T(8,128)(2,1)S(1)}, bf16[128,3584]{1,0:T(8,128)(2,1)S(1)}, bf16[128,3584]{1,0:T(8,128)(2,1)S(1)}) custom-call(s32[8]{0:T(128)S(1)} %concatenate.21.info, bf16[128,3712]{1,0:T(8,128)(2,1)S(1)} %constant_dynamic-update-slice_fusion.refs_0_.refs_8_, ...), custom_call_target="tpu_custom_call" | custom-call | flops 469762048 | bytes 7340032 | tf_op jit(solution)/shard_map/pallas_call | solution.py:121
  40.4 2.1 %collective-permute-start.10 = (bf16[128,3584]{1,0:T(8,128)(2,1)S(1)}, bf16[128,3584]{1,0:T(8,128)(2,1)S(1)}, u32[]{:S(2)}, u32[]{:S(2)}) collective-permute-start(bf16[128,3584]{1,0:T(8,128)(2,1)S(1)} %get-tuple-element.67), channel_id=1, source_target_pairs={{0,64},{1,9},{2,66},{3,11},{4,68},{5,13},{6,70},{7,15},{8,72},{9,1... | collective-permute-start | bytes 2752520 | tf_op jit(solution)/shard_map/ppermute | solution.py:63
  42.5 1.8 collective-permute-start.11
  44.3 1.6 collective-permute-start.12
  46.0 3.5 %shard_map.85 = (bf16[128,3584]{1,0:T(8,128)(2,1)}, bf16[128,3584]{1,0:T(8,128)(2,1)}, bf16[128,3584]{1,0:T(8,128)(2,1)S(1)}, bf16[128,3584]{1,0:T(8,128)(2,1)S(1)}) custom-call(s32[8]{0:T(128)S(1)} %concatenate.21.info, bf16[128,3712]{1,0:T(8,128)(2,1)S(1)} %constant_dynamic-update-slice_fusion.refs_0_.refs_8_, ...), custom_call_target="tpu_custom_call" | custom-call | flops 469762048 | bytes 7340032 | tf_op jit(solution)/shard_map/pallas_call | solution.py:121
  49.4 3.0 %collective-permute-start.13 = (bf16[128,3584]{1,0:T(8,128)(2,1)}, bf16[128,3584]{1,0:T(8,128)(2,1)S(1)}, u32[]{:S(2)}, u32[]{:S(2)}) collective-permute-start(bf16[128,3584]{1,0:T(8,128)(2,1)} %get-tuple-element.73), channel_id=1, source_target_pairs={{0,1},{1,0},{2,3},{3,2},{4,5},{5,4},{6,7},{7,6},{8,9},{9,8},{10,11... | collective-permute-start | bytes 2752520 | tf_op jit(solution)/shard_map/ppermute | solution.py:59
  52.5 2.9 %collective-permute-done.10.refs_1_ = bf16[128,3584]{1,0:T(8,128)(2,1)S(1)} collective-permute-done((bf16[128,3584]{1,0:T(8,128)(2,1)S(1)}, bf16[128,3584]{1,0:T(8,128)(2,1)S(1)}, u32[]{:S(2)}, u32[]{:S(2)}) %collective-permute-start.10) | collective-permute-done | bytes 917536 | tf_op jit(solution)/shard_map/ppermute | solution.py:63
  55.3 4.7 %collective-permute-start.15 = (bf16[128,3584]{1,0:T(8,128)(2,1)S(1)}, bf16[128,3584]{1,0:T(8,128)(2,1)S(1)}, u32[]{:S(2)}, u32[]{:S(2)}) collective-permute-start(bf16[128,3584]{1,0:T(8,128)(2,1)S(1)} %get-tuple-element.75), channel_id=1, source_target_pairs={{0,97},{1,24},{2,99},{3,26},{4,101},{5,28},{6,103},{7,30},{8,105},... | collective-permute-start | bytes 2752520 | tf_op jit(solution)/shard_map/ppermute | solution.py:63
  60.0 4.5 %collective-permute-done.11.refs_2_ = bf16[128,3584]{1,0:T(8,128)(2,1)S(1)} collective-permute-done((bf16[128,3584]{1,0:T(8,128)(2,1)S(1)}, bf16[128,3584]{1,0:T(8,128)(2,1)S(1)}, u32[]{:S(2)}, u32[]{:S(2)}) %collective-permute-start.11) | collective-permute-done | bytes 917536 | tf_op jit(solution)/shard_map/ppermute | solution.py:63
  64.5 5.5 %collective-permute-start.16 = (bf16[128,3584]{1,0:T(8,128)(2,1)S(1)}, bf16[128,3584]{1,0:T(8,128)(2,1)}, u32[]{:S(2)}, u32[]{:S(2)}) collective-permute-start(bf16[128,3584]{1,0:T(8,128)(2,1)S(1)} %get-tuple-element.76), channel_id=1, source_target_pairs={{0,33},{1,16},{2,35},{3,18},{4,37},{5,20},{6,39},{7,22},{8,41},{9,... | collective-permute-start | bytes 2752520 | tf_op jit(solution)/shard_map/ppermute | solution.py:63
  69.9 7.3 %shard_map.84 = (f32[512,1024]{1,0:T(8,128)S(1)}, bf16[3584,1024]{1,0:T(8,128)(2,1)S(1)}, bf16[512,3584]{1,0:T(8,128)(2,1)S(1)}) custom-call(s32[8]{0:T(128)S(1)} %concatenate.21.info, bf16[128,3584]{1,0:T(8,128)(2,1)S(1)} %get-tuple-element.66.refs_0_, bf16[128,3584]{1,0:T(8,128)(2,1)S(1)} %collective-permute-done.10.refs_1_, ...), custom_call_target="tpu_custom_call" | custom-call | flops 3758096384 | bytes 22020096 | tf_op jit(solution)/shard_map/pallas_call | solution.py:261
  78.2 10.3 %collective-permute-done.16.refs_3_ = bf16[128,3584]{1,0:T(8,128)(2,1)} collective-permute-done((bf16[128,3584]{1,0:T(8,128)(2,1)S(1)}, bf16[128,3584]{1,0:T(8,128)(2,1)}, u32[]{:S(2)}, u32[]{:S(2)}) %collective-permute-start.16) | collective-permute-done | bytes 917536 | tf_op jit(solution)/shard_map/ppermute | solution.py:63
  88.5 10.2 %shard_map.86 = (bf16[128,3584]{1,0:T(8,128)(2,1)S(1)}, bf16[128,3584]{1,0:T(8,128)(2,1)}, bf16[128,3584]{1,0:T(8,128)(2,1)}, bf16[128,3584]{1,0:T(8,128)(2,1)}, bf16[512,512]{1,0:T(8,128)(2,1)S(1)}) custom-call(s32[8]{0:T(128)S(1)} %concatenate.21.info, f32[512,1024]{1,0:T(8,128)S(1)} %get-tuple-element.70.near, ...), custom_call_target="tpu_custom_call" | custom-call | flops 5637144576 | bytes 7340032 | tf_op jit(solution)/shard_map/pallas_call | solution.py:332
  98.7 0.8 copy-done.1
  99.5 1.7 collective-permute-start.17
  101.2 1.3 collective-permute-start.19
  102.5 6.8 %shard_map.87 = (bf16[128,3584]{1,0:T(8,128)(2,1)}, bf16[128,3584]{1,0:T(8,128)(2,1)}, bf16[128,3584]{1,0:T(8,128)(2,1)}, bf16[128,3584]{1,0:T(8,128)(2,1)}) custom-call(s32[8]{0:T(128)} %copy-done.3, bf16[512,512]{1,0:T(8,128)(2,1)} %copy-done.1, bf16[512,7168]{1,0:T(8,128)(2,1)} %bitcast.12), custom_call_target="tpu_custom_call" | custom-call | flops 1879048192 | bytes 7340032 | tf_op jit(solution)/shard_map/pallas_call | solution.py:367
  109.5 3.8 %collective-permute-start.21 = (bf16[128,3584]{1,0:T(8,128)(2,1)}, bf16[128,3584]{1,0:T(8,128)(2,1)S(1)}, u32[]{:S(2)}, u32[]{:S(2)}) collective-permute-start(bf16[128,3584]{1,0:T(8,128)(2,1)} %get-tuple-element.83), channel_id=1, source_target_pairs={{65,0},{8,1},{67,2},{10,3},{69,4},{12,5},{71,6},{14,7},{73,8},{16,... | collective-permute-start | bytes 2752520 | tf_op jit(solution)/shard_map/ppermute | solution.py:63
  114.0 12.1 %collective-permute-done.18.refs_2_ = bf16[128,3584]{1,0:T(8,128)(2,1)S(1)} collective-permute-done((bf16[128,3584]{1,0:T(8,128)(2,1)}, bf16[128,3584]{1,0:T(8,128)(2,1)S(1)}, u32[]{:S(2)}, u32[]{:S(2)}) %collective-permute-start.18) | collective-permute-done | bytes 917536 | tf_op jit(solution)/shard_map/ppermute | solution.py:63
  126.1 1.8 collective-permute-done.19.refs_3_
  127.9 12.6 %collective-permute-done.21.refs_5_ = bf16[128,3584]{1,0:T(8,128)(2,1)S(1)} collective-permute-done((bf16[128,3584]{1,0:T(8,128)(2,1)}, bf16[128,3584]{1,0:T(8,128)(2,1)S(1)}, u32[]{:S(2)}, u32[]{:S(2)}) %collective-permute-start.21) | collective-permute-done | bytes 917536 | tf_op jit(solution)/shard_map/ppermute | solution.py:63
  140.5 3.8 %collective-permute-done.22.refs_6_ = bf16[128,3584]{1,0:T(8,128)(2,1)S(1)} collective-permute-done((bf16[128,3584]{1,0:T(8,128)(2,1)}, bf16[128,3584]{1,0:T(8,128)(2,1)S(1)}, u32[]{:S(2)}, u32[]{:S(2)}) %collective-permute-start.22) | collective-permute-done | bytes 917536 | tf_op jit(solution)/shard_map/ppermute | solution.py:63
  144.4 3.5 %shard_map.88 = (bf16[128,3584]{1,0:T(8,128)(2,1)S(1)}, bf16[128,3584]{1,0:T(8,128)(2,1)S(1)}, bf16[128,3584]{1,0:T(8,128)(2,1)S(1)}, bf16[128,3584]{1,0:T(8,128)(2,1)S(1)}) custom-call(s32[8]{0:T(128)S(1)} %copy-done.4, bf16[128,3584]{1,0:T(8,128)(2,1)S(1)} %get-tuple-element.77.refs_0_, bf16[128,3584]{1,0:T(8,128)(2,1)S(1)} %collective-permute-done.17.refs_1_, ...), custom_call_target="tpu_custom_call" | custom-call | flops 1879048192 | bytes 11010048 | tf_op jit(solution)/shard_map/pallas_call | solution.py:154
  147.9 2.2 %collective-permute-start.24 = (bf16[128,3584]{1,0:T(8,128)(2,1)S(1)}, bf16[128,3584]{1,0:T(8,128)(2,1)S(1)}, u32[]{:S(2)}, u32[]{:S(2)}) collective-permute-start(bf16[128,3584]{1,0:T(8,128)(2,1)S(1)} %get-tuple-element.86), channel_id=1, source_target_pairs={{8,0},{65,1},{10,2},{67,3},{12,4},{69,5},{14,6},{71,7},{16,8},{73,... | collective-permute-start | bytes 2752520 | tf_op jit(solution)/shard_map/ppermute | solution.py:63
  150.2 2.8 %collective-permute-start.28 = (bf16[32,3584]{1,0:T(8,128)(2,1)S(1)}, bf16[32,3584]{1,0:T(8,128)(2,1)S(1)}, u32[]{:S(2)}, u32[]{:S(2)}) collective-permute-start(bf16[32,3584]{1,0:T(8,128)(2,1)S(1)} %get-tuple-element.105), channel_id=1, source_target_pairs={{4,0},{5,1},{6,2},{7,3},{0,4},{1,5},{2,6},{3,7},{12,8},{13,9},{14,... | collective-permute-start | bytes 688136 | tf_op jit(solution)/shard_map/ppermute | solution.py:55
  153.4 2.2 %collective-permute-start.26 = (bf16[32,3584]{1,0:T(8,128)(2,1)S(1)}, bf16[32,3584]{1,0:T(8,128)(2,1)S(1)}, u32[]{:S(2)}, u32[]{:S(2)}) collective-permute-start(bf16[32,3584]{1,0:T(8,128)(2,1)S(1)} %get-tuple-element.107), channel_id=1, source_target_pairs={{2,0},{3,1},{4,2},{5,3},{6,4},{7,5},{0,6},{1,7},{10,8},{11,9},{12,... | collective-permute-start | bytes 688136 | tf_op jit(solution)/shard_map/ppermute | solution.py:55
  155.6 3.0 %collective-permute-done.28 = bf16[32,3584]{1,0:T(8,128)(2,1)S(1)} collective-permute-done((bf16[32,3584]{1,0:T(8,128)(2,1)S(1)}, bf16[32,3584]{1,0:T(8,128)(2,1)S(1)}, u32[]{:S(2)}, u32[]{:S(2)}) %collective-permute-start.28) | collective-permute-done | bytes 229408 | tf_op jit(solution)/shard_map/ppermute | solution.py:55
  158.7 5.5 %collective-permute-done.27 = bf16[32,3584]{1,0:T(8,128)(2,1)S(1)} collective-permute-done((bf16[32,3584]{1,0:T(8,128)(2,1)S(1)}, bf16[32,3584]{1,0:T(8,128)(2,1)S(1)}, u32[]{:S(2)}, u32[]{:S(2)}) %collective-permute-start.27) | collective-permute-done | bytes 229408 | tf_op jit(solution)/shard_map/ppermute | solution.py:55
  164.6 2.4 %collective-permute-start.32 = (bf16[32,3584]{1,0:T(8,128)(2,1)S(1)}, bf16[32,3584]{1,0:T(8,128)(2,1)S(1)}, u32[]{:S(2)}, u32[]{:S(2)}) collective-permute-start(bf16[32,3584]{1,0:T(8,128)(2,1)S(1)} %get-tuple-element.101), channel_id=1, source_target_pairs={{4,0},{5,1},{6,2},{7,3},{0,4},{1,5},{2,6},{3,7},{12,8},{13,9},{14,... | collective-permute-start | bytes 688136 | tf_op jit(solution)/shard_map/ppermute | solution.py:55
  167.4 2.2 %collective-permute-start.30 = (bf16[32,3584]{1,0:T(8,128)(2,1)S(1)}, bf16[32,3584]{1,0:T(8,128)(2,1)S(1)}, u32[]{:S(2)}, u32[]{:S(2)}) collective-permute-start(bf16[32,3584]{1,0:T(8,128)(2,1)S(1)} %get-tuple-element.103), channel_id=1, source_target_pairs={{2,0},{3,1},{4,2},{5,3},{6,4},{7,5},{0,6},{1,7},{10,8},{11,9},{12,... | collective-permute-start | bytes 688136 | tf_op jit(solution)/shard_map/ppermute | solution.py:55
  170.6 2.0 %collective-permute-done.32 = bf16[32,3584]{1,0:T(8,128)(2,1)S(1)} collective-permute-done((bf16[32,3584]{1,0:T(8,128)(2,1)S(1)}, bf16[32,3584]{1,0:T(8,128)(2,1)S(1)}, u32[]{:S(2)}, u32[]{:S(2)}) %collective-permute-start.32) | collective-permute-done | bytes 229408 | tf_op jit(solution)/shard_map/ppermute | solution.py:55
  172.5 5.9 %collective-permute-done.31 = bf16[32,3584]{1,0:T(8,128)(2,1)S(1)} collective-permute-done((bf16[32,3584]{1,0:T(8,128)(2,1)S(1)}, bf16[32,3584]{1,0:T(8,128)(2,1)S(1)}, u32[]{:S(2)}, u32[]{:S(2)}) %collective-permute-start.31) | collective-permute-done | bytes 229408 | tf_op jit(solution)/shard_map/ppermute | solution.py:55
  178.6 1.3 collective-permute-start.33
  179.9 1.0 collective-permute-done.33
  (61 shorter events, 10.2 us)
Async XLA Ops:
  0.8 87.7 %copy-start.3 = (s32[8]{0:T(128)}, s32[8]{0:T(128)S(1)}, u32[]{:S(2)}) copy-start(s32[8]{0:T(128)S(1)} %concatenate.21.info) | copy-start | bytes 100
  0.8 0.9 copy-start.2
  1.7 0.7 copy-start.5
  2.4 0.7 copy-start.6
  3.1 0.7 copy-start.7
  4.5 2.4 %collective-permute-start = (bf16[16,3712]{1,0:T(8,128)(2,1)S(1)}, bf16[16,3712]{1,0:T(8,128)(2,1)S(1)}, u32[]{:S(2)}, u32[]{:S(2)}) collective-permute-start(bf16[16,3712]{1,0:T(8,128)(2,1)S(1)} %get-tuple-element.54), channel_id=1, source_target_pairs={{0,1},{1,0},{2,3},{3,2},{4,5},{5,4},{6,7},{7,6},{8,9},{9,8},{10,11... | collective-permute-start | bytes 356360 | tf_op jit(solution)/shard_map/ppermute | solution.py:59
  7.0 8.7 %collective-permute-start.4 = (bf16[32,3712]{1,0:T(8,128)(2,1)S(1)}, bf16[32,3712]{1,0:T(8,128)(2,1)S(1)}, u32[]{:S(2)}, u32[]{:S(2)}) collective-permute-start(bf16[32,3712]{1,0:T(8,128)(2,1)S(1)} %maximum_select_fusion), channel_id=1, source_target_pairs={{0,4},{1,5},{2,6},{3,7},{4,0},{5,1},{6,2},{7,3},{8,12},{9,13},{10,... | collective-permute-start | bytes 712712 | tf_op jit(solution)/shard_map/ppermute | solution.py:51
  10.0 11.1 %collective-permute-start.3 = (bf16[32,3712]{1,0:T(8,128)(2,1)S(1)}, bf16[32,3712]{1,0:T(8,128)(2,1)S(1)}, u32[]{:S(2)}, u32[]{:S(2)}) collective-permute-start(bf16[32,3712]{1,0:T(8,128)(2,1)S(1)} %maximum_select_fusion), channel_id=1, source_target_pairs={{0,6},{1,7},{2,0},{3,1},{4,2},{5,3},{6,4},{7,5},{8,14},{9,15},{10,... | collective-permute-start | bytes 712712 | tf_op jit(solution)/shard_map/ppermute | solution.py:51
  10.8 10.4 %collective-permute-start.2 = (bf16[32,3712]{1,0:T(8,128)(2,1)S(1)}, bf16[32,3712]{1,0:T(8,128)(2,1)S(1)}, u32[]{:S(2)}, u32[]{:S(2)}) collective-permute-start(bf16[32,3712]{1,0:T(8,128)(2,1)S(1)} %maximum_select_fusion), channel_id=1, source_target_pairs={{0,2},{1,3},{2,4},{3,5},{4,6},{5,7},{6,0},{7,1},{8,10},{9,11},{10,... | collective-permute-start | bytes 712712 | tf_op jit(solution)/shard_map/ppermute | solution.py:51
  11.5 9.7 %collective-permute-start.1 = (bf16[32,3712]{1,0:T(8,128)(2,1)S(1)}, bf16[32,3712]{1,0:T(8,128)(2,1)S(1)}, u32[]{:S(2)}, u32[]{:S(2)}) collective-permute-start(bf16[32,3712]{1,0:T(8,128)(2,1)S(1)} %maximum_select_fusion), channel_id=1, source_target_pairs={{0,16},{1,33},{2,18},{3,35},{4,20},{5,37},{6,22},{7,39},{8,24},{9,... | collective-permute-start | bytes 712712 | tf_op jit(solution)/shard_map/ppermute | solution.py:406
  21.3 16.1 %collective-permute-start.6 = (bf16[128,3712]{1,0:T(8,128)(2,1)S(1)}, bf16[128,3712]{1,0:T(8,128)(2,1)S(1)}, u32[]{:S(2)}, u32[]{:S(2)}) collective-permute-start(bf16[128,3712]{1,0:T(8,128)(2,1)S(1)} %constant_dynamic-update-slice_fusion.refs_0_.refs_8_), channel_id=1, source_target_pairs={{0,24},{1,97},{2,26},{3,99},{4,28},{5,101},{6,30},{7,103},{8,0},{9... | collective-permute-start | bytes 2850824 | tf_op jit(solution)/shard_map/ppermute | solution.py:63
  23.9 14.1 %collective-permute-start.5 = (bf16[128,3712]{1,0:T(8,128)(2,1)S(1)}, bf16[128,3712]{1,0:T(8,128)(2,1)S(1)}, u32[]{:S(2)}, u32[]{:S(2)}) collective-permute-start(bf16[128,3712]{1,0:T(8,128)(2,1)S(1)} %constant_dynamic-update-slice_fusion.refs_0_.refs_8_), channel_id=1, source_target_pairs={{0,8},{1,65},{2,10},{3,67},{4,12},{5,69},{6,14},{7,71},{8,16},{9,7... | collective-permute-start | bytes 2850824 | tf_op jit(solution)/shard_map/ppermute | solution.py:63
  23.9 6.6 %collective-permute-start.9 = (bf16[32,3712]{1,0:T(8,128)(2,1)S(1)}, bf16[32,3712]{1,0:T(8,128)(2,1)S(1)}, u32[]{:S(2)}, u32[]{:S(2)}) collective-permute-start(bf16[32,3712]{1,0:T(8,128)(2,1)S(1)} %collective-permute-done.1), channel_id=1, source_target_pairs={{0,4},{1,5},{2,6},{3,7},{4,0},{5,1},{6,2},{7,3},{8,12},{9,13},{10,... | collective-permute-start | bytes 712712 | tf_op jit(solution)/shard_map/ppermute | solution.py:51
  27.0 10.2 %collective-permute-start.8 = (bf16[32,3712]{1,0:T(8,128)(2,1)S(1)}, bf16[32,3712]{1,0:T(8,128)(2,1)S(1)}, u32[]{:S(2)}, u32[]{:S(2)}) collective-permute-start(bf16[32,3712]{1,0:T(8,128)(2,1)S(1)} %collective-permute-done.1), channel_id=1, source_target_pairs={{0,6},{1,7},{2,0},{3,1},{4,2},{5,3},{6,4},{7,5},{8,14},{9,15},{10,... | collective-permute-start | bytes 712712 | tf_op jit(solution)/shard_map/ppermute | solution.py:51
  27.8 9.7 %collective-permute-start.7 = (bf16[32,3712]{1,0:T(8,128)(2,1)S(1)}, bf16[32,3712]{1,0:T(8,128)(2,1)S(1)}, u32[]{:S(2)}, u32[]{:S(2)}) collective-permute-start(bf16[32,3712]{1,0:T(8,128)(2,1)S(1)} %collective-permute-done.1), channel_id=1, source_target_pairs={{0,2},{1,3},{2,4},{3,5},{4,6},{5,7},{6,0},{7,1},{8,10},{9,11},{10,... | collective-permute-start | bytes 712712 | tf_op jit(solution)/shard_map/ppermute | solution.py:51
  38.1 31.8 %copy-start = (bf16[1,7168,512]{2,1,0:T(8,128)(2,1)S(1)}, bf16[1,7168,512]{2,1,0:T(8,128)(2,1)}, u32[]{:S(2)}) copy-start(bf16[1,7168,512]{2,1,0:T(8,128)(2,1)} %param.12) | copy-start | bytes 22020100
  40.4 14.9 %collective-permute-start.10 = (bf16[128,3584]{1,0:T(8,128)(2,1)S(1)}, bf16[128,3584]{1,0:T(8,128)(2,1)S(1)}, u32[]{:S(2)}, u32[]{:S(2)}) collective-permute-start(bf16[128,3584]{1,0:T(8,128)(2,1)S(1)} %get-tuple-element.67), channel_id=1, source_target_pairs={{0,64},{1,9},{2,66},{3,11},{4,68},{5,13},{6,70},{7,15},{8,72},{9,1... | collective-permute-start | bytes 2752520 | tf_op jit(solution)/shard_map/ppermute | solution.py:63
  42.5 22.0 %collective-permute-start.11 = (bf16[128,3584]{1,0:T(8,128)(2,1)S(1)}, bf16[128,3584]{1,0:T(8,128)(2,1)S(1)}, u32[]{:S(2)}, u32[]{:S(2)}) collective-permute-start(bf16[128,3584]{1,0:T(8,128)(2,1)S(1)} %get-tuple-element.68), channel_id=1, source_target_pairs={{0,96},{1,25},{2,98},{3,27},{4,100},{5,29},{6,102},{7,31},{8,104},... | collective-permute-start | bytes 2752520 | tf_op jit(solution)/shard_map/ppermute | solution.py:63
  44.3 25.6 %collective-permute-start.12 = (bf16[128,3584]{1,0:T(8,128)(2,1)S(1)}, bf16[128,3584]{1,0:T(8,128)(2,1)S(1)}, u32[]{:S(2)}, u32[]{:S(2)}) collective-permute-start(bf16[128,3584]{1,0:T(8,128)(2,1)S(1)} %get-tuple-element.69), channel_id=1, source_target_pairs={{0,32},{1,17},{2,34},{3,19},{4,36},{5,21},{6,38},{7,23},{8,40},{9,... | collective-permute-start | bytes 2752520 | tf_op jit(solution)/shard_map/ppermute | solution.py:63
  49.4 27.8 %collective-permute-start.13 = (bf16[128,3584]{1,0:T(8,128)(2,1)}, bf16[128,3584]{1,0:T(8,128)(2,1)S(1)}, u32[]{:S(2)}, u32[]{:S(2)}) collective-permute-start(bf16[128,3584]{1,0:T(8,128)(2,1)} %get-tuple-element.73), channel_id=1, source_target_pairs={{0,1},{1,0},{2,3},{3,2},{4,5},{5,4},{6,7},{7,6},{8,9},{9,8},{10,11... | collective-permute-start | bytes 2752520 | tf_op jit(solution)/shard_map/ppermute | solution.py:59
  52.4 25.4 %collective-permute-start.14 = (bf16[128,3584]{1,0:T(8,128)(2,1)}, bf16[128,3584]{1,0:T(8,128)(2,1)S(1)}, u32[]{:S(2)}, u32[]{:S(2)}) collective-permute-start(bf16[128,3584]{1,0:T(8,128)(2,1)} %get-tuple-element.74), channel_id=1, source_target_pairs={{0,65},{1,8},{2,67},{3,10},{4,69},{5,12},{6,71},{7,14},{8,73},{9,1... | collective-permute-start | bytes 2752520 | tf_op jit(solution)/shard_map/ppermute | solution.py:63
  55.3 22.9 %collective-permute-start.15 = (bf16[128,3584]{1,0:T(8,128)(2,1)S(1)}, bf16[128,3584]{1,0:T(8,128)(2,1)S(1)}, u32[]{:S(2)}, u32[]{:S(2)}) collective-permute-start(bf16[128,3584]{1,0:T(8,128)(2,1)S(1)} %get-tuple-element.75), channel_id=1, source_target_pairs={{0,97},{1,24},{2,99},{3,26},{4,101},{5,28},{6,103},{7,30},{8,105},... | collective-permute-start | bytes 2752520 | tf_op jit(solution)/shard_map/ppermute | solution.py:63
  64.5 24.0 %collective-permute-start.16 = (bf16[128,3584]{1,0:T(8,128)(2,1)S(1)}, bf16[128,3584]{1,0:T(8,128)(2,1)}, u32[]{:S(2)}, u32[]{:S(2)}) collective-permute-start(bf16[128,3584]{1,0:T(8,128)(2,1)S(1)} %get-tuple-element.76), channel_id=1, source_target_pairs={{0,33},{1,16},{2,35},{3,18},{4,37},{5,20},{6,39},{7,22},{8,41},{9,... | collective-permute-start | bytes 2752520 | tf_op jit(solution)/shard_map/ppermute | solution.py:63
  98.7 0.8 copy-start.1
  99.5 14.5 %collective-permute-start.17 = (bf16[128,3584]{1,0:T(8,128)(2,1)}, bf16[128,3584]{1,0:T(8,128)(2,1)S(1)}, u32[]{:S(2)}, u32[]{:S(2)}) collective-permute-start(bf16[128,3584]{1,0:T(8,128)(2,1)} %get-tuple-element.78), channel_id=1, source_target_pairs={{64,0},{9,1},{66,2},{11,3},{68,4},{13,5},{70,6},{15,7},{72,8},{17,... | collective-permute-start | bytes 2752520 | tf_op jit(solution)/shard_map/ppermute | solution.py:63
  101.2 24.9 %collective-permute-start.18 = (bf16[128,3584]{1,0:T(8,128)(2,1)}, bf16[128,3584]{1,0:T(8,128)(2,1)S(1)}, u32[]{:S(2)}, u32[]{:S(2)}) collective-permute-start(bf16[128,3584]{1,0:T(8,128)(2,1)} %get-tuple-element.79), channel_id=1, source_target_pairs={{96,0},{25,1},{98,2},{27,3},{100,4},{29,5},{102,6},{31,7},{104,8},... | collective-permute-start | bytes 2752520 | tf_op jit(solution)/shard_map/ppermute | solution.py:63
  101.2 26.7 %collective-permute-start.19 = (bf16[128,3584]{1,0:T(8,128)(2,1)}, bf16[128,3584]{1,0:T(8,128)(2,1)S(1)}, u32[]{:S(2)}, u32[]{:S(2)}) collective-permute-start(bf16[128,3584]{1,0:T(8,128)(2,1)} %get-tuple-element.80), channel_id=1, source_target_pairs={{32,0},{17,1},{34,2},{19,3},{36,4},{21,5},{38,6},{23,7},{40,8},{25... | collective-permute-start | bytes 2752520 | tf_op jit(solution)/shard_map/ppermute | solution.py:63
  102.5 41.8 %copy-start.4 = (s32[8]{0:T(128)S(1)}, s32[8]{0:T(128)}, u32[]{:S(2)}) copy-start(s32[8]{0:T(128)} %copy-done.3) | copy-start | bytes 100
  109.4 18.6 %collective-permute-start.20 = (bf16[128,3584]{1,0:T(8,128)(2,1)}, bf16[128,3584]{1,0:T(8,128)(2,1)S(1)}, u32[]{:S(2)}, u32[]{:S(2)}) collective-permute-start(bf16[128,3584]{1,0:T(8,128)(2,1)} %get-tuple-element.82), channel_id=1, source_target_pairs={{0,1},{1,0},{2,3},{3,2},{4,5},{5,4},{6,7},{7,6},{8,9},{9,8},{10,11... | collective-permute-start | bytes 2752520 | tf_op jit(solution)/shard_map/ppermute | solution.py:59
  109.5 31.1 %collective-permute-start.21 = (bf16[128,3584]{1,0:T(8,128)(2,1)}, bf16[128,3584]{1,0:T(8,128)(2,1)S(1)}, u32[]{:S(2)}, u32[]{:S(2)}) collective-permute-start(bf16[128,3584]{1,0:T(8,128)(2,1)} %get-tuple-element.83), channel_id=1, source_target_pairs={{65,0},{8,1},{67,2},{10,3},{69,4},{12,5},{71,6},{14,7},{73,8},{16,... | collective-permute-start | bytes 2752520 | tf_op jit(solution)/shard_map/ppermute | solution.py:63
  114.0 30.4 %collective-permute-start.22 = (bf16[128,3584]{1,0:T(8,128)(2,1)}, bf16[128,3584]{1,0:T(8,128)(2,1)S(1)}, u32[]{:S(2)}, u32[]{:S(2)}) collective-permute-start(bf16[128,3584]{1,0:T(8,128)(2,1)} %get-tuple-element.84), channel_id=1, source_target_pairs={{97,0},{24,1},{99,2},{26,3},{101,4},{28,5},{103,6},{30,7},{105,8},... | collective-permute-start | bytes 2752520 | tf_op jit(solution)/shard_map/ppermute | solution.py:63
  126.1 18.3 %collective-permute-start.23 = (bf16[128,3584]{1,0:T(8,128)(2,1)}, bf16[128,3584]{1,0:T(8,128)(2,1)S(1)}, u32[]{:S(2)}, u32[]{:S(2)}) collective-permute-start(bf16[128,3584]{1,0:T(8,128)(2,1)} %get-tuple-element.85), channel_id=1, source_target_pairs={{33,0},{16,1},{35,2},{18,3},{37,4},{20,5},{39,6},{22,7},{41,8},{24... | collective-permute-start | bytes 2752520 | tf_op jit(solution)/shard_map/ppermute | solution.py:63
  147.9 16.3 %collective-permute-start.24 = (bf16[128,3584]{1,0:T(8,128)(2,1)S(1)}, bf16[128,3584]{1,0:T(8,128)(2,1)S(1)}, u32[]{:S(2)}, u32[]{:S(2)}) collective-permute-start(bf16[128,3584]{1,0:T(8,128)(2,1)S(1)} %get-tuple-element.86), channel_id=1, source_target_pairs={{8,0},{65,1},{10,2},{67,3},{12,4},{69,5},{14,6},{71,7},{16,8},{73,... | collective-permute-start | bytes 2752520 | tf_op jit(solution)/shard_map/ppermute | solution.py:63
  150.1 14.1 %collective-permute-start.25 = (bf16[128,3584]{1,0:T(8,128)(2,1)S(1)}, bf16[128,3584]{1,0:T(8,128)(2,1)S(1)}, u32[]{:S(2)}, u32[]{:S(2)}) collective-permute-start(bf16[128,3584]{1,0:T(8,128)(2,1)S(1)} %get-tuple-element.87), channel_id=1, source_target_pairs={{24,0},{97,1},{26,2},{99,3},{28,4},{101,5},{30,6},{103,7},{0,8},{1... | collective-permute-start | bytes 2752520 | tf_op jit(solution)/shard_map/ppermute | solution.py:63
  150.2 8.5 %collective-permute-start.28 = (bf16[32,3584]{1,0:T(8,128)(2,1)S(1)}, bf16[32,3584]{1,0:T(8,128)(2,1)S(1)}, u32[]{:S(2)}, u32[]{:S(2)}) collective-permute-start(bf16[32,3584]{1,0:T(8,128)(2,1)S(1)} %get-tuple-element.105), channel_id=1, source_target_pairs={{4,0},{5,1},{6,2},{7,3},{0,4},{1,5},{2,6},{3,7},{12,8},{13,9},{14,... | collective-permute-start | bytes 688136 | tf_op jit(solution)/shard_map/ppermute | solution.py:55
  152.9 11.3 %collective-permute-start.27 = (bf16[32,3584]{1,0:T(8,128)(2,1)S(1)}, bf16[32,3584]{1,0:T(8,128)(2,1)S(1)}, u32[]{:S(2)}, u32[]{:S(2)}) collective-permute-start(bf16[32,3584]{1,0:T(8,128)(2,1)S(1)} %get-tuple-element.106), channel_id=1, source_target_pairs={{6,0},{7,1},{0,2},{1,3},{2,4},{3,5},{4,6},{5,7},{14,8},{15,9},{8,1... | collective-permute-start | bytes 688136 | tf_op jit(solution)/shard_map/ppermute | solution.py:55
  153.4 10.8 %collective-permute-start.26 = (bf16[32,3584]{1,0:T(8,128)(2,1)S(1)}, bf16[32,3584]{1,0:T(8,128)(2,1)S(1)}, u32[]{:S(2)}, u32[]{:S(2)}) collective-permute-start(bf16[32,3584]{1,0:T(8,128)(2,1)S(1)} %get-tuple-element.107), channel_id=1, source_target_pairs={{2,0},{3,1},{4,2},{5,3},{6,4},{7,5},{0,6},{1,7},{10,8},{11,9},{12,... | collective-permute-start | bytes 688136 | tf_op jit(solution)/shard_map/ppermute | solution.py:55
  164.6 7.9 %collective-permute-start.32 = (bf16[32,3584]{1,0:T(8,128)(2,1)S(1)}, bf16[32,3584]{1,0:T(8,128)(2,1)S(1)}, u32[]{:S(2)}, u32[]{:S(2)}) collective-permute-start(bf16[32,3584]{1,0:T(8,128)(2,1)S(1)} %get-tuple-element.101), channel_id=1, source_target_pairs={{4,0},{5,1},{6,2},{7,3},{0,4},{1,5},{2,6},{3,7},{12,8},{13,9},{14,... | collective-permute-start | bytes 688136 | tf_op jit(solution)/shard_map/ppermute | solution.py:55
  167.0 11.4 %collective-permute-start.31 = (bf16[32,3584]{1,0:T(8,128)(2,1)S(1)}, bf16[32,3584]{1,0:T(8,128)(2,1)S(1)}, u32[]{:S(2)}, u32[]{:S(2)}) collective-permute-start(bf16[32,3584]{1,0:T(8,128)(2,1)S(1)} %get-tuple-element.102), channel_id=1, source_target_pairs={{6,0},{7,1},{0,2},{1,3},{2,4},{3,5},{4,6},{5,7},{14,8},{15,9},{8,1... | collective-permute-start | bytes 688136 | tf_op jit(solution)/shard_map/ppermute | solution.py:55
  167.4 11.0 %collective-permute-start.30 = (bf16[32,3584]{1,0:T(8,128)(2,1)S(1)}, bf16[32,3584]{1,0:T(8,128)(2,1)S(1)}, u32[]{:S(2)}, u32[]{:S(2)}) collective-permute-start(bf16[32,3584]{1,0:T(8,128)(2,1)S(1)} %get-tuple-element.103), channel_id=1, source_target_pairs={{2,0},{3,1},{4,2},{5,3},{6,4},{7,5},{0,6},{1,7},{10,8},{11,9},{12,... | collective-permute-start | bytes 688136 | tf_op jit(solution)/shard_map/ppermute | solution.py:55
  169.8 8.6 %collective-permute-start.29 = (bf16[32,3584]{1,0:T(8,128)(2,1)S(1)}, bf16[32,3584]{1,0:T(8,128)(2,1)S(1)}, u32[]{:S(2)}, u32[]{:S(2)}) collective-permute-start(bf16[32,3584]{1,0:T(8,128)(2,1)S(1)} %add_convert_fusion.2), channel_id=1, source_target_pairs={{16,0},{33,1},{18,2},{35,3},{20,4},{37,5},{22,6},{39,7},{24,8},{41... | collective-permute-start | bytes 688136 | tf_op jit(solution)/shard_map/ppermute | solution.py:424
  178.6 2.3 %collective-permute-start.33 = (bf16[16,3584]{1,0:T(8,128)(2,1)S(1)}, bf16[16,3584]{1,0:T(8,128)(2,1)S(1)}, u32[]{:S(2)}, u32[]{:S(2)}) collective-permute-start(bf16[16,3584]{1,0:T(8,128)(2,1)S(1)} %get-tuple-element.110), channel_id=1, source_target_pairs={{0,1},{1,0},{2,3},{3,2},{4,5},{5,4},{6,7},{7,6},{8,9},{9,8},{10,11... | collective-permute-start | bytes 344072 | tf_op jit(solution)/shard_map/ppermute | solution.py:59

commit v4 on v3

--- a/solution.py
+++ b/solution.py
@@ -129,19 +129,22 @@
     )(info, *blocks))
 
 
-def combine_kernel(info, *refs):
-    blocks, metas, outs = refs[:2 * RING], refs[2 * RING:3 * RING], refs[3 * RING:]
-    experts = experts_at(info)
+def mixer_of(info, meta):
+    place, match, turned = slots_of(meta, experts_at(info))
+    parts = []
+    for offset in (TOP, 2 * TOP):
+        mix = turned[offset:offset + TOP]
+        picked = [jnp.sum(jnp.where(m, mix, 0.0), axis=0, keepdims=True) for m in match]
+        weight = jnp.concatenate([jnp.where(p, w, 0.0) for p, w in zip(place, picked)], axis=0)
+        parts.append(jnp.transpose(weight))
+    return jnp.concatenate(parts, axis=0).astype(jnp.bfloat16)
+
+
+def combine_kernel(mixers, *refs):
+    blocks, outs = refs[:2 * RING], refs[2 * RING:]
     rows = BLOCK // RING
     for b in range(RING):
-        place, match, turned = slots_of(metas[b][...], experts)
-        parts = []
-        for offset in (TOP, 2 * TOP):
-            mix = turned[offset:offset + TOP]
-            picked = [jnp.sum(jnp.where(m, mix, 0.0), axis=0, keepdims=True) for m in match]
-            weight = jnp.concatenate([jnp.where(p, w, 0.0) for p, w in zip(place, picked)], axis=0)
-            parts.append(jnp.transpose(weight))
-        mixer = jnp.concatenate(parts, axis=0).astype(jnp.bfloat16)
+        mixer = mixers[2 * BLOCK * b:2 * BLOCK * (b + 1)]
         for start, size in column_chunks(HALF):
             cols = slice(start, start + size)
             data = jnp.concatenate([block[rows * b:rows * (b + 1), cols] for block in blocks], axis=0)
@@ -149,18 +152,16 @@
             outs[b][:, cols] = (got[:BLOCK] + got[BLOCK:]).astype(jnp.bfloat16)
 
 
-def combine(info, blocks, metas):
-    meta_spec = pl.BlockSpec((BLOCK, META), lambda i: (0, HALF // META))
+def combine(mixers, blocks):
     return list(pl.pallas_call(
         combine_kernel,
-        grid=(1,),
         out_shape=[jax.ShapeDtypeStruct((BLOCK, HALF), jnp.bfloat16)] * RING,
-        in_specs=[SMEM_SPEC] + [VMEM_SPEC] * (2 * RING) + [meta_spec] * RING,
+        in_specs=[VMEM_SPEC] * (1 + 2 * RING),
         out_specs=[VMEM_SPEC] * RING,
         compiler_params=pltpu.CompilerParams(vmem_limit_bytes=SMALL_VMEM),
         cost_estimate=pl.CostEstimate(
             flops=8 * RING * BLOCK * BLOCK * HALF, bytes_accessed=24 * BLOCK * HALF, transcendentals=0),
-    )(info, *blocks, *metas))
+    )(mixers, *blocks))
 
 
 def weight_copies(chunks, gate_hbm, up_hbm, w_in, in_sem):
@@ -347,13 +348,15 @@
 
 
 def spread_kernel(info, hidden, down_hbm, *refs):
-    outs, (w_out, down_sem) = refs[:RING], refs[RING:]
+    metas, outs, (mixers, w_out, down_sem) = refs[:RING], refs[RING:2 * RING], refs[2 * RING:]
     base = (1 - info[0]) * HALF
     steps = column_chunks(HALF)
     copies = [pltpu.make_async_copy(
         down_hbm.at[:, pl.ds(pl.multiple_of(base + start, BLOCK), size)], w_out.at[:, pl.ds(start, size)],
         down_sem.at[i]) for i, (start, size) in enumerate(steps)]
     start_all(copies)
+    for b in range(RING):
+        mixers[2 * BLOCK * b:2 * BLOCK * (b + 1)] = mixer_of(info, metas[b][...])
     for (start, size), copy in zip(steps, copies):
         copy.wait()
         cols = slice(start, start + size)
@@ -362,20 +365,23 @@
             outs[r][:, cols] = got[BLOCK * r:BLOCK * (r + 1)]
 
 
-def spread(info, hidden, down_w):
+def spread(info, hidden, down_w, pool):
     rows, hid = hidden.shape
+    meta_spec = pl.BlockSpec((BLOCK, META), lambda i: (0, HALF // META))
     out = pl.pallas_call(
         spread_kernel,
-        out_shape=[jax.ShapeDtypeStruct((BLOCK, HALF), jnp.bfloat16)] * RING,
-        in_specs=[SMEM_SPEC, VMEM_SPEC, HBM_SPEC],
-        out_specs=[VMEM_SPEC] * RING,
+        grid=(1,),
+        out_shape=[jax.ShapeDtypeStruct((BLOCK, HALF), jnp.bfloat16)] * RING + [
+            jax.ShapeDtypeStruct((2 * BLOCK * RING, 2 * BLOCK), jnp.bfloat16)],
+        in_specs=[SMEM_SPEC, VMEM_SPEC, HBM_SPEC] + [meta_spec] * RING,
+        out_specs=[VMEM_SPEC] * (RING + 1),
         scratch_shapes=[
             pltpu.VMEM((hid, HALF), jnp.bfloat16), pltpu.SemaphoreType.DMA((len(column_chunks(HALF)),))],
         compiler_params=pltpu.CompilerParams(vmem_limit_bytes=LARGE_VMEM),
         cost_estimate=pl.CostEstimate(
             flops=2 * rows * HALF * hid, bytes_accessed=2 * HALF * (hid + rows), transcendentals=0),
-    )(info, hidden, down_w)
-    return list(out)
+    )(info, hidden, down_w, *pool)
+    return list(out[:RING]), out[RING]
 
 
 def summed(blocks):
@@ -414,10 +420,10 @@
     gate_w, up_w, down_w = gate_weight[0], up_weight[0], down_weight[0]
     near, w_in, w_out = project(info, own, gate_w, up_w, down_w)
     own, hidden = expert(info, near, w_in, w_out, far)
-    far = spread(info, hidden, down_w)
+    far, mixers = spread(info, hidden, down_w, pool)
     own = own[:1] + hop(own, ROUTE[2], back_perm, (1, 2, 3))
     far = hop(far, ROUTE[2], back_perm, (0, 1, 2, 3), cross=True)
-    sums = combine(info, own + far, pool)
+    sums = combine(mixers, own + far)
     ahead, part = together(hop(sums, ROUTE[1], back_perm, (1, 2)), scattered(split_rows(sums[3]), ROUTE[0]))
     line, part = summed(sums[:1] + ahead), summed(part)
     part, line = together(

time: 182 us -> 190 us (1.044)
  waiting for transfers between devices: 84.6 us -> 88.7 us
  starting transfers between devices: 56.3 us -> 60.1 us
  Pallas kernels: 34.4 us -> 31.1 us
  local copies, waits for them, and re-layouts: 4.18 us -> 7.43 us
    ppermute x16, waiting for transfers between devices: 50.2 us -> 54.3 us  [hop(): lax.ppermute(blocks[r], ALL_AXES, perm(axes, SHIFTS[r], cross))]
    ppermute x16, starting transfers between devices: 27.4 us -> 31 us  [hop(): lax.ppermute(blocks[r], ALL_AXES, perm(axes, SHIFTS[r], cross))]
    unnamed x22 -> x34, local copies, waits for them, and re-layouts: 3.92 us -> 7.17 us
  transfers between devices with their start and end apart: 34 -> 34, of which waited for: 23 -> 21; matrix products, arithmetic and copies ran while one was open for 0% -> 0% of each run, Pallas kernels for 10% -> 6%
where the time goes in v4:
time: 190 us
  waiting for transfers between devices  88.7 us (47%)
  starting transfers between devices  60.1 us (32%)
  Pallas kernels  31.1 us (16%)
  local copies, waits for them, and re-layouts  7.43 us (4%)
  other arithmetic  2.08 us (1%)
    ppermute x16, waiting for transfers between devices, hop(): lax.ppermute(blocks[r], ALL_AXES, perm(axes, SHIFTS[r], cross))  54.3 us
    ppermute x16, starting transfers between devices, hop(): lax.ppermute(blocks[r], ALL_AXES, perm(axes, SHIFTS[r], cross))  31 us
    ppermute x6, waiting for transfers between devices, scattered(): lax.ppermute(b, ALL_AXES, back_perm(axes, s))  16.5 us
    ppermute x6, waiting for transfers between devices, gathered(): lax.ppermute(value, ALL_AXES, ring_perm(axes, s))  15.9 us
    ppermute x6, starting transfers between devices, scattered(): lax.ppermute(b, ALL_AXES, back_perm(axes, s))  9.54 us
    ppermute x6, starting transfers between devices, gathered(): lax.ppermute(value, ALL_AXES, ring_perm(axes, s))  9.06 us
    pallas_call x1, Pallas kernels, expert(): pl.pallas_call(expert_kernel, out_shape=[jax.ShapeDtypeStruct((BLOCK, HAL...  8.6 us
    pallas_call x1, Pallas kernels, project(): pl.pallas_call(project_kernel, out_shape=[jax.ShapeDtypeStruct((rows, 2 *...  7.27 us
  transfers between devices with their start and end apart: 34, of which 21 were waited for; matrix products, arithmetic and copies ran while one was open for 0% of the time, Pallas kernels for 6%

profile of v4, /device:TPU:1, one launch (start us, length us, event | category | flops | bytes accessed | tf_op | source)
XLA Modules:
  0.0 189.7 jit_solution(6515461176255331358)
XLA Ops:
  0.8 0.9 copy-done.7
  4.5 1.4 collective-permute-start
  5.9 1.0 collective-permute-done
  7.0 3.1 %collective-permute-start.4 = (bf16[32,3712]{1,0:T(8,128)(2,1)S(1)}, bf16[32,3712]{1,0:T(8,128)(2,1)S(1)}, u32[]{:S(2)}, u32[]{:S(2)}) collective-permute-start(bf16[32,3712]{1,0:T(8,128)(2,1)S(1)} %maximum_select_fusion), channel_id=1, source_target_pairs={{0,4},{1,5},{2,6},{3,7},{4,0},{5,1},{6,2},{7,3},{8,12},{9,13},{10,... | collective-permute-start | bytes 712712 | tf_op jit(solution)/shard_map/ppermute | solution.py:51
  11.5 2.7 %collective-permute-start.1 = (bf16[32,3712]{1,0:T(8,128)(2,1)S(1)}, bf16[32,3712]{1,0:T(8,128)(2,1)S(1)}, u32[]{:S(2)}, u32[]{:S(2)}) collective-permute-start(bf16[32,3712]{1,0:T(8,128)(2,1)S(1)} %maximum_select_fusion), channel_id=1, source_target_pairs={{0,16},{1,33},{2,18},{3,35},{4,20},{5,37},{6,22},{7,39},{8,24},{9,... | collective-permute-start | bytes 712712 | tf_op jit(solution)/shard_map/ppermute | solution.py:412
  14.2 1.4 collective-permute-done.4
  15.6 5.5 %collective-permute-done.3 = bf16[32,3712]{1,0:T(8,128)(2,1)S(1)} collective-permute-done((bf16[32,3712]{1,0:T(8,128)(2,1)S(1)}, bf16[32,3712]{1,0:T(8,128)(2,1)S(1)}, u32[]{:S(2)}, u32[]{:S(2)}) %collective-permute-start.3) | collective-permute-done | bytes 237600 | tf_op jit(solution)/shard_map/ppermute | solution.py:51
  21.3 2.6 %collective-permute-start.6 = (bf16[128,3712]{1,0:T(8,128)(2,1)S(1)}, bf16[128,3712]{1,0:T(8,128)(2,1)S(1)}, u32[]{:S(2)}, u32[]{:S(2)}) collective-permute-start(bf16[128,3712]{1,0:T(8,128)(2,1)S(1)} %constant_dynamic-update-slice_fusion.refs_0_), channel_id=1, source_target_pairs={{0,24},{1,97},{2,26},{3,99},{4,28},{5,101},{6,30},{7,103},{8,0},{9... | collective-permute-start | bytes 2850824 | tf_op jit(solution)/shard_map/ppermute | solution.py:63
  23.9 3.1 %collective-permute-start.9 = (bf16[32,3712]{1,0:T(8,128)(2,1)S(1)}, bf16[32,3712]{1,0:T(8,128)(2,1)S(1)}, u32[]{:S(2)}, u32[]{:S(2)}) collective-permute-start(bf16[32,3712]{1,0:T(8,128)(2,1)S(1)} %collective-permute-done.1), channel_id=1, source_target_pairs={{0,4},{1,5},{2,6},{3,7},{4,0},{5,1},{6,2},{7,3},{8,12},{9,13},{10,... | collective-permute-start | bytes 712712 | tf_op jit(solution)/shard_map/ppermute | solution.py:51
  28.5 2.0 %collective-permute-done.9 = bf16[32,3712]{1,0:T(8,128)(2,1)S(1)} collective-permute-done((bf16[32,3712]{1,0:T(8,128)(2,1)S(1)}, bf16[32,3712]{1,0:T(8,128)(2,1)S(1)}, u32[]{:S(2)}, u32[]{:S(2)}) %collective-permute-start.9) | collective-permute-done | bytes 237600 | tf_op jit(solution)/shard_map/ppermute | solution.py:51
  30.5 6.7 %collective-permute-done.8 = bf16[32,3712]{1,0:T(8,128)(2,1)S(1)} collective-permute-done((bf16[32,3712]{1,0:T(8,128)(2,1)S(1)}, bf16[32,3712]{1,0:T(8,128)(2,1)S(1)}, u32[]{:S(2)}, u32[]{:S(2)}) %collective-permute-start.8) | collective-permute-done | bytes 237600 | tf_op jit(solution)/shard_map/ppermute | solution.py:51
  38.2 2.2 %shard_map.83 = (bf16[128,3584]{1,0:T(8,128)(2,1)S(1)}, bf16[128,3584]{1,0:T(8,128)(2,1)S(1)}, bf16[128,3584]{1,0:T(8,128)(2,1)S(1)}, bf16[128,3584]{1,0:T(8,128)(2,1)S(1)}) custom-call(s32[8]{0:T(128)S(1)} %concatenate.21.info, bf16[128,3712]{1,0:T(8,128)(2,1)S(1)} %constant_dynamic-update-slice_fusion.refs_0_, ...), custom_call_target="tpu_custom_call" | custom-call | flops 469762048 | bytes 7340032 | tf_op jit(solution)/shard_map/pallas_call | solution.py:121
  40.4 2.1 %collective-permute-start.10 = (bf16[128,3584]{1,0:T(8,128)(2,1)S(1)}, bf16[128,3584]{1,0:T(8,128)(2,1)S(1)}, u32[]{:S(2)}, u32[]{:S(2)}) collective-permute-start(bf16[128,3584]{1,0:T(8,128)(2,1)S(1)} %get-tuple-element.68), channel_id=1, source_target_pairs={{0,64},{1,9},{2,66},{3,11},{4,68},{5,13},{6,70},{7,15},{8,72},{9,1... | collective-permute-start | bytes 2752520 | tf_op jit(solution)/shard_map/ppermute | solution.py:63
  42.6 1.8 collective-permute-start.11
  44.3 1.7 collective-permute-start.12
  46.0 3.2 %shard_map.85 = (bf16[128,3584]{1,0:T(8,128)(2,1)}, bf16[128,3584]{1,0:T(8,128)(2,1)S(1)}, bf16[128,3584]{1,0:T(8,128)(2,1)S(1)}, bf16[128,3584]{1,0:T(8,128)(2,1)S(1)}) custom-call(s32[8]{0:T(128)S(1)} %concatenate.21.info, bf16[128,3712]{1,0:T(8,128)(2,1)S(1)} %constant_dynamic-update-slice_fusion.refs_0_, ...), custom_call_target="tpu_custom_call" | custom-call | flops 469762048 | bytes 7340032 | tf_op jit(solution)/shard_map/pallas_call | solution.py:121
  49.2 3.0 %collective-permute-start.13 = (bf16[128,3584]{1,0:T(8,128)(2,1)}, bf16[128,3584]{1,0:T(8,128)(2,1)S(1)}, u32[]{:S(2)}, u32[]{:S(2)}) collective-permute-start(bf16[128,3584]{1,0:T(8,128)(2,1)} %get-tuple-element.74), channel_id=1, source_target_pairs={{0,1},{1,0},{2,3},{3,2},{4,5},{5,4},{6,7},{7,6},{8,9},{9,8},{10,11... | collective-permute-start | bytes 2752520 | tf_op jit(solution)/shard_map/ppermute | solution.py:59
  52.2 3.2 %collective-permute-done.10.refs_1_ = bf16[128,3584]{1,0:T(8,128)(2,1)S(1)} collective-permute-done((bf16[128,3584]{1,0:T(8,128)(2,1)S(1)}, bf16[128,3584]{1,0:T(8,128)(2,1)S(1)}, u32[]{:S(2)}, u32[]{:S(2)}) %collective-permute-start.10) | collective-permute-done | bytes 917536 | tf_op jit(solution)/shard_map/ppermute | solution.py:63
  55.3 4.7 %collective-permute-start.15 = (bf16[128,3584]{1,0:T(8,128)(2,1)S(1)}, bf16[128,3584]{1,0:T(8,128)(2,1)S(1)}, u32[]{:S(2)}, u32[]{:S(2)}) collective-permute-start(bf16[128,3584]{1,0:T(8,128)(2,1)S(1)} %get-tuple-element.76), channel_id=1, source_target_pairs={{0,97},{1,24},{2,99},{3,26},{4,101},{5,28},{6,103},{7,30},{8,105},... | collective-permute-start | bytes 2752520 | tf_op jit(solution)/shard_map/ppermute | solution.py:63
  60.0 4.5 %collective-permute-done.11.refs_2_ = bf16[128,3584]{1,0:T(8,128)(2,1)S(1)} collective-permute-done((bf16[128,3584]{1,0:T(8,128)(2,1)S(1)}, bf16[128,3584]{1,0:T(8,128)(2,1)S(1)}, u32[]{:S(2)}, u32[]{:S(2)}) %collective-permute-start.11) | collective-permute-done | bytes 917536 | tf_op jit(solution)/shard_map/ppermute | solution.py:63
  64.5 5.5 %collective-permute-start.16 = (bf16[128,3584]{1,0:T(8,128)(2,1)S(1)}, bf16[128,3584]{1,0:T(8,128)(2,1)S(1)}, u32[]{:S(2)}, u32[]{:S(2)}) collective-permute-start(bf16[128,3584]{1,0:T(8,128)(2,1)S(1)} %get-tuple-element.77), channel_id=1, source_target_pairs={{0,33},{1,16},{2,35},{3,18},{4,37},{5,20},{6,39},{7,22},{8,41},{9,... | collective-permute-start | bytes 2752520 | tf_op jit(solution)/shard_map/ppermute | solution.py:63
  70.0 7.3 %shard_map.84 = (f32[512,1024]{1,0:T(8,128)S(1)}, bf16[3584,1024]{1,0:T(8,128)(2,1)S(1)}, bf16[512,3584]{1,0:T(8,128)(2,1)S(1)}) custom-call(s32[8]{0:T(128)S(1)} %concatenate.21.info, bf16[128,3584]{1,0:T(8,128)(2,1)S(1)} %get-tuple-element.67.refs_0_, bf16[128,3584]{1,0:T(8,128)(2,1)S(1)} %collective-permute-done.10.refs_1_, ...), custom_call_target="tpu_custom_call" | custom-call | flops 3758096384 | bytes 22020096 | tf_op jit(solution)/shard_map/pallas_call | solution.py:262
  78.1 10.2 %collective-permute-done.16.refs_3_ = bf16[128,3584]{1,0:T(8,128)(2,1)S(1)} collective-permute-done((bf16[128,3584]{1,0:T(8,128)(2,1)S(1)}, bf16[128,3584]{1,0:T(8,128)(2,1)S(1)}, u32[]{:S(2)}, u32[]{:S(2)}) %collective-permute-start.16) | collective-permute-done | bytes 917536 | tf_op jit(solution)/shard_map/ppermute | solution.py:63
  88.4 1.0 copy-done.12
  89.3 1.2 copy-done.13
  90.5 8.6 %shard_map.86 = (bf16[128,3584]{1,0:T(8,128)(2,1)S(1)}, bf16[128,3584]{1,0:T(8,128)(2,1)S(1)}, bf16[128,3584]{1,0:T(8,128)(2,1)S(1)}, bf16[128,3584]{1,0:T(8,128)(2,1)S(1)}, bf16[512,512]{1,0:T(8,128)(2,1)S(1)}) custom-call(s32[8]{0:T(128)S(1)} %concatenate.21.info, f32[512,1024]{1,0:T(8,128)S(1)} %get-tuple-element.71.near, ...), custom_call_target="tpu_custom_call" | custom-call | flops 5637144576 | bytes 7340032 | tf_op jit(solution)/shard_map/pallas_call | solution.py:333
  100.0 7.0 %shard_map.87 = (bf16[128,3584]{1,0:T(8,128)(2,1)}, bf16[128,3584]{1,0:T(8,128)(2,1)}, bf16[128,3584]{1,0:T(8,128)(2,1)}, bf16[128,3584]{1,0:T(8,128)(2,1)}, bf16[1024,256]{1,0:T(8,128)(2,1)}) custom-call(s32[8]{0:T(128)} %copy-done.8, bf16[512,512]{1,0:T(8,128)(2,1)} %copy-done.5, bf16[512,7168]{1,0:T(8,128)(2,1)} %bitcast.12, bf16[128,3712]{1,0:T(8,128)(2,1)} %copy-done, ...), custom_call_target="tpu_custom_call" | custom-call | flops 1879048192 | bytes 7340032 | tf_op jit(solution)/shard_map/pallas_call | solution.py:371
  107.1 2.3 %collective-permute-start.21 = (bf16[128,3584]{1,0:T(8,128)(2,1)}, bf16[128,3584]{1,0:T(8,128)(2,1)S(1)}, u32[]{:S(2)}, u32[]{:S(2)}) collective-permute-start(bf16[128,3584]{1,0:T(8,128)(2,1)} %get-tuple-element.85), channel_id=1, source_target_pairs={{65,0},{8,1},{67,2},{10,3},{69,4},{12,5},{71,6},{14,7},{73,8},{16,... | collective-permute-start | bytes 2752520 | tf_op jit(solution)/shard_map/ppermute | solution.py:63
  109.4 1.0 collective-permute-start.22
  110.3 3.0 %collective-permute-start.17 = (bf16[128,3584]{1,0:T(8,128)(2,1)S(1)}, bf16[128,3584]{1,0:T(8,128)(2,1)S(1)}, u32[]{:S(2)}, u32[]{:S(2)}) collective-permute-start(bf16[128,3584]{1,0:T(8,128)(2,1)S(1)} %get-tuple-element.81), channel_id=1, source_target_pairs={{64,0},{9,1},{66,2},{11,3},{68,4},{13,5},{70,6},{15,7},{72,8},{17,... | collective-permute-start | bytes 2752520 | tf_op jit(solution)/shard_map/ppermute | solution.py:63
  113.4 15.0 %collective-permute-done.21.refs_5_ = bf16[128,3584]{1,0:T(8,128)(2,1)S(1)} collective-permute-done((bf16[128,3584]{1,0:T(8,128)(2,1)}, bf16[128,3584]{1,0:T(8,128)(2,1)S(1)}, u32[]{:S(2)}, u32[]{:S(2)}) %collective-permute-start.21) | collective-permute-done | bytes 917536 | tf_op jit(solution)/shard_map/ppermute | solution.py:63
  128.4 4.9 %collective-permute-start.19 = (bf16[128,3584]{1,0:T(8,128)(2,1)S(1)}, bf16[128,3584]{1,0:T(8,128)(2,1)S(1)}, u32[]{:S(2)}, u32[]{:S(2)}) collective-permute-start(bf16[128,3584]{1,0:T(8,128)(2,1)S(1)} %get-tuple-element.83), channel_id=1, source_target_pairs={{32,0},{17,1},{34,2},{19,3},{36,4},{21,5},{38,6},{23,7},{40,8},{25... | collective-permute-start | bytes 2752520 | tf_op jit(solution)/shard_map/ppermute | solution.py:63
  133.3 18.0 %collective-permute-done.23.refs_7_ = bf16[128,3584]{1,0:T(8,128)(2,1)S(1)} collective-permute-done((bf16[128,3584]{1,0:T(8,128)(2,1)}, bf16[128,3584]{1,0:T(8,128)(2,1)S(1)}, u32[]{:S(2)}, u32[]{:S(2)}) %collective-permute-start.23) | collective-permute-done | bytes 917536 | tf_op jit(solution)/shard_map/ppermute | solution.py:63
  151.3 1.9 %collective-permute-done.19.refs_3_ = bf16[128,3584]{1,0:T(8,128)(2,1)S(1)} collective-permute-done((bf16[128,3584]{1,0:T(8,128)(2,1)S(1)}, bf16[128,3584]{1,0:T(8,128)(2,1)S(1)}, u32[]{:S(2)}, u32[]{:S(2)}) %collective-permute-start.19) | collective-permute-done | bytes 917536 | tf_op jit(solution)/shard_map/ppermute | solution.py:63
  153.2 1.0 copy-done.6
  154.2 2.1 %shard_map.88 = (bf16[128,3584]{1,0:T(8,128)(2,1)S(1)}, bf16[128,3584]{1,0:T(8,128)(2,1)S(1)}, bf16[128,3584]{1,0:T(8,128)(2,1)S(1)}, bf16[128,3584]{1,0:T(8,128)(2,1)S(1)}) custom-call(bf16[1024,256]{1,0:T(8,128)(2,1)S(1)} %copy-done.6, bf16[128,3584]{1,0:T(8,128)(2,1)S(1)} %get-tuple-element.80.refs_0_, ...), custom_call_target="tpu_custom_call" | custom-call | flops 1879048192 | bytes 11010048 | tf_op jit(solution)/shard_map/pallas_call | solution.py:156
  156.9 1.0 collective-permute-start.25
  157.9 2.6 %collective-permute-start.28 = (bf16[32,3584]{1,0:T(8,128)(2,1)S(1)}, bf16[32,3584]{1,0:T(8,128)(2,1)S(1)}, u32[]{:S(2)}, u32[]{:S(2)}) collective-permute-start(bf16[32,3584]{1,0:T(8,128)(2,1)S(1)} %get-tuple-element.107), channel_id=1, source_target_pairs={{4,0},{5,1},{6,2},{7,3},{0,4},{1,5},{2,6},{3,7},{12,8},{13,9},{14,... | collective-permute-start | bytes 688136 | tf_op jit(solution)/shard_map/ppermute | solution.py:55
  160.9 2.2 %collective-permute-start.26 = (bf16[32,3584]{1,0:T(8,128)(2,1)S(1)}, bf16[32,3584]{1,0:T(8,128)(2,1)S(1)}, u32[]{:S(2)}, u32[]{:S(2)}) collective-permute-start(bf16[32,3584]{1,0:T(8,128)(2,1)S(1)} %get-tuple-element.109), channel_id=1, source_target_pairs={{2,0},{3,1},{4,2},{5,3},{6,4},{7,5},{0,6},{1,7},{10,8},{11,9},{12,... | collective-permute-start | bytes 688136 | tf_op jit(solution)/shard_map/ppermute | solution.py:55
  163.2 2.6 %collective-permute-done.28 = bf16[32,3584]{1,0:T(8,128)(2,1)S(1)} collective-permute-done((bf16[32,3584]{1,0:T(8,128)(2,1)S(1)}, bf16[32,3584]{1,0:T(8,128)(2,1)S(1)}, u32[]{:S(2)}, u32[]{:S(2)}) %collective-permute-start.28) | collective-permute-done | bytes 229408 | tf_op jit(solution)/shard_map/ppermute | solution.py:55
  165.8 6.0 %collective-permute-done.27 = bf16[32,3584]{1,0:T(8,128)(2,1)S(1)} collective-permute-done((bf16[32,3584]{1,0:T(8,128)(2,1)S(1)}, bf16[32,3584]{1,0:T(8,128)(2,1)S(1)}, u32[]{:S(2)}, u32[]{:S(2)}) %collective-permute-start.27) | collective-permute-done | bytes 229408 | tf_op jit(solution)/shard_map/ppermute | solution.py:55
  172.2 1.6 collective-permute-start.32
  173.8 0.9 collective-permute-start.31
  174.7 1.8 collective-permute-start.30
  177.5 1.9 %collective-permute-done.32 = bf16[32,3584]{1,0:T(8,128)(2,1)S(1)} collective-permute-done((bf16[32,3584]{1,0:T(8,128)(2,1)S(1)}, bf16[32,3584]{1,0:T(8,128)(2,1)S(1)}, u32[]{:S(2)}, u32[]{:S(2)}) %collective-permute-start.32) | collective-permute-done | bytes 229408 | tf_op jit(solution)/shard_map/ppermute | solution.py:55
  179.4 5.9 %collective-permute-done.31 = bf16[32,3584]{1,0:T(8,128)(2,1)S(1)} collective-permute-done((bf16[32,3584]{1,0:T(8,128)(2,1)S(1)}, bf16[32,3584]{1,0:T(8,128)(2,1)S(1)}, u32[]{:S(2)}, u32[]{:S(2)}) %collective-permute-start.31) | collective-permute-done | bytes 229408 | tf_op jit(solution)/shard_map/ppermute | solution.py:55
  185.6 2.5 %collective-permute-start.33 = (bf16[16,3584]{1,0:T(8,128)(2,1)S(1)}, bf16[16,3584]{1,0:T(8,128)(2,1)S(1)}, u32[]{:S(2)}, u32[]{:S(2)}) collective-permute-start(bf16[16,3584]{1,0:T(8,128)(2,1)S(1)} %get-tuple-element.112), channel_id=1, source_target_pairs={{0,1},{1,0},{2,3},{3,2},{4,5},{5,4},{6,7},{7,6},{8,9},{9,8},{10,11... | collective-permute-start | bytes 344072 | tf_op jit(solution)/shard_map/ppermute | solution.py:59
  188.0 1.0 collective-permute-done.33
  (73 shorter events, 12.9 us)
Async XLA Ops:
  0.8 88.6 %copy-start.8 = (s32[8]{0:T(128)}, s32[8]{0:T(128)S(1)}, u32[]{:S(2)}) copy-start(s32[8]{0:T(128)S(1)} %concatenate.21.info) | copy-start | bytes 100
  0.8 0.9 copy-start.7
  1.7 0.7 copy-start.9
  2.4 0.7 copy-start.10
  3.1 0.7 copy-start.11
  4.5 2.4 %collective-permute-start = (bf16[16,3712]{1,0:T(8,128)(2,1)S(1)}, bf16[16,3712]{1,0:T(8,128)(2,1)S(1)}, u32[]{:S(2)}, u32[]{:S(2)}) collective-permute-start(bf16[16,3712]{1,0:T(8,128)(2,1)S(1)} %get-tuple-element.55), channel_id=1, source_target_pairs={{0,1},{1,0},{2,3},{3,2},{4,5},{5,4},{6,7},{7,6},{8,9},{9,8},{10,11... | collective-permute-start | bytes 356360 | tf_op jit(solution)/shard_map/ppermute | solution.py:59
  7.0 8.7 %collective-permute-start.4 = (bf16[32,3712]{1,0:T(8,128)(2,1)S(1)}, bf16[32,3712]{1,0:T(8,128)(2,1)S(1)}, u32[]{:S(2)}, u32[]{:S(2)}) collective-permute-start(bf16[32,3712]{1,0:T(8,128)(2,1)S(1)} %maximum_select_fusion), channel_id=1, source_target_pairs={{0,4},{1,5},{2,6},{3,7},{4,0},{5,1},{6,2},{7,3},{8,12},{9,13},{10,... | collective-permute-start | bytes 712712 | tf_op jit(solution)/shard_map/ppermute | solution.py:51
  10.0 11.1 %collective-permute-start.3 = (bf16[32,3712]{1,0:T(8,128)(2,1)S(1)}, bf16[32,3712]{1,0:T(8,128)(2,1)S(1)}, u32[]{:S(2)}, u32[]{:S(2)}) collective-permute-start(bf16[32,3712]{1,0:T(8,128)(2,1)S(1)} %maximum_select_fusion), channel_id=1, source_target_pairs={{0,6},{1,7},{2,0},{3,1},{4,2},{5,3},{6,4},{7,5},{8,14},{9,15},{10,... | collective-permute-start | bytes 712712 | tf_op jit(solution)/shard_map/ppermute | solution.py:51
  10.8 10.4 %collective-permute-start.2 = (bf16[32,3712]{1,0:T(8,128)(2,1)S(1)}, bf16[32,3712]{1,0:T(8,128)(2,1)S(1)}, u32[]{:S(2)}, u32[]{:S(2)}) collective-permute-start(bf16[32,3712]{1,0:T(8,128)(2,1)S(1)} %maximum_select_fusion), channel_id=1, source_target_pairs={{0,2},{1,3},{2,4},{3,5},{4,6},{5,7},{6,0},{7,1},{8,10},{9,11},{10,... | collective-permute-start | bytes 712712 | tf_op jit(solution)/shard_map/ppermute | solution.py:51
  11.5 9.7 %collective-permute-start.1 = (bf16[32,3712]{1,0:T(8,128)(2,1)S(1)}, bf16[32,3712]{1,0:T(8,128)(2,1)S(1)}, u32[]{:S(2)}, u32[]{:S(2)}) collective-permute-start(bf16[32,3712]{1,0:T(8,128)(2,1)S(1)} %maximum_select_fusion), channel_id=1, source_target_pairs={{0,16},{1,33},{2,18},{3,35},{4,20},{5,37},{6,22},{7,39},{8,24},{9,... | collective-permute-start | bytes 712712 | tf_op jit(solution)/shard_map/ppermute | solution.py:412
  21.3 24.7 %copy-start = (bf16[128,3712]{1,0:T(8,128)(2,1)}, bf16[128,3712]{1,0:T(8,128)(2,1)S(1)}, u32[]{:S(2)}) copy-start(bf16[128,3712]{1,0:T(8,128)(2,1)S(1)} %constant_dynamic-update-slice_fusion.refs_0_) | copy-start | bytes 2850820
  21.3 16.1 %collective-permute-start.6 = (bf16[128,3712]{1,0:T(8,128)(2,1)S(1)}, bf16[128,3712]{1,0:T(8,128)(2,1)S(1)}, u32[]{:S(2)}, u32[]{:S(2)}) collective-permute-start(bf16[128,3712]{1,0:T(8,128)(2,1)S(1)} %constant_dynamic-update-slice_fusion.refs_0_), channel_id=1, source_target_pairs={{0,24},{1,97},{2,26},{3,99},{4,28},{5,101},{6,30},{7,103},{8,0},{9... | collective-permute-start | bytes 2850824 | tf_op jit(solution)/shard_map/ppermute | solution.py:63
  23.9 14.1 %collective-permute-start.5 = (bf16[128,3712]{1,0:T(8,128)(2,1)S(1)}, bf16[128,3712]{1,0:T(8,128)(2,1)S(1)}, u32[]{:S(2)}, u32[]{:S(2)}) collective-permute-start(bf16[128,3712]{1,0:T(8,128)(2,1)S(1)} %constant_dynamic-update-slice_fusion.refs_0_), channel_id=1, source_target_pairs={{0,8},{1,65},{2,10},{3,67},{4,12},{5,69},{6,14},{7,71},{8,16},{9,7... | collective-permute-start | bytes 2850824 | tf_op jit(solution)/shard_map/ppermute | solution.py:63
  23.9 6.6 %collective-permute-start.9 = (bf16[32,3712]{1,0:T(8,128)(2,1)S(1)}, bf16[32,3712]{1,0:T(8,128)(2,1)S(1)}, u32[]{:S(2)}, u32[]{:S(2)}) collective-permute-start(bf16[32,3712]{1,0:T(8,128)(2,1)S(1)} %collective-permute-done.1), channel_id=1, source_target_pairs={{0,4},{1,5},{2,6},{3,7},{4,0},{5,1},{6,2},{7,3},{8,12},{9,13},{10,... | collective-permute-start | bytes 712712 | tf_op jit(solution)/shard_map/ppermute | solution.py:51
  27.0 10.2 %collective-permute-start.8 = (bf16[32,3712]{1,0:T(8,128)(2,1)S(1)}, bf16[32,3712]{1,0:T(8,128)(2,1)S(1)}, u32[]{:S(2)}, u32[]{:S(2)}) collective-permute-start(bf16[32,3712]{1,0:T(8,128)(2,1)S(1)} %collective-permute-done.1), channel_id=1, source_target_pairs={{0,6},{1,7},{2,0},{3,1},{4,2},{5,3},{6,4},{7,5},{8,14},{9,15},{10,... | collective-permute-start | bytes 712712 | tf_op jit(solution)/shard_map/ppermute | solution.py:51
  27.8 9.7 %collective-permute-start.7 = (bf16[32,3712]{1,0:T(8,128)(2,1)S(1)}, bf16[32,3712]{1,0:T(8,128)(2,1)S(1)}, u32[]{:S(2)}, u32[]{:S(2)}) collective-permute-start(bf16[32,3712]{1,0:T(8,128)(2,1)S(1)} %collective-permute-done.1), channel_id=1, source_target_pairs={{0,2},{1,3},{2,4},{3,5},{4,6},{5,7},{6,0},{7,1},{8,10},{9,11},{10,... | collective-permute-start | bytes 712712 | tf_op jit(solution)/shard_map/ppermute | solution.py:51
  37.4 8.6 %copy-start.2 = (bf16[128,3712]{1,0:T(8,128)(2,1)}, bf16[128,3712]{1,0:T(8,128)(2,1)S(1)}, u32[]{:S(2)}) copy-start(bf16[128,3712]{1,0:T(8,128)(2,1)S(1)} %collective-permute-done.6.refs_2_) | copy-start | bytes 2850820
  38.0 8.0 %copy-start.3 = (bf16[128,3712]{1,0:T(8,128)(2,1)}, bf16[128,3712]{1,0:T(8,128)(2,1)S(1)}, u32[]{:S(2)}) copy-start(bf16[128,3712]{1,0:T(8,128)(2,1)S(1)} %collective-permute-done.5.refs_1_) | copy-start | bytes 2850820
  38.2 11.0 %copy-start.1 = (bf16[128,3712]{1,0:T(8,128)(2,1)}, bf16[128,3712]{1,0:T(8,128)(2,1)S(1)}, u32[]{:S(2)}) copy-start(bf16[128,3712]{1,0:T(8,128)(2,1)S(1)} %constant_dynamic-update-slice_fusion.4.refs_3_) | copy-start | bytes 2850820
  38.2 31.8 %copy-start.4 = (bf16[1,7168,512]{2,1,0:T(8,128)(2,1)S(1)}, bf16[1,7168,512]{2,1,0:T(8,128)(2,1)}, u32[]{:S(2)}) copy-start(bf16[1,7168,512]{2,1,0:T(8,128)(2,1)} %param.12) | copy-start | bytes 22020100
  40.4 14.9 %collective-permute-start.10 = (bf16[128,3584]{1,0:T(8,128)(2,1)S(1)}, bf16[128,3584]{1,0:T(8,128)(2,1)S(1)}, u32[]{:S(2)}, u32[]{:S(2)}) collective-permute-start(bf16[128,3584]{1,0:T(8,128)(2,1)S(1)} %get-tuple-element.68), channel_id=1, source_target_pairs={{0,64},{1,9},{2,66},{3,11},{4,68},{5,13},{6,70},{7,15},{8,72},{9,1... | collective-permute-start | bytes 2752520 | tf_op jit(solution)/shard_map/ppermute | solution.py:63
  42.6 21.9 %collective-permute-start.11 = (bf16[128,3584]{1,0:T(8,128)(2,1)S(1)}, bf16[128,3584]{1,0:T(8,128)(2,1)S(1)}, u32[]{:S(2)}, u32[]{:S(2)}) collective-permute-start(bf16[128,3584]{1,0:T(8,128)(2,1)S(1)} %get-tuple-element.69), channel_id=1, source_target_pairs={{0,96},{1,25},{2,98},{3,27},{4,100},{5,29},{6,102},{7,31},{8,104},... | collective-permute-start | bytes 2752520 | tf_op jit(solution)/shard_map/ppermute | solution.py:63
  44.3 25.6 %collective-permute-start.12 = (bf16[128,3584]{1,0:T(8,128)(2,1)S(1)}, bf16[128,3584]{1,0:T(8,128)(2,1)S(1)}, u32[]{:S(2)}, u32[]{:S(2)}) collective-permute-start(bf16[128,3584]{1,0:T(8,128)(2,1)S(1)} %get-tuple-element.70), channel_id=1, source_target_pairs={{0,32},{1,17},{2,34},{3,19},{4,36},{5,21},{6,38},{7,23},{8,40},{9,... | collective-permute-start | bytes 2752520 | tf_op jit(solution)/shard_map/ppermute | solution.py:63
  49.2 28.1 %collective-permute-start.13 = (bf16[128,3584]{1,0:T(8,128)(2,1)}, bf16[128,3584]{1,0:T(8,128)(2,1)S(1)}, u32[]{:S(2)}, u32[]{:S(2)}) collective-permute-start(bf16[128,3584]{1,0:T(8,128)(2,1)} %get-tuple-element.74), channel_id=1, source_target_pairs={{0,1},{1,0},{2,3},{3,2},{4,5},{5,4},{6,7},{7,6},{8,9},{9,8},{10,11... | collective-permute-start | bytes 2752520 | tf_op jit(solution)/shard_map/ppermute | solution.py:59
  52.2 25.6 %collective-permute-start.14 = (bf16[128,3584]{1,0:T(8,128)(2,1)S(1)}, bf16[128,3584]{1,0:T(8,128)(2,1)S(1)}, u32[]{:S(2)}, u32[]{:S(2)}) collective-permute-start(bf16[128,3584]{1,0:T(8,128)(2,1)S(1)} %get-tuple-element.75), channel_id=1, source_target_pairs={{0,65},{1,8},{2,67},{3,10},{4,69},{5,12},{6,71},{7,14},{8,73},{9,1... | collective-permute-start | bytes 2752520 | tf_op jit(solution)/shard_map/ppermute | solution.py:63
  55.3 22.8 %collective-permute-start.15 = (bf16[128,3584]{1,0:T(8,128)(2,1)S(1)}, bf16[128,3584]{1,0:T(8,128)(2,1)S(1)}, u32[]{:S(2)}, u32[]{:S(2)}) collective-permute-start(bf16[128,3584]{1,0:T(8,128)(2,1)S(1)} %get-tuple-element.76), channel_id=1, source_target_pairs={{0,97},{1,24},{2,99},{3,26},{4,101},{5,28},{6,103},{7,30},{8,105},... | collective-permute-start | bytes 2752520 | tf_op jit(solution)/shard_map/ppermute | solution.py:63
  64.5 23.9 %collective-permute-start.16 = (bf16[128,3584]{1,0:T(8,128)(2,1)S(1)}, bf16[128,3584]{1,0:T(8,128)(2,1)S(1)}, u32[]{:S(2)}, u32[]{:S(2)}) collective-permute-start(bf16[128,3584]{1,0:T(8,128)(2,1)S(1)} %get-tuple-element.77), channel_id=1, source_target_pairs={{0,33},{1,16},{2,35},{3,18},{4,37},{5,20},{6,39},{7,22},{8,41},{9,... | collective-permute-start | bytes 2752520 | tf_op jit(solution)/shard_map/ppermute | solution.py:63
  88.4 1.0 copy-start.12
  89.3 1.2 copy-start.13
  99.1 0.9 copy-start.5
  107.0 6.4 %collective-permute-start.20 = (bf16[128,3584]{1,0:T(8,128)(2,1)}, bf16[128,3584]{1,0:T(8,128)(2,1)S(1)}, u32[]{:S(2)}, u32[]{:S(2)}) collective-permute-start(bf16[128,3584]{1,0:T(8,128)(2,1)} %get-tuple-element.84), channel_id=1, source_target_pairs={{0,1},{1,0},{2,3},{3,2},{4,5},{5,4},{6,7},{7,6},{8,9},{9,8},{10,11... | collective-permute-start | bytes 2752520 | tf_op jit(solution)/shard_map/ppermute | solution.py:59
  107.1 21.3 %collective-permute-start.21 = (bf16[128,3584]{1,0:T(8,128)(2,1)}, bf16[128,3584]{1,0:T(8,128)(2,1)S(1)}, u32[]{:S(2)}, u32[]{:S(2)}) collective-permute-start(bf16[128,3584]{1,0:T(8,128)(2,1)} %get-tuple-element.85), channel_id=1, source_target_pairs={{65,0},{8,1},{67,2},{10,3},{69,4},{12,5},{71,6},{14,7},{73,8},{16,... | collective-permute-start | bytes 2752520 | tf_op jit(solution)/shard_map/ppermute | solution.py:63
  109.4 23.9 %collective-permute-start.22 = (bf16[128,3584]{1,0:T(8,128)(2,1)}, bf16[128,3584]{1,0:T(8,128)(2,1)S(1)}, u32[]{:S(2)}, u32[]{:S(2)}) collective-permute-start(bf16[128,3584]{1,0:T(8,128)(2,1)} %get-tuple-element.86), channel_id=1, source_target_pairs={{97,0},{24,1},{99,2},{26,3},{101,4},{28,5},{103,6},{30,7},{105,8},... | collective-permute-start | bytes 2752520 | tf_op jit(solution)/shard_map/ppermute | solution.py:63
  110.3 40.9 %collective-permute-start.23 = (bf16[128,3584]{1,0:T(8,128)(2,1)}, bf16[128,3584]{1,0:T(8,128)(2,1)S(1)}, u32[]{:S(2)}, u32[]{:S(2)}) collective-permute-start(bf16[128,3584]{1,0:T(8,128)(2,1)} %get-tuple-element.87), channel_id=1, source_target_pairs={{33,0},{16,1},{35,2},{18,3},{37,4},{20,5},{39,6},{22,7},{41,8},{24... | collective-permute-start | bytes 2752520 | tf_op jit(solution)/shard_map/ppermute | solution.py:63
  110.3 40.9 %collective-permute-start.17 = (bf16[128,3584]{1,0:T(8,128)(2,1)S(1)}, bf16[128,3584]{1,0:T(8,128)(2,1)S(1)}, u32[]{:S(2)}, u32[]{:S(2)}) collective-permute-start(bf16[128,3584]{1,0:T(8,128)(2,1)S(1)} %get-tuple-element.81), channel_id=1, source_target_pairs={{64,0},{9,1},{66,2},{11,3},{68,4},{13,5},{70,6},{15,7},{72,8},{17,... | collective-permute-start | bytes 2752520 | tf_op jit(solution)/shard_map/ppermute | solution.py:63
  113.4 37.9 %collective-permute-start.18 = (bf16[128,3584]{1,0:T(8,128)(2,1)S(1)}, bf16[128,3584]{1,0:T(8,128)(2,1)S(1)}, u32[]{:S(2)}, u32[]{:S(2)}) collective-permute-start(bf16[128,3584]{1,0:T(8,128)(2,1)S(1)} %get-tuple-element.82), channel_id=1, source_target_pairs={{96,0},{25,1},{98,2},{27,3},{100,4},{29,5},{102,6},{31,7},{104,8},... | collective-permute-start | bytes 2752520 | tf_op jit(solution)/shard_map/ppermute | solution.py:63
  128.4 24.8 %collective-permute-start.19 = (bf16[128,3584]{1,0:T(8,128)(2,1)S(1)}, bf16[128,3584]{1,0:T(8,128)(2,1)S(1)}, u32[]{:S(2)}, u32[]{:S(2)}) collective-permute-start(bf16[128,3584]{1,0:T(8,128)(2,1)S(1)} %get-tuple-element.83), channel_id=1, source_target_pairs={{32,0},{17,1},{34,2},{19,3},{36,4},{21,5},{38,6},{23,7},{40,8},{25... | collective-permute-start | bytes 2752520 | tf_op jit(solution)/shard_map/ppermute | solution.py:63
  153.2 1.0 copy-start.6
  156.3 15.5 %collective-permute-start.24 = (bf16[128,3584]{1,0:T(8,128)(2,1)S(1)}, bf16[128,3584]{1,0:T(8,128)(2,1)S(1)}, u32[]{:S(2)}, u32[]{:S(2)}) collective-permute-start(bf16[128,3584]{1,0:T(8,128)(2,1)S(1)} %get-tuple-element.88), channel_id=1, source_target_pairs={{8,0},{65,1},{10,2},{67,3},{12,4},{69,5},{14,6},{71,7},{16,8},{73,... | collective-permute-start | bytes 2752520 | tf_op jit(solution)/shard_map/ppermute | solution.py:63
  156.9 15.0 %collective-permute-start.25 = (bf16[128,3584]{1,0:T(8,128)(2,1)S(1)}, bf16[128,3584]{1,0:T(8,128)(2,1)S(1)}, u32[]{:S(2)}, u32[]{:S(2)}) collective-permute-start(bf16[128,3584]{1,0:T(8,128)(2,1)S(1)} %get-tuple-element.89), channel_id=1, source_target_pairs={{24,0},{97,1},{26,2},{99,3},{28,4},{101,5},{30,6},{103,7},{0,8},{1... | collective-permute-start | bytes 2752520 | tf_op jit(solution)/shard_map/ppermute | solution.py:63
  157.9 7.8 %collective-permute-start.28 = (bf16[32,3584]{1,0:T(8,128)(2,1)S(1)}, bf16[32,3584]{1,0:T(8,128)(2,1)S(1)}, u32[]{:S(2)}, u32[]{:S(2)}) collective-permute-start(bf16[32,3584]{1,0:T(8,128)(2,1)S(1)} %get-tuple-element.107), channel_id=1, source_target_pairs={{4,0},{5,1},{6,2},{7,3},{0,4},{1,5},{2,6},{3,7},{12,8},{13,9},{14,... | collective-permute-start | bytes 688136 | tf_op jit(solution)/shard_map/ppermute | solution.py:55
  160.5 11.3 %collective-permute-start.27 = (bf16[32,3584]{1,0:T(8,128)(2,1)S(1)}, bf16[32,3584]{1,0:T(8,128)(2,1)S(1)}, u32[]{:S(2)}, u32[]{:S(2)}) collective-permute-start(bf16[32,3584]{1,0:T(8,128)(2,1)S(1)} %get-tuple-element.108), channel_id=1, source_target_pairs={{6,0},{7,1},{0,2},{1,3},{2,4},{3,5},{4,6},{5,7},{14,8},{15,9},{8,1... | collective-permute-start | bytes 688136 | tf_op jit(solution)/shard_map/ppermute | solution.py:55
  160.9 10.9 %collective-permute-start.26 = (bf16[32,3584]{1,0:T(8,128)(2,1)S(1)}, bf16[32,3584]{1,0:T(8,128)(2,1)S(1)}, u32[]{:S(2)}, u32[]{:S(2)}) collective-permute-start(bf16[32,3584]{1,0:T(8,128)(2,1)S(1)} %get-tuple-element.109), channel_id=1, source_target_pairs={{2,0},{3,1},{4,2},{5,3},{6,4},{7,5},{0,6},{1,7},{10,8},{11,9},{12,... | collective-permute-start | bytes 688136 | tf_op jit(solution)/shard_map/ppermute | solution.py:55
  172.2 7.2 %collective-permute-start.32 = (bf16[32,3584]{1,0:T(8,128)(2,1)S(1)}, bf16[32,3584]{1,0:T(8,128)(2,1)S(1)}, u32[]{:S(2)}, u32[]{:S(2)}) collective-permute-start(bf16[32,3584]{1,0:T(8,128)(2,1)S(1)} %get-tuple-element.103), channel_id=1, source_target_pairs={{4,0},{5,1},{6,2},{7,3},{0,4},{1,5},{2,6},{3,7},{12,8},{13,9},{14,... | collective-permute-start | bytes 688136 | tf_op jit(solution)/shard_map/ppermute | solution.py:55
  173.8 11.5 %collective-permute-start.31 = (bf16[32,3584]{1,0:T(8,128)(2,1)S(1)}, bf16[32,3584]{1,0:T(8,128)(2,1)S(1)}, u32[]{:S(2)}, u32[]{:S(2)}) collective-permute-start(bf16[32,3584]{1,0:T(8,128)(2,1)S(1)} %get-tuple-element.104), channel_id=1, source_target_pairs={{6,0},{7,1},{0,2},{1,3},{2,4},{3,5},{4,6},{5,7},{14,8},{15,9},{8,1... | collective-permute-start | bytes 688136 | tf_op jit(solution)/shard_map/ppermute | solution.py:55
  174.7 10.6 %collective-permute-start.30 = (bf16[32,3584]{1,0:T(8,128)(2,1)S(1)}, bf16[32,3584]{1,0:T(8,128)(2,1)S(1)}, u32[]{:S(2)}, u32[]{:S(2)}) collective-permute-start(bf16[32,3584]{1,0:T(8,128)(2,1)S(1)} %get-tuple-element.105), channel_id=1, source_target_pairs={{2,0},{3,1},{4,2},{5,3},{6,4},{7,5},{0,6},{1,7},{10,8},{11,9},{12,... | collective-permute-start | bytes 688136 | tf_op jit(solution)/shard_map/ppermute | solution.py:55
  176.6 8.8 %collective-permute-start.29 = (bf16[32,3584]{1,0:T(8,128)(2,1)S(1)}, bf16[32,3584]{1,0:T(8,128)(2,1)S(1)}, u32[]{:S(2)}, u32[]{:S(2)}) collective-permute-start(bf16[32,3584]{1,0:T(8,128)(2,1)S(1)} %add_convert_fusion.2), channel_id=1, source_target_pairs={{16,0},{33,1},{18,2},{35,3},{20,4},{37,5},{22,6},{39,7},{24,8},{41... | collective-permute-start | bytes 688136 | tf_op jit(solution)/shard_map/ppermute | solution.py:430
  185.6 3.4 %collective-permute-start.33 = (bf16[16,3584]{1,0:T(8,128)(2,1)S(1)}, bf16[16,3584]{1,0:T(8,128)(2,1)S(1)}, u32[]{:S(2)}, u32[]{:S(2)}) collective-permute-start(bf16[16,3584]{1,0:T(8,128)(2,1)S(1)} %get-tuple-element.112), channel_id=1, source_target_pairs={{0,1},{1,0},{2,3},{3,2},{4,5},{5,4},{6,7},{7,6},{8,9},{9,8},{10,11... | collective-permute-start | bytes 344072 | tf_op jit(solution)/shard_map/ppermute | solution.py:59
